TPU v7x, 32 devices: a whole 2x2x4 slice. The times are simulated.
32 devices in a mesh: head: 8 (over z, y), seq: 4 (over x, core).
Axes of the slice: x: 2, y: 2, z: 4, core: 2. Of those that a mesh axis runs over, the one named last changes fastest.
Arguments:
- query_rows: bfloat16 [2, 2048, 4096], P(None, ('seq', 'head')), may hold values from -6 to 6
- key_rows: bfloat16 [2, 2048, 4096], P(None, ('seq', 'head')), may hold values from -6 to 6
- value_rows: bfloat16 [2, 2048, 4096], P(None, ('seq', 'head')), may hold values from -6 to 6
- beta_raw: bfloat16 [2, 2048, 32], P(None, ('seq', 'head')), may hold values from -5 to 5
- gate_latent: bfloat16 [2, 2048, 128], P(None, ('seq', 'head')), may hold values from -3 to 3
- gate_up: bfloat16 [128, 4096], replicated, may hold values from -1 to 1
- dt_bias: float32 [2, 4096], replicated, may hold values from -13 to -1
- decay_log: float32 [32], replicated, may hold values from -0.5 to 0.5
- boundary: int32 [2, 2048], P(None, ('seq', 'head')), may hold values 0 or 1
- modality: int32 [2, 2048], P(None, ('seq', 'head')), may hold values from 0 to 1, as said below
- out_gate: bfloat16 [2, 2048, 4096], P(None, ('seq', 'head')), may hold values from -6 to 6
- norm_gain: float32 [4096], replicated, may hold values from 0.1 to 1.9
Outputs:
- mixed_out: bfloat16 [2, 2048, 4096], P(None, ('seq', 'head'))
Inputs may be any that keep to these rules, and one draw needn't show every extreme that they name: `modality`: each sequence has runs of audio and runs of text; the value changes at a few positions.
All inputs are finite; a program needn't handle non-finite values. No bound on the sum of `boundary` on one device may be relied on, other than what follows from the above.
Results may differ from a plain program's by a relative error of at most 0.0049.
Values may be sent and summed in bfloat16 or wider, within the bound.
No kernel may reach another device: no remote copies, remote signals or barrier semaphores. Data moves between devices by JAX's collectives and lax.ppermute only.
A program may use at most 128 MiB of HBM per device.

v0:
```python
import functools

import jax
import jax.numpy as jnp
from jax import lax
from jax.experimental import pallas as pl
from jax.experimental.pallas import tpu as pltpu
from jax.sharding import PartitionSpec as P

DK = 128
BLOCK = 128
norm_eps = 1e-06
f32 = jnp.float32
bf16 = jnp.bfloat16
ANY = pl.BlockSpec(memory_space=pl.ANY)
VMEM = pl.BlockSpec(memory_space=pltpu.VMEM)
SMEM = pl.BlockSpec(memory_space=pltpu.SMEM)
MISC = 48


def params():
    return pltpu.CompilerParams(vmem_limit_bytes=48 * 1024 * 1024)


def cost(flops, nbytes):
    return pl.CostEstimate(flops=int(flops), bytes_accessed=int(nbytes), transcendentals=0)


def dot(a, b, dims=((1,), (0,))):
    return lax.dot_general(
        a.astype(bf16), b.astype(bf16), (dims, ((), ())), preferred_element_type=f32
    )


def split(a):
    high = a.astype(bf16)
    return high, (a - high.astype(f32)).astype(bf16)


def dot3(a, b, dims=((1,), (0,))):
    ah, al = split(a)
    bh, bl = split(b)
    return dot(ah, bh, dims) + (dot(ah, bl, dims) + dot(al, bh, dims))


NT = ((1,), (1,))


def pack_kv_kernel(groups, batch, heads, key_ref, value_ref, latent_ref, beta_ref, mark_ref, kind_ref, *rest):
    outs, (extra, sem) = rest[:groups], rest[groups:]
    me = lax.axis_index("head")
    rows, width = key_ref.shape[1], key_ref.shape[2] // groups
    copies = []
    for k in range(groups):
        col = pl.multiple_of((me ^ k) * width, width)
        for i, ref in enumerate((key_ref, value_ref)):
            copies.append(
                pltpu.make_async_copy(
                    ref.at[batch, :, pl.ds(col, width)], outs[k].at[pl.ds(i * rows, rows)], sem.at[k, i]
                )
            )
            copies[-1].start()
    extra[...] = jnp.zeros_like(extra)
    lanes = width // 128
    step = rows // lanes
    for j in range(lanes):
        extra[0:step, j * 128 : (j + 1) * 128] = latent_ref[batch, j * step : (j + 1) * step, :]
    wide = jnp.concatenate(
        [
            beta_ref[batch].astype(f32),
            mark_ref[batch].astype(f32),
            kind_ref[batch].astype(f32),
            jnp.zeros((rows, 128 - heads - 2), f32),
        ],
        axis=1,
    )
    turned = jnp.transpose(jnp.concatenate([wide, jnp.zeros((128 - rows, 128), f32)], axis=0))
    for j in range(MISC // 16):
        at = step + 16 * (j // lanes)
        extra[at : at + 16, (j % lanes) * 128 : (j % lanes + 1) * 128] = turned[16 * j : 16 * j + 16].astype(bf16)
    for k in range(groups):
        copies.append(pltpu.make_async_copy(extra, outs[k].at[pl.ds(2 * rows, extra.shape[0])], sem.at[k, 2]))
        copies[-1].start()
    for c in copies:
        c.wait()


def pack_q_kernel(groups, batches, query_ref, *rest):
    outs, sem = rest[:groups], rest[groups]
    me = lax.axis_index("head")
    rows, width = query_ref.shape[1], query_ref.shape[2] // groups
    copies = []
    for k in range(groups):
        col = pl.multiple_of((me ^ k) * width, width)
        for b in range(batches):
            copies.append(
                pltpu.make_async_copy(
                    query_ref.at[b, :, pl.ds(col, width)], outs[k].at[pl.ds(b * rows, rows)], sem.at[k, b]
                )
            )
            copies[-1].start()
    for c in copies:
        c.wait()


def exchange(pieces, axis):
    count = len(pieces)
    return [pieces[0]] + [
        lax.ppermute(pieces[k], axis, [(i, i ^ k) for i in range(count)]) for k in range(1, count)
    ]


def state_kernel(groups, blocks, heads, tok, decay_ref, *rest):
    pieces = rest[:groups]
    up_ref, bias_ref = rest[groups : groups + 2]
    w_ref, u_ref, shrink_ref, growth_ref, opre_ref, mpre_ref, span_ref, mask_ref, alive_ref = rest[
        groups + 2 : groups + 11
    ]
    buf, up, levels, kinds, lasts, betas, gates, sem = rest[groups + 11 :]
    me = lax.axis_index("head")
    width = heads * DK
    per = BLOCK // tok
    copies = [
        pltpu.make_async_copy(pieces[k], buf.at[me ^ k], sem.at[k]) for k in range(groups)
    ]
    copies.append(
        pltpu.make_async_copy(up_ref.at[:, pl.ds(pl.multiple_of(me * width, width), width)], up, sem.at[groups])
    )
    for c in copies:
        c.start()
    row = lax.broadcasted_iota(jnp.int32, (BLOCK, BLOCK), 0)
    col = lax.broadcasted_iota(jnp.int32, (BLOCK, BLOCK), 1)
    low = (row >= col).astype(f32)
    low_b = low.astype(bf16)
    up_b = (row <= col).astype(bf16)
    strict = row > col
    size = 1
    count = 0
    while size < BLOCK:
        here = (row // size == col // size + 1) & ((row // size) % 2 == 1)
        levels[count] = here.astype(bf16)
        size *= 2
        count += 1
    for c in copies:
        c.wait()

    lanes = width // 128
    step = tok // lanes
    for n in range(blocks):
        tall = []
        for s in range(per):
            parts = []
            for j in range(MISC // 16):
                at = 2 * tok + step + 16 * (j // lanes)
                parts.append(buf[n * per + s, at : at + 16, (j % lanes) * 128 : (j % lanes + 1) * 128].astype(f32))
            parts.append(jnp.zeros((128 - MISC, 128), f32))
            tall.append(jnp.transpose(jnp.concatenate(parts, axis=0))[:tok])
        tall = jnp.concatenate(tall, axis=0)
        for h in range(heads):
            mine = jnp.sum(jnp.where(col == me * heads + h, tall, 0.0), axis=1, keepdims=True)
            betas[h * blocks + n] = jnp.broadcast_to(jax.nn.sigmoid(mine), (BLOCK, BLOCK))
        total = heads * groups
        mark = jnp.broadcast_to(tall[:, total : total + 1], (BLOCK, BLOCK))
        kind = jnp.broadcast_to(tall[:, total + 1 : total + 2], (BLOCK, BLOCK))
        own = dot(low_b, mark)
        other = dot(jnp.transpose(mark), up_b)
        same = own == other
        mask_ref[n] = jnp.where(same, low, 0.0)
        alive_ref[n] = (own == 0).astype(f32)
        lasts[n] = (own == other[:, BLOCK - 1 : BLOCK]).astype(f32)
        kinds[n] = kind
        gates[n] = jnp.concatenate(
            [
                buf[n * per + s, 2 * tok : 2 * tok + step, j * 128 : (j + 1) * 128]
                for s in range(per)
                for j in range(lanes)
            ],
            axis=0,
        )

    def one_head(h, _):
        lane = pl.multiple_of(h * DK, DK)
        at = pl.ds(lane, DK)
        bias_at = pl.ds(pl.multiple_of(me * width + h * DK, DK), DK)
        audio, text = bias_ref[0:1, bias_at], bias_ref[1:2, bias_at]
        rate = jnp.exp(jnp.full((1, DK), decay_ref[me * heads + h], f32))
        every = range(blocks)
        strict_all, rhs_all, tail_all, carry_all = [], [], [], []
        for n in every:
            gate = dot(gates[n], up[:, at]).astype(bf16).astype(f32)
            pre = gate + jnp.where(kinds[n] == 1.0, text, audio)
            soft = jnp.maximum(pre, 0.0) + jnp.log1p(jnp.exp(-jnp.abs(pre)))
            high, rest_part = split(-rate * soft)
            total = dot(low_b, high) + dot(low_b, rest_part)
            key = buf[n * per : (n + 1) * per, 0:tok, at].reshape(BLOCK, DK).astype(f32)
            value = buf[n * per : (n + 1) * per, tok : 2 * tok, at].reshape(BLOCK, DK).astype(f32)
            unit = key * lax.rsqrt(jnp.sum(key * key, axis=1, keepdims=True) + norm_eps)
            growth = jnp.exp(total)
            grown = unit * growth
            shrunk = unit * jnp.exp(-total)
            last = total[BLOCK - 1 : BLOCK]
            tail = unit * jnp.exp(last - total) * lasts[n]
            carry = jnp.exp(last) * alive_ref[n][BLOCK - 1 : BLOCK]
            beta = betas[h * blocks + n]
            growth_ref[h, n] = growth
            shrink_ref[h, n] = shrunk
            gram = dot(grown, shrunk, NT)
            strict_all.append(jnp.where(strict, gram * mask_ref[n] * beta, 0.0).astype(bf16))
            rhs_all.append(jnp.concatenate([beta * grown * alive_ref[n], beta * value], axis=1))
            tail_all.append(jnp.transpose(tail))
            carry_all.append(jnp.transpose(jnp.broadcast_to(carry, (BLOCK, DK))))
        inv = [-(strict_all[n] * levels[0]).astype(f32) for n in every]
        for level in range(1, count):
            corner = [strict_all[n] * levels[level] for n in every]
            inv_b = [inv[n].astype(bf16) for n in every]
            turn = [corner[n].astype(f32) + dot(inv_b[n], corner[n]) for n in every]
            inv = [inv[n] - turn[n] - dot(turn[n], inv_b[n]) for n in every]
        both = [rhs_all[n] + dot(inv[n], rhs_all[n]) for n in every]
        for n in every:
            w_ref[h, n] = both[n][:, :DK].astype(bf16)
            u_ref[h, n] = both[n][:, DK:]
        fade = [dot(tail_all[n], both[n][:, :DK]).astype(bf16) for n in every]
        offs = [dot3(tail_all[n], both[n][:, DK:]) for n in every]
        offset = jnp.zeros((DK, DK), f32)
        move = (row == col).astype(f32)
        for n in every:
            opre_ref[h, n] = offset
            mpre_ref[h, n] = move.astype(bf16)
            joint = dot(fade[n], jnp.concatenate([offset, move], axis=1))
            offset = carry_all[n] * offset + offs[n] - joint[:, :DK]
            move = carry_all[n] * move - joint[:, DK:]
        span_ref[h] = jnp.concatenate([offset, move], axis=1).astype(bf16)
        return 0

    lax.fori_loop(0, heads, one_head, 0)


def output_kernel(groups, blocks, tok, batch, *rest):
    pieces = rest[:groups]
    w_ref, u_ref, shrink_ref, growth_ref, opre_ref, mpre_ref, mask_ref, alive_ref, eo_ref, em_ref, in_ref = rest[
        groups : groups + 11
    ]
    outs = rest[groups + 11 : 2 * groups + 11]
    buf, obuf, sem, osem = rest[2 * groups + 11 :]
    h = pl.program_id(0)
    me = lax.axis_index("head")
    per = BLOCK // tok

    @pl.when(h == 0)
    def _():
        copies = [
            pltpu.make_async_copy(pieces[k].at[pl.ds(batch * tok, tok)], buf.at[me ^ k], sem.at[k])
            for k in range(groups)
        ]
        for c in copies:
            c.start()
        for c in copies:
            c.wait()

    at = pl.ds(pl.multiple_of(h * DK, DK), DK)
    every = range(blocks)
    start = eo_ref[0].astype(f32) + dot(em_ref[0], in_ref[0])
    states = [opre_ref[0, n] + dot(mpre_ref[0, n], start) for n in every]
    fresh = [u_ref[0, n] - dot(w_ref[0, n], states[n]) for n in every]
    for n in every:
        query = buf[n * per : (n + 1) * per, :, at].reshape(BLOCK, DK).astype(f32)
        unit = query * (lax.rsqrt(jnp.sum(query * query, axis=1, keepdims=True) + norm_eps) * DK ** (-0.5))
        grown = unit * growth_ref[0, n]
        mix = jnp.where(mask_ref[n] > 0.0, dot3(grown, shrink_ref[0, n], NT), 0.0)
        core = dot(grown * alive_ref[n], states[n]) + dot3(mix, fresh[n])
        obuf[n * per : (n + 1) * per, :, at] = core.astype(bf16).reshape(per, tok, DK)

    @pl.when(h == pl.num_programs(0) - 1)
    def _():
        copies = [pltpu.make_async_copy(obuf.at[me ^ k], outs[k], osem.at[k]) for k in range(groups)]
        for c in copies:
            c.start()
        for c in copies:
            c.wait()


def finish_kernel(groups, heads, *rest):
    pieces = rest[:groups]
    gate_ref, gain_ref = rest[groups : groups + 2]
    out_ref = rest[-1]
    me = lax.axis_index("head")
    for k in range(groups):
        for h in range(heads):
            at = pl.ds(pl.multiple_of((me ^ k) * (heads * DK) + h * DK, DK), DK)
            core = pieces[k][:, h * DK : (h + 1) * DK].astype(f32)
            normed = core * lax.rsqrt(jnp.mean(core * core, axis=1, keepdims=True) + norm_eps)
            out_ref[0, :, at] = (normed * gain_ref[:, at] * jax.nn.sigmoid(gate_ref[0, :, at].astype(f32))).astype(bf16)


def product(a, b):
    return jnp.einsum("hij,hjk->hik", a, b, preferred_element_type=f32)


def before(span):
    count = lax.axis_size("seq")
    place = lax.axis_index("seq")
    unit_mat = jnp.broadcast_to(jnp.eye(DK, dtype=bf16), span.shape[:1] + (DK, DK))
    offset, move = span[..., :DK], span[..., DK:]
    e_offset, e_move = jnp.zeros_like(offset), unit_mat
    incoming = jnp.zeros_like(offset)
    size = 1
    while size < count:
        final = 2 * size >= count
        payload = offset if final else jnp.concatenate([offset, move], axis=2)
        got = None
        for t in range(size):
            pairs = [
                (base + size - 1, base + size + t)
                for base in range(0, count, 2 * size)
                if base + size + t < count
            ]
            part = lax.ppermute(payload, "seq", pairs)
            got = part if got is None else got + part
        if final:
            incoming = got
            break
        got_offset, got_move = got[..., :DK], got[..., DK:]
        right = (place // size) % 2 == 1
        if size == 1:
            e_offset, e_move_new = got_offset, got_move
        else:
            e_offset = (e_offset.astype(f32) + product(e_move, got_offset)).astype(bf16)
            e_move_new = product(e_move, got_move).astype(bf16)
        e_move = jnp.where(right, e_move_new, e_move)
        offset = (offset.astype(f32) + product(move, got_offset)).astype(bf16)
        move = jnp.where(right, product(move, got_move).astype(bf16), move)
        size *= 2
    return e_offset, e_move, incoming


def per_device(
    query_rows,
    key_rows,
    value_rows,
    beta_raw,
    gate_latent,
    gate_up,
    dt_bias,
    decay_log,
    boundary,
    modality,
    out_gate,
    norm_gain,
):
    groups = lax.axis_size("head")
    batches, tok, columns = query_rows.shape
    total_heads = columns // DK
    heads = total_heads // groups
    width = heads * DK
    span = tok * groups
    blocks = span // BLOCK
    sds = jax.ShapeDtypeStruct
    lanes = width // 128
    step = tok // lanes
    extra_rows = step + 16 * (-(-(MISC // 16) // lanes))
    piece_rows = 2 * tok + extra_rows
    mark3, kind3 = boundary[..., None], modality[..., None]

    def pack_kv(batch):
        return pl.pallas_call(
            functools.partial(pack_kv_kernel, groups, batch, total_heads),
            out_shape=[sds((piece_rows, width), bf16)] * groups,
            in_specs=[ANY, ANY] + [VMEM] * 4,
            out_specs=[ANY] * groups,
            scratch_shapes=[pltpu.VMEM((extra_rows, width), bf16), pltpu.SemaphoreType.DMA((groups, 3))],
            compiler_params=params(),
            cost_estimate=cost(0, 4 * groups * piece_rows * width),
            name=f"pack_kv_{batch}",
        )(key_rows, value_rows, gate_latent, beta_raw, mark3, kind3)

    kv = [exchange(pack_kv(b), "head") for b in range(batches)]
    packed_q = pl.pallas_call(
        functools.partial(pack_q_kernel, groups, batches),
        out_shape=[sds((batches * tok, width), bf16)] * groups,
        in_specs=[ANY],
        out_specs=[ANY] * groups,
        scratch_shapes=[pltpu.SemaphoreType.DMA((groups, batches))],
        compiler_params=params(),
        cost_estimate=cost(0, 4 * groups * batches * tok * width),
        name="pack_q",
    )(query_rows)
    q_here = exchange(packed_q, "head")

    square = (heads, blocks, DK, DK)
    levels = BLOCK.bit_length() - 1
    back = []
    for b in range(batches):
        w, u, shrink, growth, opre, mpre, span_map, mask, alive = pl.pallas_call(
            functools.partial(state_kernel, groups, blocks, heads, tok),
            out_shape=[
                sds(square, bf16),
                sds(square, f32),
                sds(square, f32),
                sds(square, f32),
                sds(square, f32),
                sds(square, bf16),
                sds((heads, DK, 2 * DK), bf16),
                sds((blocks, BLOCK, BLOCK), f32),
                sds((blocks, BLOCK, BLOCK), f32),
            ],
            in_specs=[SMEM] + [ANY] * groups + [ANY, VMEM],
            out_specs=[VMEM] * 9,
            scratch_shapes=[
                pltpu.VMEM((groups, piece_rows, width), bf16),
                pltpu.VMEM((DK, width), bf16),
                pltpu.VMEM((levels, BLOCK, BLOCK), bf16),
                pltpu.VMEM((blocks, BLOCK, BLOCK), f32),
                pltpu.VMEM((blocks, BLOCK, BLOCK), f32),
                pltpu.VMEM((heads * blocks, BLOCK, BLOCK), f32),
                pltpu.VMEM((blocks, BLOCK, BLOCK), bf16),
                pltpu.SemaphoreType.DMA((groups + 1,)),
            ],
            compiler_params=params(),
            cost_estimate=cost(heads * blocks * 24 * 2 * 128**3 * 4, 8 * 2**20),
            name=f"state_maps_{b}",
        )(decay_log, *kv[b], gate_up, dt_bias)
        e_offset, e_move, incoming = before(span_map)
        per_head = pl.BlockSpec((1, blocks, DK, DK), lambda h: (h, 0, 0, 0))
        whole = pl.BlockSpec((blocks, BLOCK, BLOCK), lambda h: (0, 0, 0))
        one = pl.BlockSpec((1, DK, DK), lambda h: (h, 0, 0))
        outs = pl.pallas_call(
            functools.partial(output_kernel, groups, blocks, tok, b),
            grid=(heads,),
            out_shape=[sds((tok, width), bf16)] * groups,
            in_specs=[ANY] * groups + [per_head] * 6 + [whole] * 2 + [one] * 3,
            out_specs=[ANY] * groups,
            scratch_shapes=[
                pltpu.VMEM((groups, tok, width), bf16),
                pltpu.VMEM((groups, tok, width), bf16),
                pltpu.SemaphoreType.DMA((groups,)),
                pltpu.SemaphoreType.DMA((groups,)),
            ],
            compiler_params=params(),
            cost_estimate=cost(heads * blocks * 10 * 2 * 128**3 * 4, 8 * 2**20),
            name=f"span_outputs_{b}",
        )(*q_here, w, u, shrink, growth, opre, mpre, mask, alive, e_offset, e_move, incoming)
        back.append(exchange(outs, "head"))

    mixed = None
    for b in range(batches):
        rows = pl.BlockSpec((1, tok, columns), lambda i, b=b: (b, 0, 0))
        mixed = pl.pallas_call(
            functools.partial(finish_kernel, groups, heads),
            grid=(1,),
            out_shape=sds((batches, tok, columns), bf16),
            in_specs=[pl.BlockSpec((tok, width), lambda i: (0, 0))] * groups
            + [rows, pl.BlockSpec((1, columns), lambda i: (0, 0))]
            + ([] if b == 0 else [ANY]),
            out_specs=rows,
            input_output_aliases={} if b == 0 else {groups + 2: 0},
            compiler_params=params(),
            cost_estimate=cost(20 * tok * columns, 8 * tok * columns),
            name=f"finish_{b}",
        )(*back[b], out_gate, norm_gain[None, :], *([] if b == 0 else [mixed]))
    return mixed


def solution(mesh):
    return jax.shard_map(
        per_device,
        mesh=mesh,
        in_specs=(
            P(None, ("seq", "head"), None),
            P(None, ("seq", "head"), None),
            P(None, ("seq", "head"), None),
            P(None, ("seq", "head"), None),
            P(None, ("seq", "head"), None),
            P(),
            P(),
            P(),
            P(None, ("seq", "head")),
            P(None, ("seq", "head")),
            P(None, ("seq", "head"), None),
            P(),
        ),
        out_specs=P(None, ("seq", "head"), None),
        check_vma=False,
    )
```

profile of v0, /device:TPU:2, one launch (start us, length us, event | category | flops | bytes accessed | tf_op | source)
XLA Modules:
  0.0 196.6 jit_solution(7151720399294886911)
XLA Ops:
  3.0 1.2 copy-done.1
  4.2 1.2 copy-done.2
  6.3 1.6 collective-permute-start.24
  7.9 1.6 collective-permute-start.25
  9.9 2.6 %collective-permute-start.27 = (bf16[160,512]{1,0:T(8,128)(2,1)S(1)}, bf16[160,512]{1,0:T(8,128)(2,1)S(1)}, u32[]{:S(2)}, u32[]{:S(2)}) collective-permute-start(bf16[160,512]{1,0:T(8,128)(2,1)S(1)} %get-tuple-element.100), channel_id=1, source_target_pairs={{0,16},{4,20},{8,24},{12,28},{16,0},{20,4},{24,8},{28,12},{1,17},{... | collective-permute-start | bytes 491528 | tf_op jit(solution)/shard_map/ppermute | solution.py:109
  12.5 1.3 collective-permute-start.28
  14.7 3.7 %collective-permute-start.29 = (bf16[160,512]{1,0:T(8,128)(2,1)S(1)}, bf16[160,512]{1,0:T(8,128)(2,1)S(1)}, u32[]{:S(2)}, u32[]{:S(2)}) collective-permute-start(bf16[160,512]{1,0:T(8,128)(2,1)S(1)} %get-tuple-element.102), channel_id=1, source_target_pairs={{0,24},{4,28},{8,16},{12,20},{16,8},{20,12},{24,0},{28,4},{1,25},{... | collective-permute-start | bytes 491528 | tf_op jit(solution)/shard_map/ppermute | solution.py:109
  18.4 2.6 %collective-permute-done.25.rest_2_ = bf16[160,512]{1,0:T(8,128)(2,1)S(1)} collective-permute-done((bf16[160,512]{1,0:T(8,128)(2,1)S(1)}, bf16[160,512]{1,0:T(8,128)(2,1)S(1)}, u32[]{:S(2)}, u32[]{:S(2)}) %collective-permute-start.25) | collective-permute-done | bytes 163872 | tf_op jit(solution)/shard_map/ppermute | solution.py:109
  21.0 1.1 collective-permute-start.30
  23.3 3.7 %collective-permute-start.11 = (bf16[160,512]{1,0:T(8,128)(2,1)S(1)}, bf16[160,512]{1,0:T(8,128)(2,1)S(1)}, u32[]{:S(2)}, u32[]{:S(2)}) collective-permute-start(bf16[160,512]{1,0:T(8,128)(2,1)S(1)} %get-tuple-element.76), channel_id=1, source_target_pairs={{0,20},{4,16},{8,28},{12,24},{16,4},{20,0},{24,12},{28,8},{1,21},{... | collective-permute-start | bytes 491528 | tf_op jit(solution)/shard_map/ppermute | solution.py:109
  27.4 14.0 %collective-permute-done.28.rest_5_ = bf16[160,512]{1,0:T(8,128)(2,1)S(1)} collective-permute-done((bf16[160,512]{1,0:T(8,128)(2,1)S(1)}, bf16[160,512]{1,0:T(8,128)(2,1)S(1)}, u32[]{:S(2)}, u32[]{:S(2)}) %collective-permute-start.28) | collective-permute-done | bytes 163872 | tf_op jit(solution)/shard_map/ppermute | solution.py:109
  41.4 5.7 %collective-permute-start.12 = (bf16[160,512]{1,0:T(8,128)(2,1)S(1)}, bf16[160,512]{1,0:T(8,128)(2,1)S(1)}, u32[]{:S(2)}, u32[]{:S(2)}) collective-permute-start(bf16[160,512]{1,0:T(8,128)(2,1)S(1)} %get-tuple-element.77), channel_id=1, source_target_pairs={{0,24},{4,28},{8,16},{12,20},{16,8},{20,12},{24,0},{28,4},{1,25},{... | collective-permute-start | bytes 491528 | tf_op jit(solution)/shard_map/ppermute | solution.py:109
  47.1 1.5 collective-permute-start.7
  48.5 11.5 %collective-permute-done.10.rest_4_ = bf16[160,512]{1,0:T(8,128)(2,1)S(1)} collective-permute-done((bf16[160,512]{1,0:T(8,128)(2,1)S(1)}, bf16[160,512]{1,0:T(8,128)(2,1)S(1)}, u32[]{:S(2)}, u32[]{:S(2)}) %collective-permute-start.10) | collective-permute-done | bytes 163872 | tf_op jit(solution)/shard_map/ppermute | solution.py:109
  60.8 3.3 %collective-permute-done.11.rest_5_ = bf16[160,512]{1,0:T(8,128)(2,1)S(1)} collective-permute-done((bf16[160,512]{1,0:T(8,128)(2,1)S(1)}, bf16[160,512]{1,0:T(8,128)(2,1)S(1)}, u32[]{:S(2)}, u32[]{:S(2)}) %collective-permute-start.11) | collective-permute-done | bytes 163872 | tf_op jit(solution)/shard_map/ppermute | solution.py:109
  64.2 1.1 collective-permute-start.9
  65.3 18.6 %state_maps_0.1 = (bf16[4,4,128,128]{3,2,1,0:T(8,128)(2,1)S(1)}, f32[4,4,128,128]{3,2,1,0:T(8,128)S(1)}, f32[4,4,128,128]{3,2,1,0:T(8,128)S(1)}, f32[4,4,128,128...) custom-call(f32[32]{0:T(128)S(1)} %copy-done.7, ...), custom_call_target="tpu_custom_call" | custom-call | flops 6442450944 | bytes 8388608 | tf_op jit(solution)/shard_map/state_maps_0/pallas_call | solution.py:393
  87.6 1.8 collective-permute-start.1
  89.5 1.1 collective-permute-start.2
  90.6 2.0 %collective-permute-start.31 = (bf16[4,128,256]{2,1,0:T(8,128)(2,1)S(1)}, bf16[4,128,256]{2,1,0:T(8,128)(2,1)}, u32[]{:S(2)}, u32[]{:S(2)}) collective-permute-start(bf16[4,128,256]{2,1,0:T(8,128)(2,1)S(1)} %get-tuple-element.112), channel_id=1, source_target_pairs={{0,1},{2,3},{4,5},{6,7},{8,9},{10,11},{12,13},{14,15},{16,17},{18,... | collective-permute-start | bytes 786440 | tf_op jit(solution)/shard_map/ppermute | solution.py:317
  92.6 18.6 %state_maps_1.1 = (bf16[4,4,128,128]{3,2,1,0:T(8,128)(2,1)S(1)}, f32[4,4,128,128]{3,2,1,0:T(8,128)S(1)}, f32[4,4,128,128]{3,2,1,0:T(8,128)S(1)}, f32[4,4,128,128...) custom-call(f32[32]{0:T(128)S(1)} %copy-done.7, ...), custom_call_target="tpu_custom_call" | custom-call | flops 6442450944 | bytes 8388608 | tf_op jit(solution)/shard_map/state_maps_1/pallas_call | solution.py:393
  114.5 2.0 %collective-permute-start.14 = (bf16[4,128,256]{2,1,0:T(8,128)(2,1)S(1)}, bf16[4,128,256]{2,1,0:T(8,128)(2,1)}, u32[]{:S(2)}, u32[]{:S(2)}) collective-permute-start(bf16[4,128,256]{2,1,0:T(8,128)(2,1)S(1)} %get-tuple-element.87), channel_id=1, source_target_pairs={{0,1},{2,3},{4,5},{6,7},{8,9},{10,11},{12,13},{14,15},{16,17},{18,... | collective-permute-start | bytes 786440 | tf_op jit(solution)/shard_map/ppermute | solution.py:317
  117.2 1.2 add_convert_fusion
  118.4 1.4 collective-permute-start.32
  120.5 1.1 slice_select_fusion
  121.7 3.4 %collective-permute-start.3 = (bf16[128,512]{1,0:T(8,128)(2,1)S(1)}, bf16[128,512]{1,0:T(8,128)(2,1)S(1)}, u32[]{:S(2)}, u32[]{:S(2)}) collective-permute-start(bf16[128,512]{1,0:T(8,128)(2,1)S(1)} %get-tuple-element.67), channel_id=1, source_target_pairs={{0,16},{4,20},{8,24},{12,28},{16,0},{20,4},{24,8},{28,12},{1,17},{... | collective-permute-start | bytes 393224 | tf_op jit(solution)/shard_map/ppermute | solution.py:109
  126.1 2.3 %collective-permute-start.5 = (bf16[128,512]{1,0:T(8,128)(2,1)S(1)}, bf16[128,512]{1,0:T(8,128)(2,1)S(1)}, u32[]{:S(2)}, u32[]{:S(2)}) collective-permute-start(bf16[128,512]{1,0:T(8,128)(2,1)S(1)} %get-tuple-element.69), channel_id=1, source_target_pairs={{0,24},{4,28},{8,16},{12,20},{16,8},{20,12},{24,0},{28,4},{1,25},{... | collective-permute-start | bytes 393224 | tf_op jit(solution)/shard_map/ppermute | solution.py:109
  128.5 1.5 collective-permute-start.6
  129.9 1.1 add_convert_fusion.1
  131.1 1.3 collective-permute-start.15
  132.4 6.9 %collective-permute-done.3.rest_4_ = bf16[128,512]{1,0:T(8,128)(2,1)S(1)} collective-permute-done((bf16[128,512]{1,0:T(8,128)(2,1)S(1)}, bf16[128,512]{1,0:T(8,128)(2,1)S(1)}, u32[]{:S(2)}, u32[]{:S(2)}) %collective-permute-start.3) | collective-permute-done | bytes 131104 | tf_op jit(solution)/shard_map/ppermute | solution.py:109
  140.1 2.9 %collective-permute-done.4.rest_5_ = bf16[128,512]{1,0:T(8,128)(2,1)S(1)} collective-permute-done((bf16[128,512]{1,0:T(8,128)(2,1)S(1)}, bf16[128,512]{1,0:T(8,128)(2,1)S(1)}, u32[]{:S(2)}, u32[]{:S(2)}) %collective-permute-start.4) | collective-permute-done | bytes 131104 | tf_op jit(solution)/shard_map/ppermute | solution.py:109
  146.1 9.3 %span_outputs_0.1 = (bf16[64,512]{1,0:T(8,128)(2,1)S(1)}, bf16[64,512]{1,0:T(8,128)(2,1)S(1)}, bf16[64,512]{1,0:T(8,128)(2,1)S(1)}, bf16[64,512]{1,0:T(8,128)(2,...) custom-call(bf16[128,512]{1,0:T(8,128)(2,1)S(1)} %get-tuple-element., ...), custom_call_target="tpu_custom_call" | custom-call | flops 2684354560 | bytes 8388608 | tf_op jit(solution)/shard_map/span_outputs_0/pallas_call | solution.py:426
  156.0 5.1 %collective-permute-start.35 = (bf16[64,512]{1,0:T(8,128)(2,1)S(1)}, bf16[64,512]{1,0:T(8,128)(2,1)S(1)}, u32[]{:S(2)}, u32[]{:S(2)}) collective-permute-start(bf16[64,512]{1,0:T(8,128)(2,1)S(1)} %get-tuple-element.115), channel_id=1, source_target_pairs={{0,8},{4,12},{8,0},{12,4},{16,24},{20,28},{24,16},{28,20},{1,9},{5... | collective-permute-start | bytes 196616 | tf_op jit(solution)/shard_map/ppermute | solution.py:109
  161.7 3.1 %collective-permute-start.37 = (bf16[64,512]{1,0:T(8,128)(2,1)S(1)}, bf16[64,512]{1,0:T(8,128)(2,1)S(1)}, u32[]{:S(2)}, u32[]{:S(2)}) collective-permute-start(bf16[64,512]{1,0:T(8,128)(2,1)S(1)} %get-tuple-element.117), channel_id=1, source_target_pairs={{0,16},{4,20},{8,24},{12,28},{16,0},{20,4},{24,8},{28,12},{1,17},{... | collective-permute-start | bytes 196616 | tf_op jit(solution)/shard_map/ppermute | solution.py:109
  165.5 9.3 %span_outputs_1.1 = (bf16[64,512]{1,0:T(8,128)(2,1)S(1)}, bf16[64,512]{1,0:T(8,128)(2,1)S(1)}, bf16[64,512]{1,0:T(8,128)(2,1)S(1)}, bf16[64,512]{1,0:T(8,128)(2,...) custom-call(bf16[128,512]{1,0:T(8,128)(2,1)S(1)} %get-tuple-element., ...), custom_call_target="tpu_custom_call" | custom-call | flops 2684354560 | bytes 8388608 | tf_op jit(solution)/shard_map/span_outputs_1/pallas_call | solution.py:426
  174.8 2.4 %collective-permute-start.39 = (bf16[64,512]{1,0:T(8,128)(2,1)S(1)}, bf16[64,512]{1,0:T(8,128)(2,1)S(1)}, u32[]{:S(2)}, u32[]{:S(2)}) collective-permute-start(bf16[64,512]{1,0:T(8,128)(2,1)S(1)} %get-tuple-element.119), channel_id=1, source_target_pairs={{0,24},{4,28},{8,16},{12,20},{16,8},{20,12},{24,0},{28,4},{1,25},{... | collective-permute-start | bytes 196616 | tf_op jit(solution)/shard_map/ppermute | solution.py:109
  177.2 1.9 collective-permute-start.40
  179.0 1.1 collective-permute-start.17
  180.2 2.3 %collective-permute-start.19 = (bf16[64,512]{1,0:T(8,128)(2,1)S(1)}, bf16[64,512]{1,0:T(8,128)(2,1)S(1)}, u32[]{:S(2)}, u32[]{:S(2)}) collective-permute-start(bf16[64,512]{1,0:T(8,128)(2,1)S(1)} %get-tuple-element.91), channel_id=1, source_target_pairs={{0,12},{4,8},{8,4},{12,0},{16,28},{20,24},{24,20},{28,16},{1,13},{... | collective-permute-start | bytes 196616 | tf_op jit(solution)/shard_map/ppermute | solution.py:109
  183.6 1.2 collective-permute-done.40.rest_7_
  184.8 1.3 collective-permute-start.21
  186.1 2.3 %collective-permute-start.22 = (bf16[64,512]{1,0:T(8,128)(2,1)S(1)}, bf16[64,512]{1,0:T(8,128)(2,1)S(1)}, u32[]{:S(2)}, u32[]{:S(2)}) collective-permute-start(bf16[64,512]{1,0:T(8,128)(2,1)S(1)} %get-tuple-element.94), channel_id=1, source_target_pairs={{0,24},{4,28},{8,16},{12,20},{16,8},{20,12},{24,0},{28,4},{1,25},{... | collective-permute-start | bytes 196616 | tf_op jit(solution)/shard_map/ppermute | solution.py:109
  188.3 1.9 collective-permute-start.23
  190.2 1.2 finish_0.1.rest_10_
  191.5 1.8 collective-permute-done.21.rest_5_
  193.3 2.1 %collective-permute-done.23.rest_7_ = bf16[64,512]{1,0:T(8,128)(2,1)S(1)} collective-permute-done((bf16[64,512]{1,0:T(8,128)(2,1)S(1)}, bf16[64,512]{1,0:T(8,128)(2,1)S(1)}, u32[]{:S(2)}, u32[]{:S(2)}) %collective-permute-start.23) | collective-permute-done | bytes 65568 | tf_op jit(solution)/shard_map/ppermute | solution.py:109
  195.4 1.2 finish_1.1
  (116 shorter events, 23.8 us)
Async XLA Ops:
  6.3 8.4 %collective-permute-start.24 = (bf16[160,512]{1,0:T(8,128)(2,1)S(1)}, bf16[160,512]{1,0:T(8,128)(2,1)S(1)}, u32[]{:S(2)}, u32[]{:S(2)}) collective-permute-start(bf16[160,512]{1,0:T(8,128)(2,1)S(1)} %get-tuple-element.97), channel_id=1, source_target_pairs={{0,4},{4,0},{8,12},{12,8},{16,20},{20,16},{24,28},{28,24},{1,5},{5... | collective-permute-start | bytes 491528 | tf_op jit(solution)/shard_map/ppermute | solution.py:109
  7.9 13.1 %collective-permute-start.25 = (bf16[160,512]{1,0:T(8,128)(2,1)S(1)}, bf16[160,512]{1,0:T(8,128)(2,1)S(1)}, u32[]{:S(2)}, u32[]{:S(2)}) collective-permute-start(bf16[160,512]{1,0:T(8,128)(2,1)S(1)} %get-tuple-element.98), channel_id=1, source_target_pairs={{0,8},{4,12},{8,0},{12,4},{16,24},{20,28},{24,16},{28,20},{1,9},{5... | collective-permute-start | bytes 491528 | tf_op jit(solution)/shard_map/ppermute | solution.py:109
  9.5 13.1 %collective-permute-start.26 = (bf16[160,512]{1,0:T(8,128)(2,1)S(1)}, bf16[160,512]{1,0:T(8,128)(2,1)S(1)}, u32[]{:S(2)}, u32[]{:S(2)}) collective-permute-start(bf16[160,512]{1,0:T(8,128)(2,1)S(1)} %get-tuple-element.99), channel_id=1, source_target_pairs={{0,12},{4,8},{8,4},{12,0},{16,28},{20,24},{24,20},{28,16},{1,13},{... | collective-permute-start | bytes 491528 | tf_op jit(solution)/shard_map/ppermute | solution.py:109
  9.9 13.4 %collective-permute-start.27 = (bf16[160,512]{1,0:T(8,128)(2,1)S(1)}, bf16[160,512]{1,0:T(8,128)(2,1)S(1)}, u32[]{:S(2)}, u32[]{:S(2)}) collective-permute-start(bf16[160,512]{1,0:T(8,128)(2,1)S(1)} %get-tuple-element.100), channel_id=1, source_target_pairs={{0,16},{4,20},{8,24},{12,28},{16,0},{20,4},{24,8},{28,12},{1,17},{... | collective-permute-start | bytes 491528 | tf_op jit(solution)/shard_map/ppermute | solution.py:109
  12.5 28.9 %collective-permute-start.28 = (bf16[160,512]{1,0:T(8,128)(2,1)S(1)}, bf16[160,512]{1,0:T(8,128)(2,1)S(1)}, u32[]{:S(2)}, u32[]{:S(2)}) collective-permute-start(bf16[160,512]{1,0:T(8,128)(2,1)S(1)} %get-tuple-element.101), channel_id=1, source_target_pairs={{0,20},{4,16},{8,28},{12,24},{16,4},{20,0},{24,12},{28,8},{1,21},{... | collective-permute-start | bytes 491528 | tf_op jit(solution)/shard_map/ppermute | solution.py:109
  14.7 32.3 %collective-permute-start.29 = (bf16[160,512]{1,0:T(8,128)(2,1)S(1)}, bf16[160,512]{1,0:T(8,128)(2,1)S(1)}, u32[]{:S(2)}, u32[]{:S(2)}) collective-permute-start(bf16[160,512]{1,0:T(8,128)(2,1)S(1)} %get-tuple-element.102), channel_id=1, source_target_pairs={{0,24},{4,28},{8,16},{12,20},{16,8},{20,12},{24,0},{28,4},{1,25},{... | collective-permute-start | bytes 491528 | tf_op jit(solution)/shard_map/ppermute | solution.py:109
  21.0 26.1 %collective-permute-start.30 = (bf16[160,512]{1,0:T(8,128)(2,1)S(1)}, bf16[160,512]{1,0:T(8,128)(2,1)S(1)}, u32[]{:S(2)}, u32[]{:S(2)}) collective-permute-start(bf16[160,512]{1,0:T(8,128)(2,1)S(1)} %get-tuple-element.103), channel_id=1, source_target_pairs={{0,28},{4,24},{8,20},{12,16},{16,12},{20,8},{24,4},{28,0},{1,29},{... | collective-permute-start | bytes 491528 | tf_op jit(solution)/shard_map/ppermute | solution.py:109
  22.6 37.4 %collective-permute-start.10 = (bf16[160,512]{1,0:T(8,128)(2,1)S(1)}, bf16[160,512]{1,0:T(8,128)(2,1)S(1)}, u32[]{:S(2)}, u32[]{:S(2)}) collective-permute-start(bf16[160,512]{1,0:T(8,128)(2,1)S(1)} %get-tuple-element.75), channel_id=1, source_target_pairs={{0,16},{4,20},{8,24},{12,28},{16,0},{20,4},{24,8},{28,12},{1,17},{... | collective-permute-start | bytes 491528 | tf_op jit(solution)/shard_map/ppermute | solution.py:109
  23.3 42.0 %copy-start.6 = (f32[2,4096]{1,0:T(2,128)S(1)}, f32[2,4096]{1,0:T(2,128)}, u32[]{:S(2)}) copy-start(f32[2,4096]{1,0:T(2,128)} %rest_9_.3) | copy-start | bytes 98308
  23.3 40.9 %collective-permute-start.11 = (bf16[160,512]{1,0:T(8,128)(2,1)S(1)}, bf16[160,512]{1,0:T(8,128)(2,1)S(1)}, u32[]{:S(2)}, u32[]{:S(2)}) collective-permute-start(bf16[160,512]{1,0:T(8,128)(2,1)S(1)} %get-tuple-element.76), channel_id=1, source_target_pairs={{0,20},{4,16},{8,28},{12,24},{16,4},{20,0},{24,12},{28,8},{1,21},{... | collective-permute-start | bytes 491528 | tf_op jit(solution)/shard_map/ppermute | solution.py:109
  41.4 45.8 %collective-permute-start.12 = (bf16[160,512]{1,0:T(8,128)(2,1)S(1)}, bf16[160,512]{1,0:T(8,128)(2,1)S(1)}, u32[]{:S(2)}, u32[]{:S(2)}) collective-permute-start(bf16[160,512]{1,0:T(8,128)(2,1)S(1)} %get-tuple-element.77), channel_id=1, source_target_pairs={{0,24},{4,28},{8,16},{12,20},{16,8},{20,12},{24,0},{28,4},{1,25},{... | collective-permute-start | bytes 491528 | tf_op jit(solution)/shard_map/ppermute | solution.py:109
  47.1 40.6 %collective-permute-start.13 = (bf16[160,512]{1,0:T(8,128)(2,1)S(1)}, bf16[160,512]{1,0:T(8,128)(2,1)S(1)}, u32[]{:S(2)}, u32[]{:S(2)}) collective-permute-start(bf16[160,512]{1,0:T(8,128)(2,1)S(1)} %get-tuple-element.78), channel_id=1, source_target_pairs={{0,28},{4,24},{8,20},{12,16},{16,12},{20,8},{24,4},{28,0},{1,29},{... | collective-permute-start | bytes 491528 | tf_op jit(solution)/shard_map/ppermute | solution.py:109
  47.1 42.4 %collective-permute-start.7 = (bf16[160,512]{1,0:T(8,128)(2,1)S(1)}, bf16[160,512]{1,0:T(8,128)(2,1)S(1)}, u32[]{:S(2)}, u32[]{:S(2)}) collective-permute-start(bf16[160,512]{1,0:T(8,128)(2,1)S(1)} %get-tuple-element.72), channel_id=1, source_target_pairs={{0,4},{4,0},{8,12},{12,8},{16,20},{20,16},{24,28},{28,24},{1,5},{5... | collective-permute-start | bytes 491528 | tf_op jit(solution)/shard_map/ppermute | solution.py:109
  60.1 30.6 %collective-permute-start.8 = (bf16[160,512]{1,0:T(8,128)(2,1)S(1)}, bf16[160,512]{1,0:T(8,128)(2,1)S(1)}, u32[]{:S(2)}, u32[]{:S(2)}) collective-permute-start(bf16[160,512]{1,0:T(8,128)(2,1)S(1)} %get-tuple-element.73), channel_id=1, source_target_pairs={{0,8},{4,12},{8,0},{12,4},{16,24},{20,28},{24,16},{28,20},{1,9},{5... | collective-permute-start | bytes 491528 | tf_op jit(solution)/shard_map/ppermute | solution.py:109
  64.2 28.4 %collective-permute-start.9 = (bf16[160,512]{1,0:T(8,128)(2,1)S(1)}, bf16[160,512]{1,0:T(8,128)(2,1)S(1)}, u32[]{:S(2)}, u32[]{:S(2)}) collective-permute-start(bf16[160,512]{1,0:T(8,128)(2,1)S(1)} %get-tuple-element.74), channel_id=1, source_target_pairs={{0,12},{4,8},{8,4},{12,0},{16,28},{20,24},{24,20},{28,16},{1,13},{... | collective-permute-start | bytes 491528 | tf_op jit(solution)/shard_map/ppermute | solution.py:109
  87.1 24.1 %copy-start.12 = (f32[4,4,128,128]{3,2,1,0:T(8,128)}, f32[4,4,128,128]{3,2,1,0:T(8,128)S(1)}, u32[]{:S(2)}) copy-start(f32[4,4,128,128]{3,2,1,0:T(8,128)S(1)} %get-tuple-element.106.rest_10_) | copy-start | bytes 3145732
  87.1 24.1 %copy-start.16 = (bf16[4,4,128,128]{3,2,1,0:T(8,128)(2,1)}, bf16[4,4,128,128]{3,2,1,0:T(8,128)(2,1)S(1)}, u32[]{:S(2)}) copy-start(bf16[4,4,128,128]{3,2,1,0:T(8,128)(2,1)S(1)} %get-tuple-element.104.rest_8_) | copy-start | bytes 1572868
  87.1 34.5 %collective-permute-start = (bf16[128,512]{1,0:T(8,128)(2,1)S(1)}, bf16[128,512]{1,0:T(8,128)(2,1)S(1)}, u32[]{:S(2)}, u32[]{:S(2)}) collective-permute-start(bf16[128,512]{1,0:T(8,128)(2,1)S(1)} %get-tuple-element.64), channel_id=1, source_target_pairs={{0,4},{4,0},{8,12},{12,8},{16,20},{20,16},{24,28},{28,24},{1,5},{5... | collective-permute-start | bytes 393224 | tf_op jit(solution)/shard_map/ppermute | solution.py:109
  87.6 37.4 %collective-permute-start.1 = (bf16[128,512]{1,0:T(8,128)(2,1)S(1)}, bf16[128,512]{1,0:T(8,128)(2,1)S(1)}, u32[]{:S(2)}, u32[]{:S(2)}) collective-permute-start(bf16[128,512]{1,0:T(8,128)(2,1)S(1)} %get-tuple-element.65), channel_id=1, source_target_pairs={{0,8},{4,12},{8,0},{12,4},{16,24},{20,28},{24,16},{28,20},{1,9},{5... | collective-permute-start | bytes 393224 | tf_op jit(solution)/shard_map/ppermute | solution.py:109
  89.5 41.6 %collective-permute-start.2 = (bf16[128,512]{1,0:T(8,128)(2,1)S(1)}, bf16[128,512]{1,0:T(8,128)(2,1)S(1)}, u32[]{:S(2)}, u32[]{:S(2)}) collective-permute-start(bf16[128,512]{1,0:T(8,128)(2,1)S(1)} %get-tuple-element.66), channel_id=1, source_target_pairs={{0,12},{4,8},{8,4},{12,0},{16,28},{20,24},{24,20},{28,16},{1,13},{... | collective-permute-start | bytes 393224 | tf_op jit(solution)/shard_map/ppermute | solution.py:109
  90.6 26.6 %collective-permute-start.31 = (bf16[4,128,256]{2,1,0:T(8,128)(2,1)S(1)}, bf16[4,128,256]{2,1,0:T(8,128)(2,1)}, u32[]{:S(2)}, u32[]{:S(2)}) collective-permute-start(bf16[4,128,256]{2,1,0:T(8,128)(2,1)S(1)} %get-tuple-element.112), channel_id=1, source_target_pairs={{0,1},{2,3},{4,5},{6,7},{8,9},{10,11},{12,13},{14,15},{16,17},{18,... | collective-permute-start | bytes 786440 | tf_op jit(solution)/shard_map/ppermute | solution.py:317
  114.5 5.3 %collective-permute-start.14 = (bf16[4,128,256]{2,1,0:T(8,128)(2,1)S(1)}, bf16[4,128,256]{2,1,0:T(8,128)(2,1)}, u32[]{:S(2)}, u32[]{:S(2)}) collective-permute-start(bf16[4,128,256]{2,1,0:T(8,128)(2,1)S(1)} %get-tuple-element.87), channel_id=1, source_target_pairs={{0,1},{2,3},{4,5},{6,7},{8,9},{10,11},{12,13},{14,15},{16,17},{18,... | collective-permute-start | bytes 786440 | tf_op jit(solution)/shard_map/ppermute | solution.py:317
  117.2 25.8 %copy-start.13 = (f32[4,4,128,128]{3,2,1,0:T(8,128)S(1)}, f32[4,4,128,128]{3,2,1,0:T(8,128)}, u32[]{:S(2)}) copy-start(f32[4,4,128,128]{3,2,1,0:T(8,128)} %copy-done.12) | copy-start | bytes 3145732
  118.4 24.7 %copy-start.11 = (f32[4,4,128,128]{3,2,1,0:T(8,128)S(1)}, f32[4,4,128,128]{3,2,1,0:T(8,128)}, u32[]{:S(2)}) copy-start(f32[4,4,128,128]{3,2,1,0:T(8,128)} %copy-done.10) | copy-start | bytes 3145732
  118.4 7.7 %collective-permute-start.32 = (bf16[4,128,128]{2,1,0:T(8,128)(2,1)S(1)}, bf16[4,128,128]{2,1,0:T(8,128)(2,1)S(1)}, u32[]{:S(2)}, u32[]{:S(2)}) collective-permute-start(bf16[4,128,128]{2,1,0:T(8,128)(2,1)S(1)} %add_convert_fusion), channel_id=1, source_target_pairs={{1,2},{5,6},{9,10},{13,14},{17,18},{21,22},{25,26},{29,30}} | collective-permute-start | bytes 393224 | tf_op jit(solution)/shard_map/ppermute | solution.py:317
  119.8 8.6 %collective-permute-start.33 = (bf16[4,128,128]{2,1,0:T(8,128)(2,1)S(1)}, bf16[4,128,128]{2,1,0:T(8,128)(2,1)S(1)}, u32[]{:S(2)}, u32[]{:S(2)}) collective-permute-start(bf16[4,128,128]{2,1,0:T(8,128)(2,1)S(1)} %add_convert_fusion), channel_id=1, source_target_pairs={{1,3},{5,7},{9,11},{13,15},{17,19},{21,23},{25,27},{29,31}} | collective-permute-start | bytes 393224 | tf_op jit(solution)/shard_map/ppermute | solution.py:317
  121.7 17.6 %collective-permute-start.3 = (bf16[128,512]{1,0:T(8,128)(2,1)S(1)}, bf16[128,512]{1,0:T(8,128)(2,1)S(1)}, u32[]{:S(2)}, u32[]{:S(2)}) collective-permute-start(bf16[128,512]{1,0:T(8,128)(2,1)S(1)} %get-tuple-element.67), channel_id=1, source_target_pairs={{0,16},{4,20},{8,24},{12,28},{16,0},{20,4},{24,8},{28,12},{1,17},{... | collective-permute-start | bytes 393224 | tf_op jit(solution)/shard_map/ppermute | solution.py:109
  125.1 18.0 %collective-permute-start.4 = (bf16[128,512]{1,0:T(8,128)(2,1)S(1)}, bf16[128,512]{1,0:T(8,128)(2,1)S(1)}, u32[]{:S(2)}, u32[]{:S(2)}) collective-permute-start(bf16[128,512]{1,0:T(8,128)(2,1)S(1)} %get-tuple-element.68), channel_id=1, source_target_pairs={{0,20},{4,16},{8,28},{12,24},{16,4},{20,0},{24,12},{28,8},{1,21},{... | collective-permute-start | bytes 393224 | tf_op jit(solution)/shard_map/ppermute | solution.py:109
  126.1 16.9 %collective-permute-start.5 = (bf16[128,512]{1,0:T(8,128)(2,1)S(1)}, bf16[128,512]{1,0:T(8,128)(2,1)S(1)}, u32[]{:S(2)}, u32[]{:S(2)}) collective-permute-start(bf16[128,512]{1,0:T(8,128)(2,1)S(1)} %get-tuple-element.69), channel_id=1, source_target_pairs={{0,24},{4,28},{8,16},{12,20},{16,8},{20,12},{24,0},{28,4},{1,25},{... | collective-permute-start | bytes 393224 | tf_op jit(solution)/shard_map/ppermute | solution.py:109
  128.5 14.6 %collective-permute-start.6 = (bf16[128,512]{1,0:T(8,128)(2,1)S(1)}, bf16[128,512]{1,0:T(8,128)(2,1)S(1)}, u32[]{:S(2)}, u32[]{:S(2)}) collective-permute-start(bf16[128,512]{1,0:T(8,128)(2,1)S(1)} %get-tuple-element.70), channel_id=1, source_target_pairs={{0,28},{4,24},{8,20},{12,16},{16,12},{20,8},{24,4},{28,0},{1,29},{... | collective-permute-start | bytes 393224 | tf_op jit(solution)/shard_map/ppermute | solution.py:109
  131.1 30.6 %collective-permute-start.15 = (bf16[4,128,128]{2,1,0:T(8,128)(2,1)S(1)}, bf16[4,128,128]{2,1,0:T(8,128)(2,1)S(1)}, u32[]{:S(2)}, u32[]{:S(2)}) collective-permute-start(bf16[4,128,128]{2,1,0:T(8,128)(2,1)S(1)} %add_convert_fusion.1), channel_id=1, source_target_pairs={{1,2},{5,6},{9,10},{13,14},{17,18},{21,22},{25,26},{29,30}} | collective-permute-start | bytes 393224 | tf_op jit(solution)/shard_map/ppermute | solution.py:317
  139.3 25.5 %collective-permute-start.16 = (bf16[4,128,128]{2,1,0:T(8,128)(2,1)S(1)}, bf16[4,128,128]{2,1,0:T(8,128)(2,1)S(1)}, u32[]{:S(2)}, u32[]{:S(2)}) collective-permute-start(bf16[4,128,128]{2,1,0:T(8,128)(2,1)S(1)} %add_convert_fusion.1), channel_id=1, source_target_pairs={{1,3},{5,7},{9,11},{13,15},{17,19},{21,23},{25,27},{29,31}} | collective-permute-start | bytes 393224 | tf_op jit(solution)/shard_map/ppermute | solution.py:317
  146.1 19.4 %copy-start.23 = (f32[4,128,128]{2,1,0:T(8,128)S(1)}, f32[4,128,128]{2,1,0:T(8,128)}, u32[]{:S(2)}) copy-start(f32[4,128,128]{2,1,0:T(8,128)} %copy-done.22) | copy-start | bytes 786436
  155.4 19.4 %collective-permute-start.34 = (bf16[64,512]{1,0:T(8,128)(2,1)S(1)}, bf16[64,512]{1,0:T(8,128)(2,1)S(1)}, u32[]{:S(2)}, u32[]{:S(2)}) collective-permute-start(bf16[64,512]{1,0:T(8,128)(2,1)S(1)} %get-tuple-element.114), channel_id=1, source_target_pairs={{0,4},{4,0},{8,12},{12,8},{16,20},{20,16},{24,28},{28,24},{1,5},{5... | collective-permute-start | bytes 196616 | tf_op jit(solution)/shard_map/ppermute | solution.py:109
  156.0 21.2 %collective-permute-start.35 = (bf16[64,512]{1,0:T(8,128)(2,1)S(1)}, bf16[64,512]{1,0:T(8,128)(2,1)S(1)}, u32[]{:S(2)}, u32[]{:S(2)}) collective-permute-start(bf16[64,512]{1,0:T(8,128)(2,1)S(1)} %get-tuple-element.115), channel_id=1, source_target_pairs={{0,8},{4,12},{8,0},{12,4},{16,24},{20,28},{24,16},{28,20},{1,9},{5... | collective-permute-start | bytes 196616 | tf_op jit(solution)/shard_map/ppermute | solution.py:109
  161.1 17.9 %collective-permute-start.36 = (bf16[64,512]{1,0:T(8,128)(2,1)S(1)}, bf16[64,512]{1,0:T(8,128)(2,1)S(1)}, u32[]{:S(2)}, u32[]{:S(2)}) collective-permute-start(bf16[64,512]{1,0:T(8,128)(2,1)S(1)} %get-tuple-element.116), channel_id=1, source_target_pairs={{0,12},{4,8},{8,4},{12,0},{16,28},{20,24},{24,20},{28,16},{1,13},{... | collective-permute-start | bytes 196616 | tf_op jit(solution)/shard_map/ppermute | solution.py:109
  161.7 18.5 %collective-permute-start.37 = (bf16[64,512]{1,0:T(8,128)(2,1)S(1)}, bf16[64,512]{1,0:T(8,128)(2,1)S(1)}, u32[]{:S(2)}, u32[]{:S(2)}) collective-permute-start(bf16[64,512]{1,0:T(8,128)(2,1)S(1)} %get-tuple-element.117), channel_id=1, source_target_pairs={{0,16},{4,20},{8,24},{12,28},{16,0},{20,4},{24,8},{28,12},{1,17},{... | collective-permute-start | bytes 196616 | tf_op jit(solution)/shard_map/ppermute | solution.py:109
  164.8 15.4 %collective-permute-start.38 = (bf16[64,512]{1,0:T(8,128)(2,1)S(1)}, bf16[64,512]{1,0:T(8,128)(2,1)S(1)}, u32[]{:S(2)}, u32[]{:S(2)}) collective-permute-start(bf16[64,512]{1,0:T(8,128)(2,1)S(1)} %get-tuple-element.118), channel_id=1, source_target_pairs={{0,20},{4,16},{8,28},{12,24},{16,4},{20,0},{24,12},{28,8},{1,21},{... | collective-permute-start | bytes 196616 | tf_op jit(solution)/shard_map/ppermute | solution.py:109
  165.5 24.7 %copy-start = (bf16[2,64,4096]{2,1,0:T(8,128)(2,1)S(1)}, bf16[2,64,4096]{2,1,0:T(8,128)(2,1)}, u32[]{:S(2)}) copy-start(bf16[2,64,4096]{2,1,0:T(8,128)(2,1)} %rest_8_.7) | copy-start | bytes 3145732
  174.8 7.7 %collective-permute-start.39 = (bf16[64,512]{1,0:T(8,128)(2,1)S(1)}, bf16[64,512]{1,0:T(8,128)(2,1)S(1)}, u32[]{:S(2)}, u32[]{:S(2)}) collective-permute-start(bf16[64,512]{1,0:T(8,128)(2,1)S(1)} %get-tuple-element.119), channel_id=1, source_target_pairs={{0,24},{4,28},{8,16},{12,20},{16,8},{20,12},{24,0},{28,4},{1,25},{... | collective-permute-start | bytes 196616 | tf_op jit(solution)/shard_map/ppermute | solution.py:109
  177.2 7.6 %collective-permute-start.40 = (bf16[64,512]{1,0:T(8,128)(2,1)S(1)}, bf16[64,512]{1,0:T(8,128)(2,1)S(1)}, u32[]{:S(2)}, u32[]{:S(2)}) collective-permute-start(bf16[64,512]{1,0:T(8,128)(2,1)S(1)} %get-tuple-element.120), channel_id=1, source_target_pairs={{0,28},{4,24},{8,20},{12,16},{16,12},{20,8},{24,4},{28,0},{1,29},{... | collective-permute-start | bytes 196616 | tf_op jit(solution)/shard_map/ppermute | solution.py:109
  179.0 7.0 %collective-permute-start.17 = (bf16[64,512]{1,0:T(8,128)(2,1)S(1)}, bf16[64,512]{1,0:T(8,128)(2,1)S(1)}, u32[]{:S(2)}, u32[]{:S(2)}) collective-permute-start(bf16[64,512]{1,0:T(8,128)(2,1)S(1)} %get-tuple-element.89), channel_id=1, source_target_pairs={{0,4},{4,0},{8,12},{12,8},{16,20},{20,16},{24,28},{28,24},{1,5},{5... | collective-permute-start | bytes 196616 | tf_op jit(solution)/shard_map/ppermute | solution.py:109
  180.2 8.2 %collective-permute-start.18 = (bf16[64,512]{1,0:T(8,128)(2,1)S(1)}, bf16[64,512]{1,0:T(8,128)(2,1)S(1)}, u32[]{:S(2)}, u32[]{:S(2)}) collective-permute-start(bf16[64,512]{1,0:T(8,128)(2,1)S(1)} %get-tuple-element.90), channel_id=1, source_target_pairs={{0,8},{4,12},{8,0},{12,4},{16,24},{20,28},{24,16},{28,20},{1,9},{5... | collective-permute-start | bytes 196616 | tf_op jit(solution)/shard_map/ppermute | solution.py:109
  180.2 11.3 %collective-permute-start.19 = (bf16[64,512]{1,0:T(8,128)(2,1)S(1)}, bf16[64,512]{1,0:T(8,128)(2,1)S(1)}, u32[]{:S(2)}, u32[]{:S(2)}) collective-permute-start(bf16[64,512]{1,0:T(8,128)(2,1)S(1)} %get-tuple-element.91), channel_id=1, source_target_pairs={{0,12},{4,8},{8,4},{12,0},{16,28},{20,24},{24,20},{28,16},{1,13},{... | collective-permute-start | bytes 196616 | tf_op jit(solution)/shard_map/ppermute | solution.py:109
  182.5 8.9 %collective-permute-start.20 = (bf16[64,512]{1,0:T(8,128)(2,1)S(1)}, bf16[64,512]{1,0:T(8,128)(2,1)S(1)}, u32[]{:S(2)}, u32[]{:S(2)}) collective-permute-start(bf16[64,512]{1,0:T(8,128)(2,1)S(1)} %get-tuple-element.92), channel_id=1, source_target_pairs={{0,16},{4,20},{8,24},{12,28},{16,0},{20,4},{24,8},{28,12},{1,17},{... | collective-permute-start | bytes 196616 | tf_op jit(solution)/shard_map/ppermute | solution.py:109
  184.8 8.5 %collective-permute-start.21 = (bf16[64,512]{1,0:T(8,128)(2,1)S(1)}, bf16[64,512]{1,0:T(8,128)(2,1)S(1)}, u32[]{:S(2)}, u32[]{:S(2)}) collective-permute-start(bf16[64,512]{1,0:T(8,128)(2,1)S(1)} %get-tuple-element.93), channel_id=1, source_target_pairs={{0,20},{4,16},{8,28},{12,24},{16,4},{20,0},{24,12},{28,8},{1,21},{... | collective-permute-start | bytes 196616 | tf_op jit(solution)/shard_map/ppermute | solution.py:109
  186.1 7.2 %collective-permute-start.22 = (bf16[64,512]{1,0:T(8,128)(2,1)S(1)}, bf16[64,512]{1,0:T(8,128)(2,1)S(1)}, u32[]{:S(2)}, u32[]{:S(2)}) collective-permute-start(bf16[64,512]{1,0:T(8,128)(2,1)S(1)} %get-tuple-element.94), channel_id=1, source_target_pairs={{0,24},{4,28},{8,16},{12,20},{16,8},{20,12},{24,0},{28,4},{1,25},{... | collective-permute-start | bytes 196616 | tf_op jit(solution)/shard_map/ppermute | solution.py:109
  188.3 7.0 %collective-permute-start.23 = (bf16[64,512]{1,0:T(8,128)(2,1)S(1)}, bf16[64,512]{1,0:T(8,128)(2,1)S(1)}, u32[]{:S(2)}, u32[]{:S(2)}) collective-permute-start(bf16[64,512]{1,0:T(8,128)(2,1)S(1)} %get-tuple-element.95), channel_id=1, source_target_pairs={{0,28},{4,24},{8,20},{12,16},{16,12},{20,8},{24,4},{28,0},{1,29},{... | collective-permute-start | bytes 196616 | tf_op jit(solution)/shard_map/ppermute | solution.py:109
  (25 other events, 110.1 us)
where the time goes:
time: 200 us; the launch traced here: 197 us
  starting transfers between devices  69.9 us (35%)
  Pallas kernels  60.4 us (30%)
  waiting for transfers between devices  46.9 us (23%)
  local copies, waits for them, and re-layouts  14.9 us (7%)
  matrix products  2.24 us (1%)
    ppermute x35, starting transfers between devices, exchange(): lax.ppermute(pieces[k], axis, [(i, i ^ k) for i in range(count)])  61.6 us
    ppermute x35, waiting for transfers between devices, exchange(): lax.ppermute(pieces[k], axis, [(i, i ^ k) for i in range(count)])  46.9 us
    pallas_call x2, Pallas kernels, per_device(): pl.pallas_call(functools.partial(state_kernel, groups, blocks, heads, tok...  37.2 us
    pallas_call x2, Pallas kernels, per_device(): pl.pallas_call(functools.partial(output_kernel, groups, blocks, tok, b),...  18.6 us
    unnamed x65, local copies, waits for them, and re-layouts  14.7 us
    ppermute x6, starting transfers between devices, before(): part = lax.ppermute(payload, 'seq', pairs)  8.24 us
  transfers between devices with their start and end apart: 41, of which 10 were waited for; matrix products, arithmetic and copies ran while one was open for 2% of the time, Pallas kernels for 30%

commit v1 on v0

v1 whole, which is shorter than its diff:
```python
import functools

import jax
import jax.numpy as jnp
from jax import lax
from jax.experimental import pallas as pl
from jax.experimental.pallas import tpu as pltpu
from jax.sharding import PartitionSpec as P

DK = 128
BLOCK = 128
norm_eps = 1e-06
LOG2E = 1.4426950408889634
f32 = jnp.float32
bf16 = jnp.bfloat16
ANY = pl.BlockSpec(memory_space=pl.ANY)
VMEM = pl.BlockSpec(memory_space=pltpu.VMEM)
SMEM = pl.BlockSpec(memory_space=pltpu.SMEM)


def params(mib=48):
    return pltpu.CompilerParams(vmem_limit_bytes=mib * 1024 * 1024)


def misc_rows(total_heads):
    return -(-(total_heads + 2) // 16) * 16


def cost(flops, nbytes):
    return pl.CostEstimate(flops=int(flops), bytes_accessed=int(nbytes), transcendentals=0)


def dot(a, b, dims=((1,), (0,))):
    return lax.dot_general(
        a.astype(bf16), b.astype(bf16), (dims, ((), ())), preferred_element_type=f32
    )


def split(a):
    high = a.astype(bf16)
    return high, (a - high.astype(f32)).astype(bf16)


def dot3(a, b, dims=((1,), (0,))):
    ah, al = split(a)
    bh, bl = split(b)
    return dot(ah, bh, dims) + (dot(ah, bl, dims) + dot(al, bh, dims))


NT = ((1,), (1,))


def pack_kv_kernel(sub, batch, heads, key_ref, value_ref, latent_ref, beta_ref, mark_ref, kind_ref, *rest):
    outs, (extra, sem) = rest[:sub], rest[sub:]
    lo = lax.rem(lax.axis_index("head"), sub)
    rows, width = key_ref.shape[1], key_ref.shape[2] // sub
    copies = []
    for k in range(sub):
        col = pl.multiple_of((lo ^ k) * width, width)
        for i, ref in enumerate((key_ref, value_ref)):
            copies.append(
                pltpu.make_async_copy(
                    ref.at[batch, :, pl.ds(col, width)], outs[k].at[pl.ds(i * rows, rows)], sem.at[k, i]
                )
            )
            copies[-1].start()
    extra[...] = jnp.zeros_like(extra)
    lanes = width // 128
    wide = jnp.concatenate(
        [
            beta_ref[batch].astype(f32),
            mark_ref[batch].astype(f32),
            kind_ref[batch].astype(f32),
            jnp.zeros((rows, 128 - heads - 2), f32),
        ],
        axis=1,
    )
    turned = jnp.transpose(jnp.concatenate([wide, jnp.zeros((128 - rows, 128), f32)], axis=0)).astype(bf16)
    chunks = [latent_ref[batch, 16 * j : 16 * j + 16] for j in range(rows // 16)]
    chunks += [turned[16 * j : 16 * j + 16] for j in range(misc_rows(heads) // 16)]
    for c, chunk in enumerate(chunks):
        extra[16 * (c // lanes) : 16 * (c // lanes) + 16, (c % lanes) * 128 : (c % lanes + 1) * 128] = chunk
    for k in range(sub):
        copies.append(pltpu.make_async_copy(extra, outs[k].at[pl.ds(2 * rows, extra.shape[0])], sem.at[k, 2]))
        copies[-1].start()
    for c in copies:
        c.wait()


def pack_q_kernel(sub, batches, query_ref, *rest):
    outs, sem = rest[-sub - 1 : -1], rest[-1]
    lo = lax.rem(lax.axis_index("head"), sub)
    rows, width = query_ref.shape[1], query_ref.shape[2] // sub
    copies = []
    for k in range(sub):
        col = pl.multiple_of((lo ^ k) * width, width)
        for b in range(batches):
            copies.append(
                pltpu.make_async_copy(
                    query_ref.at[b, :, pl.ds(col, width)], outs[k].at[pl.ds(b * rows, rows)], sem.at[k, b]
                )
            )
            copies[-1].start()
    for c in copies:
        c.wait()


def exchange(pieces):
    count = lax.axis_size("head")
    got = {
        k: lax.ppermute(pieces[k], "head", [(i, i ^ k) for i in range(count)]) for k in range(len(pieces) - 1, 0, -1)
    }
    return [pieces[0]] + [got[k] for k in range(1, len(pieces))]


def state_kernel(sub, outer, blocks, heads, tok, hp, decay_ref, *rest):
    pieces = rest[:sub]
    up_ref, bias_ref = rest[sub : sub + 2]
    w_ref, u_ref, shrink_ref, growth_ref, opre_ref, mpre_ref, mask_ref, alive_ref = rest[sub + 2 : sub + 10]
    parts = rest[sub + 10 : sub + 10 + outer]
    buf, up, levels, kinds, lasts, betas, gates, spans, sem, part_sem = rest[sub + 10 + outer :]
    me = lax.rem(lax.axis_index("head"), sub)
    hi = lax.div(lax.axis_index("head"), sub)
    total_heads = heads * sub
    width = heads * DK
    per = BLOCK // tok
    row = lax.broadcasted_iota(jnp.int32, (BLOCK, BLOCK), 0)
    col = lax.broadcasted_iota(jnp.int32, (BLOCK, BLOCK), 1)
    low = (row >= col).astype(f32)
    low_b = low.astype(bf16)
    up_b = (row <= col).astype(bf16)
    unit_mat = (row == col).astype(bf16)
    count = BLOCK.bit_length() - 1
    step = pl.program_id(0)

    @pl.when(step == 0)
    def _():
        copies = [pltpu.make_async_copy(pieces[k], buf.at[me ^ k], sem.at[k]) for k in range(sub)]
        copies.append(
            pltpu.make_async_copy(up_ref.at[:, pl.ds(pl.multiple_of(me * width, width), width)], up, sem.at[sub])
        )
        for c in copies:
            c.start()
        for level in range(count):
            size = 2**level
            here = (row // size == col // size + 1) & ((row // size) % 2 == 1)
            levels[level] = here.astype(bf16)
        for c in copies:
            c.wait()
        lanes = width // 128
        misc = misc_rows(total_heads)

        def chunk(source, c):
            at = 2 * tok + 16 * (c // lanes)
            return buf[source, at : at + 16, (c % lanes) * 128 : (c % lanes + 1) * 128]

        for n in range(blocks):
            tall = []
            for s in range(n * per, (n + 1) * per):
                values = [chunk(s, tok // 16 + j).astype(f32) for j in range(misc // 16)]
                values.append(jnp.zeros((128 - misc, 128), f32))
                tall.append(jnp.transpose(jnp.concatenate(values, axis=0))[:tok])
            tall = jnp.concatenate(tall, axis=0)
            sig = jax.nn.sigmoid(tall)
            for h in range(heads):
                mine = jnp.sum(jnp.where(col == me * heads + h, sig, 0.0), axis=1, keepdims=True)
                betas[h, n] = jnp.broadcast_to(mine, (BLOCK, BLOCK))
            mark = jnp.broadcast_to(tall[:, total_heads : total_heads + 1], (BLOCK, BLOCK))
            own = dot(low_b, mark)
            other = dot(jnp.transpose(mark), up_b)
            mask_ref[n] = jnp.where(own == other, low, 0.0)
            alive_ref[n] = (own == 0).astype(f32)
            lasts[n] = (own == other[:, BLOCK - 1 : BLOCK]).astype(f32)
            kinds[n] = jnp.broadcast_to(tall[:, total_heads + 1 : total_heads + 2], (BLOCK, BLOCK))
            gates[n] = jnp.concatenate(
                [chunk(s, j) for s in range(n * per, (n + 1) * per) for j in range(tok // 16)], axis=0
            )

    low2 = jnp.concatenate([low_b, low_b], axis=1)
    lower = (row > col).astype(f32)
    items = [(i, n) for i in range(hp) for n in range(blocks)]
    strict_all, rhs_all, tail_all, carry_all = {}, {}, {}, {}
    for i in range(hp):
        h = step * hp + i
        at = pl.ds(pl.multiple_of(h * DK, DK), DK)
        bias_at = pl.ds(pl.multiple_of(me * width + h * DK, DK), DK)
        audio, text = bias_ref[0:1, bias_at], bias_ref[1:2, bias_at]
        rate = -LOG2E * jnp.exp(jnp.full((1, DK), decay_ref[me * heads + h], f32))
        for n in range(blocks):
            gate = dot(gates[n], up[:, at]).astype(bf16).astype(f32)
            pre = gate + jnp.where(kinds[n] == 1.0, text, audio)
            soft = jnp.maximum(pre, 0.0) + jnp.log(1.0 + jnp.exp(-jnp.abs(pre)))
            high, rest_part = split(rate * soft)
            total = dot(low2, jnp.concatenate([high, rest_part], axis=0))
            key = buf[n * per : (n + 1) * per, 0:tok, at].reshape(BLOCK, DK).astype(f32)
            value = buf[n * per : (n + 1) * per, tok : 2 * tok, at].reshape(BLOCK, DK).astype(f32)
            unit = key * lax.rsqrt(jnp.sum(key * key, axis=1, keepdims=True) + norm_eps)
            growth = jnp.exp2(total)
            grown = unit * growth
            shrunk, shrunk_rest = split(unit * jnp.exp2(-total))
            last = total[BLOCK - 1 : BLOCK]
            tail = unit * (jnp.exp2(last - total) * lasts[n])
            carry = jnp.exp2(last) * alive_ref[n, BLOCK - 1 : BLOCK]
            beta = betas[h, n]
            growth_ref[i, n] = growth
            shrink_ref[i, n, :, :DK] = shrunk
            shrink_ref[i, n, :, DK:] = shrunk_rest
            gram = dot(grown, shrunk, NT)
            strict_all[i, n] = (gram * (mask_ref[n] * lower) * beta).astype(bf16)
            rhs_all[i, n] = jnp.concatenate([beta * grown * alive_ref[n], beta * value], axis=1)
            tail_all[i, n] = jnp.transpose(tail)
            carry_all[i, n] = carry
    turned = jnp.transpose(jnp.concatenate([carry_all[t] for t in items] + [jnp.zeros((BLOCK - len(items), DK), f32)]))
    carry_all = {t: turned[:, j : j + 1] for j, t in enumerate(items)}
    inv = {t: unit_mat - strict_all[t] * levels[0] for t in items}
    for level in range(1, count):
        size = 2**level
        corner = {t: strict_all[t] * levels[level] for t in items}
        if size < 16:
            turn = {t: dot(inv[t], corner[t]) for t in items}
            inv = {t: inv[t] - dot(turn[t], inv[t]).astype(bf16) for t in items}
        else:
            pairs = BLOCK // (2 * size)
            four = {t: inv[t].reshape(pairs, 2, size, BLOCK) for t in items}
            odd = {t: four[t][:, 1].reshape(BLOCK // 2, BLOCK) for t in items}
            turn = {t: dot(odd[t], corner[t]) for t in items}
            odd = {t: odd[t] - dot(turn[t], inv[t]).astype(bf16) for t in items}
            inv = {
                t: jnp.stack([four[t][:, 0], odd[t].reshape(pairs, size, BLOCK)], axis=1).reshape(BLOCK, BLOCK)
                for t in items
            }
    both = {t: rhs_all[t] + dot(inv[t] - unit_mat, rhs_all[t]) for t in items}
    fade, offs = {}, {}
    for t in items:
        i, n = t
        w = both[t][:, :DK].astype(bf16)
        w_ref[i, n] = w
        u_ref[i, n] = both[t][:, DK:]
        uh, ul = split(both[t][:, DK:])
        th, tl = split(tail_all[t])
        joint = dot(th, jnp.concatenate([w, uh], axis=1))
        fade[t] = joint[:, :DK]
        offs[t] = joint[:, DK:] + dot(jnp.concatenate([th, tl], axis=1), jnp.concatenate([ul, uh], axis=0))
    offset = {i: offs[i, 0] for i in range(hp)}
    move = {i: jnp.where(row == col, carry_all[i, 0], 0.0) - fade[i, 0] for i in range(hp)}
    for n in range(1, blocks):
        for i in range(hp):
            opre_ref[i, n - 1] = offset[i]
            mpre_ref[i, n - 1] = move[i].astype(bf16)
            joint = dot(fade[i, n], jnp.concatenate([offset[i], move[i]], axis=1))
            offset[i] = carry_all[i, n] * offset[i] + offs[i, n] - joint[:, :DK]
            move[i] = carry_all[i, n] * move[i] - joint[:, DK:]
    for i in range(hp):
        spans[step * hp + i] = jnp.concatenate([offset[i], move[i]], axis=1).astype(bf16)

    @pl.when(step == pl.num_programs(0) - 1)
    def _():
        share = heads // outer
        copies = [
            pltpu.make_async_copy(spans.at[pl.ds((hi ^ j) * share, share)], parts[j], part_sem.at[j])
            for j in range(outer)
        ]
        for c in copies:
            c.start()
        for c in copies:
            c.wait()


def joined(later, earlier):
    both = dot(later[1], jnp.concatenate([earlier[0], earlier[1]], axis=1))
    return (later[0].astype(f32) + both[:, :DK]).astype(bf16), both[:, DK:].astype(bf16)


def ordered(outer, parts, order):
    hi = lax.div(lax.axis_index("head"), lax.axis_size("head") // outer)
    for j in range(outer):
        order[hi ^ j] = parts[j][...]


def compose_kernel(outer, share, *rest):
    parts, out_ref, order = rest[:outer], rest[outer], rest[outer + 1]
    ordered(outer, parts, order)
    for h in range(share):
        whole = (order[0, h, :, :DK], order[0, h, :, DK:])
        for o in range(1, outer):
            whole = joined((order[o, h, :, :DK], order[o, h, :, DK:]), whole)
        out_ref[h, :, :DK] = whole[0]
        out_ref[h, :, DK:] = whole[1]


def seed_kernel(outer, share, raw, *rest):
    parts = rest[:outer]
    early_ref, in_ref = rest[outer : outer + 2]
    outs = rest[outer + 2 : 2 * outer + 2]
    order, seeds = rest[2 * outer + 2 :]
    hi = lax.div(lax.axis_index("head"), lax.axis_size("head") // outer)
    ordered(outer, parts, order)
    row = lax.broadcasted_iota(jnp.int32, (DK, DK), 0)
    col = lax.broadcasted_iota(jnp.int32, (DK, DK), 1)
    odd = lax.rem(lax.axis_index("seq"), 2) == 1
    for h in range(share):
        incoming = in_ref[h]
        through = dot(early_ref[h, :, DK:], incoming)
        if raw:
            through = jnp.where(odd, through, incoming.astype(f32))
        state = (early_ref[h, :, :DK].astype(f32) + through).astype(bf16)
        seeds[0, h] = state
        for o in range(1, outer):
            moved = dot(order[o - 1, h, :, DK:], state)
            state = (order[o - 1, h, :, :DK].astype(f32) + moved).astype(bf16)
            seeds[o, h] = state
    for j in range(outer):
        outs[j][...] = seeds[hi ^ j]


def output_kernel(sub, outer, blocks, heads, tok, batch, hp, *rest):
    pieces = rest[:sub]
    w_ref, u_ref, shrink_ref, growth_ref, opre_ref, mpre_ref, mask_ref, alive_ref = rest[sub : sub + 8]
    seeds = rest[sub + 8 : sub + 8 + outer]
    outs = rest[sub + 8 + outer : 2 * sub + 8 + outer]
    buf, obuf, begin, sem, osem, seed_sem = rest[2 * sub + 8 + outer :]
    step = pl.program_id(0)
    lo = lax.rem(lax.axis_index("head"), sub)
    hi = lax.div(lax.axis_index("head"), sub)
    per = BLOCK // tok

    @pl.when(step == 0)
    def _():
        share = heads // outer
        copies = [
            pltpu.make_async_copy(pieces[k].at[pl.ds(batch * tok, tok)], buf.at[lo ^ k], sem.at[k])
            for k in range(sub)
        ]
        copies += [
            pltpu.make_async_copy(seeds[j], begin.at[pl.ds((hi ^ j) * share, share)], seed_sem.at[j])
            for j in range(outer)
        ]
        for c in copies:
            c.start()
        for c in copies:
            c.wait()

    items = [(i, n) for i in range(hp) for n in range(blocks)]
    at = [pl.ds(pl.multiple_of((step * hp + i) * DK, DK), DK) for i in range(hp)]
    start = [begin[step * hp + i].astype(f32) for i in range(hp)]
    states = {
        (i, n): start[i] if n == 0 else opre_ref[i, n - 1] + dot(mpre_ref[i, n - 1], start[i]) for i, n in items
    }
    grown, mix = {}, {}
    for i, n in items:
        query = buf[n * per : (n + 1) * per, :, at[i]].reshape(BLOCK, DK).astype(f32)
        unit = query * (lax.rsqrt(jnp.sum(query * query, axis=1, keepdims=True) + norm_eps) * DK ** (-0.5))
        grown[i, n] = unit * growth_ref[i, n]
        gh, gl = split(grown[i, n])
        shrunk = shrink_ref[i, n]
        mix[i, n] = mask_ref[n] * dot(
            jnp.concatenate([gh, gh, gl], axis=1), jnp.concatenate([shrunk, shrunk[:, :DK]], axis=1), NT
        )
    fresh = {(i, n): u_ref[i, n] - dot(w_ref[i, n], states[i, n]) for i, n in items}
    for i, n in items:
        fh, fl = split(fresh[i, n])
        mh, ml = split(mix[i, n])
        live = (grown[i, n] * alive_ref[n]).astype(bf16)
        core = dot(
            jnp.concatenate([live, mh, mh, ml], axis=1),
            jnp.concatenate([states[i, n].astype(bf16), fh, fl, fh], axis=0),
        )
        obuf[n * per : (n + 1) * per, :, at[i]] = core.astype(bf16).reshape(per, tok, DK)

    @pl.when(step == pl.num_programs(0) - 1)
    def _():
        copies = [pltpu.make_async_copy(obuf.at[lo ^ k], outs[k], osem.at[k]) for k in range(sub)]
        for c in copies:
            c.start()
        for c in copies:
            c.wait()


def finish_kernel(sub, heads, *rest):
    pieces = rest[:sub]
    gate_ref, gain_ref = rest[sub : sub + 2]
    out_ref = rest[-1]
    me = lax.rem(lax.axis_index("head"), sub)
    for k in range(sub):
        for h in range(heads):
            at = pl.ds(pl.multiple_of((me ^ k) * (heads * DK) + h * DK, DK), DK)
            core = pieces[k][:, h * DK : (h + 1) * DK].astype(f32)
            normed = core * lax.rsqrt(jnp.mean(core * core, axis=1, keepdims=True) + norm_eps)
            out_ref[0, :, at] = (normed * gain_ref[:, at] * jax.nn.sigmoid(gate_ref[0, :, at].astype(f32))).astype(bf16)


def product(a, b):
    return jnp.einsum("hij,hjk->hik", a, b, preferred_element_type=f32)


def before(span):
    count = lax.axis_size("seq")
    place = lax.axis_index("seq")
    unit_mat = jnp.broadcast_to(jnp.eye(DK, dtype=bf16), span.shape[:1] + (DK, DK))
    raw = True
    early, whole = None, span
    size = 1
    while size < count:
        final = 2 * size >= count
        payload = whole[..., :DK] if final else whole
        got = None
        for t in range(size):
            pairs = [
                (base + size - 1, base + size + t)
                for base in range(0, count, 2 * size)
                if base + size + t < count
            ]
            part = lax.ppermute(payload, "seq", pairs)
            got = part if got is None else got + part
        if final:
            break
        right = (place // size) % 2 == 1
        if size == 1:
            early = got
        else:
            e_move = early[..., DK:]
            if raw:
                e_move = jnp.where(place % 2 == 1, e_move, unit_mat)
            raw = False
            moved = product(e_move, got)
            early = jnp.concatenate(
                [
                    (early[..., :DK].astype(f32) + moved[..., :DK]).astype(bf16),
                    jnp.where(right, moved[..., DK:].astype(bf16), e_move),
                ],
                axis=2,
            )
        moved = product(whole[..., DK:], got)
        whole = jnp.concatenate(
            [
                (whole[..., :DK].astype(f32) + moved[..., :DK]).astype(bf16),
                jnp.where(right, moved[..., DK:].astype(bf16), whole[..., DK:]),
            ],
            axis=2,
        )
        size *= 2
    if early is None:
        early = jnp.concatenate([jnp.zeros_like(unit_mat), unit_mat], axis=2)
    return early, got, raw


def per_device(
    query_rows,
    key_rows,
    value_rows,
    beta_raw,
    gate_latent,
    gate_up,
    dt_bias,
    decay_log,
    boundary,
    modality,
    out_gate,
    norm_gain,
):
    places = lax.axis_size("head")
    batches, tok, columns = query_rows.shape
    sub = min(places, 4)
    outer = places // sub
    total_heads = columns // DK
    heads = total_heads // sub
    share = heads // outer
    width = heads * DK
    blocks = tok * sub // BLOCK
    sds = jax.ShapeDtypeStruct
    extra_rows = 16 * -(-(tok // 16 + misc_rows(total_heads) // 16) // (width // 128))
    piece_rows = 2 * tok + extra_rows
    mark3, kind3 = boundary[..., None], modality[..., None]

    def pack_kv(batch):
        return pl.pallas_call(
            functools.partial(pack_kv_kernel, sub, batch, total_heads),
            out_shape=[sds((piece_rows, width), bf16)] * sub,
            in_specs=[ANY, ANY] + [VMEM] * 4,
            out_specs=[ANY] * sub,
            scratch_shapes=[pltpu.VMEM((extra_rows, width), bf16), pltpu.SemaphoreType.DMA((sub, 3))],
            compiler_params=params(),
            cost_estimate=cost(0, 4 * sub * piece_rows * width),
            name=f"pack_kv_{batch}",
        )(key_rows, value_rows, gate_latent, beta_raw, mark3, kind3)

    kv = [exchange(pack_kv(b)) for b in range(batches)]
    hp = max(1, 8 // blocks)
    while heads % hp:
        hp -= 1
    before_rows = max(1, blocks - 1)

    def by_head(*dims):
        return pl.BlockSpec((hp, *dims), lambda i: (i,) + (0,) * len(dims))

    per_head = by_head(blocks, DK, DK)
    wide_head = by_head(blocks, DK, 2 * DK)
    pre_head = by_head(before_rows, DK, DK)
    whole = pl.BlockSpec((blocks, BLOCK, BLOCK), lambda i: (0, 0, 0))
    square = (heads, blocks, DK, DK)
    levels = BLOCK.bit_length() - 1
    local, seeds = [], []
    q_here = None
    for b in range(batches):
        made = pl.pallas_call(
            functools.partial(state_kernel, sub, outer, blocks, heads, tok, hp),
            grid=(heads // hp,),
            out_shape=[
                sds(square, bf16),
                sds(square, f32),
                sds((heads, blocks, DK, 2 * DK), bf16),
                sds(square, f32),
                sds((heads, before_rows, DK, DK), f32),
                sds((heads, before_rows, DK, DK), bf16),
                sds((blocks, BLOCK, BLOCK), f32),
                sds((blocks, BLOCK, BLOCK), f32),
            ]
            + [sds((share, DK, 2 * DK), bf16)] * outer,
            in_specs=[SMEM] + [ANY] * sub + [ANY, VMEM],
            out_specs=[per_head, per_head, wide_head, per_head, pre_head, pre_head, whole, whole] + [ANY] * outer,
            scratch_shapes=[
                pltpu.VMEM((sub, piece_rows, width), bf16),
                pltpu.VMEM((DK, width), bf16),
                pltpu.VMEM((levels, BLOCK, BLOCK), bf16),
                pltpu.VMEM((blocks, BLOCK, BLOCK), f32),
                pltpu.VMEM((blocks, BLOCK, BLOCK), f32),
                pltpu.VMEM((heads, blocks, BLOCK, BLOCK), f32),
                pltpu.VMEM((blocks, BLOCK, BLOCK), bf16),
                pltpu.VMEM((heads, DK, 2 * DK), bf16),
                pltpu.SemaphoreType.DMA((sub + 1,)),
                pltpu.SemaphoreType.DMA((outer,)),
            ],
            compiler_params=params(),
            cost_estimate=cost(heads * blocks * 24 * 2 * 128**3 * 4, 8 * 2**20),
            name=f"state_maps_{b}",
        )(decay_log, *kv[b], gate_up, dt_bias)
        local.append(made[:8])
        if q_here is None:
            q_here = exchange(
                pl.pallas_call(
                    functools.partial(pack_q_kernel, sub, batches),
                    out_shape=[sds((batches * tok, width), bf16)] * sub,
                    in_specs=[ANY, ANY],
                    out_specs=[ANY] * sub,
                    scratch_shapes=[pltpu.SemaphoreType.DMA((sub, batches))],
                    compiler_params=params(),
                    cost_estimate=cost(0, 4 * sub * batches * tok * width),
                    name="pack_q",
                )(query_rows, made[-1])
            )
        count = lax.axis_size("head")

        def swap(parts):
            return [parts[0]] + [
                lax.ppermute(parts[j], "head", [(i, i ^ (j * sub)) for i in range(count)]) for j in range(1, outer)
            ]

        parts = swap(made[8:])
        total = pl.pallas_call(
            functools.partial(compose_kernel, outer, share),
            out_shape=sds((share, DK, 2 * DK), bf16),
            in_specs=[VMEM] * outer,
            out_specs=VMEM,
            scratch_shapes=[pltpu.VMEM((outer, share, DK, 2 * DK), bf16)],
            compiler_params=params(),
            cost_estimate=cost(share * outer * 4 * 128**3, 2**20),
            name=f"compose_{b}",
        )(*parts)
        early, incoming, raw = before(total)
        mine = pl.pallas_call(
            functools.partial(seed_kernel, outer, share, raw),
            out_shape=[sds((share, DK, DK), bf16)] * outer,
            in_specs=[VMEM] * (outer + 2),
            out_specs=[VMEM] * outer,
            scratch_shapes=[
                pltpu.VMEM((outer, share, DK, 2 * DK), bf16),
                pltpu.VMEM((outer, share, DK, DK), bf16),
            ],
            compiler_params=params(),
            cost_estimate=cost(share * outer * 4 * 128**3, 2**20),
            name=f"seeds_{b}",
        )(*parts, early, incoming)
        seeds.append(swap(mine))
    back = []
    for b in range(batches):
        outs = pl.pallas_call(
            functools.partial(output_kernel, sub, outer, blocks, heads, tok, b, hp),
            grid=(heads // hp,),
            out_shape=[sds((tok, width), bf16)] * sub,
            in_specs=[ANY] * sub
            + [per_head, per_head, wide_head, per_head, pre_head, pre_head]
            + [whole] * 2
            + [ANY] * outer,
            out_specs=[ANY] * sub,
            scratch_shapes=[
                pltpu.VMEM((sub, tok, width), bf16),
                pltpu.VMEM((sub, tok, width), bf16),
                pltpu.VMEM((heads, DK, DK), bf16),
                pltpu.SemaphoreType.DMA((sub,)),
                pltpu.SemaphoreType.DMA((sub,)),
                pltpu.SemaphoreType.DMA((outer,)),
            ],
            compiler_params=params(),
            cost_estimate=cost(heads * blocks * 10 * 2 * 128**3 * 4, 8 * 2**20),
            name=f"span_outputs_{b}",
        )(*q_here, *local[b], *seeds[b])
        back.append(exchange(outs))

    mixed = None
    for b in range(batches):
        rows = pl.BlockSpec((1, tok, columns), lambda i, b=b: (b, 0, 0))
        mixed = pl.pallas_call(
            functools.partial(finish_kernel, sub, heads),
            grid=(1,),
            out_shape=sds((batches, tok, columns), bf16),
            in_specs=[pl.BlockSpec((tok, width), lambda i: (0, 0))] * sub
            + [rows, pl.BlockSpec((1, columns), lambda i: (0, 0))]
            + ([] if b == 0 else [ANY]),
            out_specs=rows,
            input_output_aliases={} if b == 0 else {sub + 2: 0},
            compiler_params=params(),
            cost_estimate=cost(20 * tok * columns, 8 * tok * columns),
            name=f"finish_{b}",
        )(*back[b], out_gate, norm_gain[None, :], *([] if b == 0 else [mixed]))
    return mixed


def solution(mesh):
    return jax.shard_map(
        per_device,
        mesh=mesh,
        in_specs=(
            P(None, ("seq", "head"), None),
            P(None, ("seq", "head"), None),
            P(None, ("seq", "head"), None),
            P(None, ("seq", "head"), None),
            P(None, ("seq", "head"), None),
            P(),
            P(),
            P(),
            P(None, ("seq", "head")),
            P(None, ("seq", "head")),
            P(None, ("seq", "head"), None),
            P(),
        ),
        out_specs=P(None, ("seq", "head"), None),
        check_vma=False,
    )
```

time: 200 us -> 110 us (0.55); the launches traced: 197 us -> 110 us
  starting transfers between devices: 69.9 us -> 35.9 us
  Pallas kernels: 60.4 us -> 38.6 us
  waiting for transfers between devices: 46.9 us -> 28.9 us
  local copies, waits for them, and re-layouts: 14.9 us -> 5.49 us
    ppermute x35 -> x19, starting transfers between devices: 61.6 us -> 29.2 us  [the longest x15 20 us: exchange(): lax.ppermute(pieces[k], 'head', [(i, i ^ k) for i in range(count)])]
    pallas_call x9 -> x13, Pallas kernels: 60.4 us -> 38.6 us  [the longest x2 23.2 us: per_device(): pl.pallas_call(functools.partial(state_kernel, sub, outer, blocks, heads,...]
    ppermute x35 -> x19, waiting for transfers between devices: 46.9 us -> 25.5 us  [the longest x4 14.4 us: swap(): lax.ppermute(parts[j], 'head', [(i, i ^ j * sub) for i in range(count)])]
    unnamed x65 -> x21, local copies, waits for them, and re-layouts: 14.7 us -> 5.29 us
    ppermute x6, waiting for transfers between devices: 0.02 us -> 3.38 us  [before(): part = lax.ppermute(payload, 'seq', pairs)]
  transfers between devices with their start and end apart: 41 -> 25, of which waited for: 10 -> 9; matrix products, arithmetic and copies ran while one was open for 2% -> 0% of each run, Pallas kernels for 30% -> 34%
where the time goes in v1:
time: 110 us
  Pallas kernels  38.6 us (35%)
  starting transfers between devices  35.9 us (33%)
  waiting for transfers between devices  28.9 us (26%)
  local copies, waits for them, and re-layouts  5.49 us (5%)
    pallas_call x2, Pallas kernels, per_device(): pl.pallas_call(functools.partial(state_kernel, sub, outer, blocks, heads,...  23.2 us
    ppermute x15, starting transfers between devices, exchange(): lax.ppermute(pieces[k], 'head', [(i, i ^ k) for i in range(count)])  20 us
    ppermute x4, waiting for transfers between devices, swap(): lax.ppermute(parts[j], 'head', [(i, i ^ j * sub) for i in range(count)])  14.4 us
    ppermute x15, waiting for transfers between devices, exchange(): lax.ppermute(pieces[k], 'head', [(i, i ^ k) for i in range(count)])  11.1 us
    pallas_call x2, Pallas kernels, per_device(): pl.pallas_call(functools.partial(output_kernel, sub, outer, blocks, heads...  10.2 us
    ppermute x4, starting transfers between devices, swap(): lax.ppermute(parts[j], 'head', [(i, i ^ j * sub) for i in range(count)])  9.23 us
    ppermute x6, starting transfers between devices, before(): part = lax.ppermute(payload, 'seq', pairs)  6.7 us
    unnamed x21, local copies, waits for them, and re-layouts  5.29 us
  transfers between devices with their start and end apart: 25, of which 9 were waited for; matrix products, arithmetic and copies ran while one was open for 0% of the time, Pallas kernels for 34%

profile of v1, /device:TPU:2, one launch (start us, length us, event | category | flops | bytes accessed | tf_op | source)
XLA Modules:
  0.0 109.6 jit_solution(5837094113065918344)
XLA Ops:
  0.0 0.8 copy.14.beta_ref
  0.8 0.7 copy-done.8
  1.6 0.7 copy-done.9
  2.4 0.7 copy-done.4
  3.0 1.2 %copy-done.1 = bf16[2,64,4096]{2,1,0:T(8,128)(2,1)S(1)} copy-done((bf16[2,64,4096]{2,1,0:T(8,128)(2,1)S(1)}, bf16[2,64,4096]{2,1,0:T(8,128)(2,1)}, u32[]{:S(2)}) %copy-start.1) | copy-done | bytes 1048600
  4.3 1.2 %copy-done.2 = bf16[2,64,4096]{2,1,0:T(8,128)(2,1)S(1)} copy-done((bf16[2,64,4096]{2,1,0:T(8,128)(2,1)S(1)}, bf16[2,64,4096]{2,1,0:T(8,128)(2,1)}, u32[]{:S(2)}) %copy-start.2) | copy-done | bytes 1048600
  5.5 0.6 pack_kv_0.1
  6.1 1.6 %collective-permute-start = (bf16[144,1024]{1,0:T(8,128)(2,1)S(1)}, bf16[144,1024]{1,0:T(8,128)(2,1)S(1)}, u32[]{:S(2)}, u32[]{:S(2)}) collective-permute-start(bf16[144,1024]{1,0:T(8,128)(2,1)S(1)} %get-tuple-element.50), channel_id=1, source_target_pairs={{0,4},{4,0},{8,12},{12,8},{16,20},{20,16},{24,28},{28,24},{1,5},{5... | collective-permute-start | bytes 884744 | tf_op jit(solution)/shard_map/ppermute | solution.py:111
  7.7 1.6 %collective-permute-start.1 = (bf16[144,1024]{1,0:T(8,128)(2,1)S(1)}, bf16[144,1024]{1,0:T(8,128)(2,1)S(1)}, u32[]{:S(2)}, u32[]{:S(2)}) collective-permute-start(bf16[144,1024]{1,0:T(8,128)(2,1)S(1)} %get-tuple-element.51), channel_id=1, source_target_pairs={{0,8},{4,12},{8,0},{12,4},{16,24},{20,28},{24,16},{28,20},{1,9},{5... | collective-permute-start | bytes 884744 | tf_op jit(solution)/shard_map/ppermute | solution.py:111
  9.3 0.4 collective-permute-start.2
  9.7 0.6 pack_kv_1.1
  10.3 1.6 %collective-permute-start.6 = (bf16[144,1024]{1,0:T(8,128)(2,1)S(1)}, bf16[144,1024]{1,0:T(8,128)(2,1)S(1)}, u32[]{:S(2)}, u32[]{:S(2)}) collective-permute-start(bf16[144,1024]{1,0:T(8,128)(2,1)S(1)} %get-tuple-element.59), channel_id=1, source_target_pairs={{0,4},{4,0},{8,12},{12,8},{16,20},{20,16},{24,28},{28,24},{1,5},{5... | collective-permute-start | bytes 884744 | tf_op jit(solution)/shard_map/ppermute | solution.py:111
  11.9 1.6 %collective-permute-start.7 = (bf16[144,1024]{1,0:T(8,128)(2,1)S(1)}, bf16[144,1024]{1,0:T(8,128)(2,1)S(1)}, u32[]{:S(2)}, u32[]{:S(2)}) collective-permute-start(bf16[144,1024]{1,0:T(8,128)(2,1)S(1)} %get-tuple-element.60), channel_id=1, source_target_pairs={{0,8},{4,12},{8,0},{12,4},{16,24},{20,28},{24,16},{28,20},{1,9},{5... | collective-permute-start | bytes 884744 | tf_op jit(solution)/shard_map/ppermute | solution.py:111
  13.5 4.0 %collective-permute-done.rest_1_ = bf16[144,1024]{1,0:T(8,128)(2,1)S(1)} collective-permute-done((bf16[144,1024]{1,0:T(8,128)(2,1)S(1)}, bf16[144,1024]{1,0:T(8,128)(2,1)S(1)}, u32[]{:S(2)}, u32[]{:S(2)}) %collective-permute-start) | collective-permute-done | bytes 294944 | tf_op jit(solution)/shard_map/ppermute | solution.py:111
  17.5 2.5 %collective-permute-start.8 = (bf16[144,1024]{1,0:T(8,128)(2,1)S(1)}, bf16[144,1024]{1,0:T(8,128)(2,1)S(1)}, u32[]{:S(2)}, u32[]{:S(2)}) collective-permute-start(bf16[144,1024]{1,0:T(8,128)(2,1)S(1)} %get-tuple-element.61), channel_id=1, source_target_pairs={{0,12},{4,8},{8,4},{12,0},{16,28},{20,24},{24,20},{28,16},{1,13},{... | collective-permute-start | bytes 884744 | tf_op jit(solution)/shard_map/ppermute | solution.py:111
  20.0 3.9 %collective-permute-done.2.rest_3_ = bf16[144,1024]{1,0:T(8,128)(2,1)S(1)} collective-permute-done((bf16[144,1024]{1,0:T(8,128)(2,1)S(1)}, bf16[144,1024]{1,0:T(8,128)(2,1)S(1)}, u32[]{:S(2)}, u32[]{:S(2)}) %collective-permute-start.2) | collective-permute-done | bytes 294944 | tf_op jit(solution)/shard_map/ppermute | solution.py:111
  24.0 11.5 %state_maps_0.1 = (bf16[8,2,128,128]{3,2,1,0:T(8,128)(2,1)S(1)}, f32[8,2,128,128]{3,2,1,0:T(8,128)S(1)}, bf16[8,2,128,256]{3,2,1,0:T(8,128)(2,1)S(1)}, f32[8,2,1...) custom-call(f32[32]{0:T(128)S(1)} %copy-done.7, ...), custom_call_target="tpu_custom_call" | custom-call | flops 6442450944 | bytes 8388608 | tf_op jit(solution)/shard_map/state_maps_0/pallas_call | solution.py:505
  35.5 2.6 %collective-permute-start.17 = (bf16[4,128,256]{2,1,0:T(8,128)(2,1)S(1)}, bf16[4,128,256]{2,1,0:T(8,128)(2,1)S(1)}, u32[]{:S(2)}, u32[]{:S(2)}) collective-permute-start(bf16[4,128,256]{2,1,0:T(8,128)(2,1)S(1)} %get-tuple-element.53.rest_0_), channel_id=1, source_target_pairs={{0,16},{4,20},{8,24},{12,28},{16,0},{20,4},{24,8},{28,12},{1,17},{... | collective-permute-start | bytes 786440 | tf_op jit(solution)/shard_map/ppermute | solution.py:555
  38.2 11.6 %state_maps_1.1 = (bf16[8,2,128,128]{3,2,1,0:T(8,128)(2,1)S(1)}, f32[8,2,128,128]{3,2,1,0:T(8,128)S(1)}, bf16[8,2,128,256]{3,2,1,0:T(8,128)(2,1)S(1)}, f32[8,2,1...) custom-call(f32[32]{0:T(128)S(1)} %copy-done.7, ...), custom_call_target="tpu_custom_call" | custom-call | flops 6442450944 | bytes 8388608 | tf_op jit(solution)/shard_map/state_maps_1/pallas_call | solution.py:505
  49.8 0.4 collective-permute-start.9
  50.2 0.3 compose_0.1
  50.5 1.3 %collective-permute-start.18 = (bf16[4,128,256]{2,1,0:T(8,128)(2,1)S(1)}, bf16[4,128,256]{2,1,0:T(8,128)(2,1)S(1)}, u32[]{:S(2)}, u32[]{:S(2)}) collective-permute-start(bf16[4,128,256]{2,1,0:T(8,128)(2,1)S(1)} %compose_0.1), channel_id=1, source_target_pairs={{0,1},{2,3},{4,5},{6,7},{8,9},{10,11},{12,13},{14,15},{16,17},{18,... | collective-permute-start | bytes 786440 | tf_op jit(solution)/shard_map/ppermute | solution.py:413
  51.8 9.7 %collective-permute-done.9.rest_1_ = bf16[4,128,256]{2,1,0:T(8,128)(2,1)S(1)} collective-permute-done((bf16[4,128,256]{2,1,0:T(8,128)(2,1)S(1)}, bf16[4,128,256]{2,1,0:T(8,128)(2,1)S(1)}, u32[]{:S(2)}, u32[]{:S(2)}) %collective-permute-start.9) | collective-permute-done | bytes 262176 | tf_op jit(solution)/shard_map/ppermute | solution.py:555
  61.5 0.3 compose_1.1
  61.8 1.3 %collective-permute-start.10 = (bf16[4,128,256]{2,1,0:T(8,128)(2,1)S(1)}, bf16[4,128,256]{2,1,0:T(8,128)(2,1)S(1)}, u32[]{:S(2)}, u32[]{:S(2)}) collective-permute-start(bf16[4,128,256]{2,1,0:T(8,128)(2,1)S(1)} %compose_1.1), channel_id=1, source_target_pairs={{0,1},{2,3},{4,5},{6,7},{8,9},{10,11},{12,13},{14,15},{16,17},{18,... | collective-permute-start | bytes 786440 | tf_op jit(solution)/shard_map/ppermute | solution.py:413
  63.1 0.3 pack_q.1
  63.4 1.6 %collective-permute-start.3 = (bf16[128,1024]{1,0:T(8,128)(2,1)S(1)}, bf16[128,1024]{1,0:T(8,128)(2,1)S(1)}, u32[]{:S(2)}, u32[]{:S(2)}) collective-permute-start(bf16[128,1024]{1,0:T(8,128)(2,1)S(1)} %get-tuple-element.55), channel_id=1, source_target_pairs={{0,4},{4,0},{8,12},{12,8},{16,20},{20,16},{24,28},{28,24},{1,5},{5... | collective-permute-start | bytes 786440 | tf_op jit(solution)/shard_map/ppermute | solution.py:111
  65.2 0.7 collective-permute-start.20
  65.8 1.3 %collective-permute-start.19 = (bf16[4,128,128]{2,1,0:T(8,128)(2,1)S(1)}, bf16[4,128,128]{2,1,0:T(8,128)(2,1)S(1)}, u32[]{:S(2)}, u32[]{:S(2)}) collective-permute-start(bf16[4,128,128]{2,1,0:T(8,128)(2,1)S(1)} %add_convert_fusion), channel_id=1, source_target_pairs={{1,2},{5,6},{9,10},{13,14},{17,18},{21,22},{25,26},{29,30}} | collective-permute-start | bytes 393224 | tf_op jit(solution)/shard_map/ppermute | solution.py:413
  67.3 0.7 collective-permute-start.12
  68.0 2.0 %collective-permute-start.5 = (bf16[128,1024]{1,0:T(8,128)(2,1)S(1)}, bf16[128,1024]{1,0:T(8,128)(2,1)S(1)}, u32[]{:S(2)}, u32[]{:S(2)}) collective-permute-start(bf16[128,1024]{1,0:T(8,128)(2,1)S(1)} %get-tuple-element.57), channel_id=1, source_target_pairs={{0,12},{4,8},{8,4},{12,0},{16,28},{20,24},{24,20},{28,16},{1,13},{... | collective-permute-start | bytes 786440 | tf_op jit(solution)/shard_map/ppermute | solution.py:111
  70.0 2.1 %collective-permute-done.19 = bf16[4,128,128]{2,1,0:T(8,128)(2,1)S(1)} collective-permute-done((bf16[4,128,128]{2,1,0:T(8,128)(2,1)S(1)}, bf16[4,128,128]{2,1,0:T(8,128)(2,1)S(1)}, u32[]{:S(2)}, u32[]{:S(2)}) %collective-permute-start.19) | collective-permute-done | bytes 131104 | tf_op jit(solution)/shard_map/ppermute | solution.py:413
  72.1 1.5 %collective-permute-start.11 = (bf16[4,128,128]{2,1,0:T(8,128)(2,1)S(1)}, bf16[4,128,128]{2,1,0:T(8,128)(2,1)S(1)}, u32[]{:S(2)}, u32[]{:S(2)}) collective-permute-start(bf16[4,128,128]{2,1,0:T(8,128)(2,1)S(1)} %add_convert_fusion.1), channel_id=1, source_target_pairs={{1,2},{5,6},{9,10},{13,14},{17,18},{21,22},{25,26},{29,30}} | collective-permute-start | bytes 393224 | tf_op jit(solution)/shard_map/ppermute | solution.py:413
  73.6 0.4 seeds_0.1
  74.0 3.1 %collective-permute-start.21 = (bf16[4,128,128]{2,1,0:T(8,128)(2,1)S(1)}, bf16[4,128,128]{2,1,0:T(8,128)(2,1)S(1)}, u32[]{:S(2)}, u32[]{:S(2)}) collective-permute-start(bf16[4,128,128]{2,1,0:T(8,128)(2,1)S(1)} %get-tuple-element.88), channel_id=1, source_target_pairs={{0,16},{4,20},{8,24},{12,28},{16,0},{20,4},{24,8},{28,12},{1,17},{... | collective-permute-start | bytes 393224 | tf_op jit(solution)/shard_map/ppermute | solution.py:555
  77.1 1.3 %collective-permute-done.11 = bf16[4,128,128]{2,1,0:T(8,128)(2,1)S(1)} collective-permute-done((bf16[4,128,128]{2,1,0:T(8,128)(2,1)S(1)}, bf16[4,128,128]{2,1,0:T(8,128)(2,1)S(1)}, u32[]{:S(2)}, u32[]{:S(2)}) %collective-permute-start.11) | collective-permute-done | bytes 131104 | tf_op jit(solution)/shard_map/ppermute | solution.py:413
  78.4 0.4 seeds_1.1
  78.8 3.1 %collective-permute-start.13 = (bf16[4,128,128]{2,1,0:T(8,128)(2,1)S(1)}, bf16[4,128,128]{2,1,0:T(8,128)(2,1)S(1)}, u32[]{:S(2)}, u32[]{:S(2)}) collective-permute-start(bf16[4,128,128]{2,1,0:T(8,128)(2,1)S(1)} %get-tuple-element.73), channel_id=1, source_target_pairs={{0,16},{4,20},{8,24},{12,28},{16,0},{20,4},{24,8},{28,12},{1,17},{... | collective-permute-start | bytes 393224 | tf_op jit(solution)/shard_map/ppermute | solution.py:555
  81.9 4.7 %collective-permute-done.21.rest_13_ = bf16[4,128,128]{2,1,0:T(8,128)(2,1)S(1)} collective-permute-done((bf16[4,128,128]{2,1,0:T(8,128)(2,1)S(1)}, bf16[4,128,128]{2,1,0:T(8,128)(2,1)S(1)}, u32[]{:S(2)}, u32[]{:S(2)}) %collective-permute-start.21) | collective-permute-done | bytes 131104 | tf_op jit(solution)/shard_map/ppermute | solution.py:555
  86.6 5.1 %span_outputs_0.1 = (bf16[64,1024]{1,0:T(8,128)(2,1)S(1)}, bf16[64,1024]{1,0:T(8,128)(2,1)S(1)}, bf16[64,1024]{1,0:T(8,128)(2,1)S(1)}, bf16[64,1024]{1,0:T(8,128)(2,1)S(1)}) custom-call(bf16[128,1024]{1,0:T(8,128)(2,1)S(1)} %get-tuple-element.54.rest_0_, bf16[128,1024]{1,0:T(8,128)(2,1)S(1)} %collective-permute-done.3.rest_1_, ...), custom_call_target="tpu_custom_call" | custom-call | flops 2684354560 | bytes 8388608 | tf_op jit(solution)/shard_map/span_outputs_0/pallas_call | solution.py:586
  91.8 0.3 collective-permute-start.23
  92.1 3.1 %collective-permute-start.24 = (bf16[64,1024]{1,0:T(8,128)(2,1)S(1)}, bf16[64,1024]{1,0:T(8,128)(2,1)S(1)}, u32[]{:S(2)}, u32[]{:S(2)}) collective-permute-start(bf16[64,1024]{1,0:T(8,128)(2,1)S(1)} %get-tuple-element.92), channel_id=1, source_target_pairs={{0,12},{4,8},{8,4},{12,0},{16,28},{20,24},{24,20},{28,16},{1,13},{... | collective-permute-start | bytes 393224 | tf_op jit(solution)/shard_map/ppermute | solution.py:111
  95.3 5.2 %span_outputs_1.1 = (bf16[64,1024]{1,0:T(8,128)(2,1)S(1)}, bf16[64,1024]{1,0:T(8,128)(2,1)S(1)}, bf16[64,1024]{1,0:T(8,128)(2,1)S(1)}, bf16[64,1024]{1,0:T(8,128)(2,1)S(1)}) custom-call(bf16[128,1024]{1,0:T(8,128)(2,1)S(1)} %get-tuple-element.54.rest_0_, bf16[128,1024]{1,0:T(8,128)(2,1)S(1)} %collective-permute-done.3.rest_1_, ...), custom_call_target="tpu_custom_call" | custom-call | flops 2684354560 | bytes 8388608 | tf_op jit(solution)/shard_map/span_outputs_1/pallas_call | solution.py:586
  100.6 0.5 collective-permute-start.15
  101.1 2.9 %collective-permute-start.16 = (bf16[64,1024]{1,0:T(8,128)(2,1)S(1)}, bf16[64,1024]{1,0:T(8,128)(2,1)S(1)}, u32[]{:S(2)}, u32[]{:S(2)}) collective-permute-start(bf16[64,1024]{1,0:T(8,128)(2,1)S(1)} %get-tuple-element.77), channel_id=1, source_target_pairs={{0,12},{4,8},{8,4},{12,0},{16,28},{20,24},{24,20},{28,16},{1,13},{... | collective-permute-start | bytes 393224 | tf_op jit(solution)/shard_map/ppermute | solution.py:111
  104.0 1.2 %finish_0.1.rest_6_ = bf16[2,64,4096]{2,1,0:T(8,128)(2,1)} custom-call(bf16[64,1024]{1,0:T(8,128)(2,1)S(1)} %get-tuple-element.89.rest_0_, bf16[64,1024]{1,0:T(8,128)(2,1)S(1)} %collective-permute-done.22.rest_1_, bf16[64,1024]{1,0:T(8,128)(2,1)S(1)} %collective-permute-done.23.rest_2_, bf16[64,1024]{1,0:T(8,128)(2,1)S(1)} %collective-permute-done.24.rest_3_, ...), custom_call_target="tpu_custom_call" | custom-call | flops 5242880 | bytes 2097152 | tf_op jit(solution)/shard_map/finish_0/pallas_call | solution.py:612
  105.5 2.8 %collective-permute-done.16.rest_3_ = bf16[64,1024]{1,0:T(8,128)(2,1)S(1)} collective-permute-done((bf16[64,1024]{1,0:T(8,128)(2,1)S(1)}, bf16[64,1024]{1,0:T(8,128)(2,1)S(1)}, u32[]{:S(2)}, u32[]{:S(2)}) %collective-permute-start.16) | collective-permute-done | bytes 131104 | tf_op jit(solution)/shard_map/ppermute | solution.py:111
  108.3 1.2 %finish_1.1 = bf16[2,64,4096]{2,1,0:T(8,128)(2,1)} custom-call(bf16[64,1024]{1,0:T(8,128)(2,1)S(1)} %get-tuple-element.74.rest_0_, bf16[64,1024]{1,0:T(8,128)(2,1)S(1)} %collective-permute-done.14.rest_1_, bf16[64,1024]{1,0:T(8,128)(2,1)S(1)} %collective-permute-done.15.rest_2_, ...), custom_call_target="tpu_custom_call", output_to_operand_aliasing={{}: (6, {})} | custom-call | flops 5242880 | bytes 2097152 | tf_op jit(solution)/shard_map/finish_1/pallas_call | solution.py:612
  (42 shorter events, 1.2 us)
Async XLA Ops:
  0.8 0.7 copy-start.8
  1.6 0.7 copy-start.9
  2.3 0.8 copy-start.4
  3.0 1.2 %copy-start.1 = (bf16[2,64,4096]{2,1,0:T(8,128)(2,1)S(1)}, bf16[2,64,4096]{2,1,0:T(8,128)(2,1)}, u32[]{:S(2)}) copy-start(bf16[2,64,4096]{2,1,0:T(8,128)(2,1)} %key_ref.3) | copy-start | bytes 3145732
  4.3 1.2 %copy-start.2 = (bf16[2,64,4096]{2,1,0:T(8,128)(2,1)S(1)}, bf16[2,64,4096]{2,1,0:T(8,128)(2,1)}, u32[]{:S(2)}) copy-start(bf16[2,64,4096]{2,1,0:T(8,128)(2,1)} %value_ref.3) | copy-start | bytes 3145732
  6.1 11.4 %collective-permute-start = (bf16[144,1024]{1,0:T(8,128)(2,1)S(1)}, bf16[144,1024]{1,0:T(8,128)(2,1)S(1)}, u32[]{:S(2)}, u32[]{:S(2)}) collective-permute-start(bf16[144,1024]{1,0:T(8,128)(2,1)S(1)} %get-tuple-element.50), channel_id=1, source_target_pairs={{0,4},{4,0},{8,12},{12,8},{16,20},{20,16},{24,28},{28,24},{1,5},{5... | collective-permute-start | bytes 884744 | tf_op jit(solution)/shard_map/ppermute | solution.py:111
  7.7 12.3 %collective-permute-start.1 = (bf16[144,1024]{1,0:T(8,128)(2,1)S(1)}, bf16[144,1024]{1,0:T(8,128)(2,1)S(1)}, u32[]{:S(2)}, u32[]{:S(2)}) collective-permute-start(bf16[144,1024]{1,0:T(8,128)(2,1)S(1)} %get-tuple-element.51), channel_id=1, source_target_pairs={{0,8},{4,12},{8,0},{12,4},{16,24},{20,28},{24,16},{28,20},{1,9},{5... | collective-permute-start | bytes 884744 | tf_op jit(solution)/shard_map/ppermute | solution.py:111
  9.3 14.7 %copy-start.6 = (f32[2,4096]{1,0:T(2,128)S(1)}, f32[2,4096]{1,0:T(2,128)}, u32[]{:S(2)}) copy-start(f32[2,4096]{1,0:T(2,128)} %rest_5_.3) | copy-start | bytes 98308
  9.3 14.7 %collective-permute-start.2 = (bf16[144,1024]{1,0:T(8,128)(2,1)S(1)}, bf16[144,1024]{1,0:T(8,128)(2,1)S(1)}, u32[]{:S(2)}, u32[]{:S(2)}) collective-permute-start(bf16[144,1024]{1,0:T(8,128)(2,1)S(1)} %get-tuple-element.52), channel_id=1, source_target_pairs={{0,12},{4,8},{8,4},{12,0},{16,28},{20,24},{24,20},{28,16},{1,13},{... | collective-permute-start | bytes 884744 | tf_op jit(solution)/shard_map/ppermute | solution.py:111
  10.3 27.8 %collective-permute-start.6 = (bf16[144,1024]{1,0:T(8,128)(2,1)S(1)}, bf16[144,1024]{1,0:T(8,128)(2,1)S(1)}, u32[]{:S(2)}, u32[]{:S(2)}) collective-permute-start(bf16[144,1024]{1,0:T(8,128)(2,1)S(1)} %get-tuple-element.59), channel_id=1, source_target_pairs={{0,4},{4,0},{8,12},{12,8},{16,20},{20,16},{24,28},{28,24},{1,5},{5... | collective-permute-start | bytes 884744 | tf_op jit(solution)/shard_map/ppermute | solution.py:111
  11.9 26.3 %collective-permute-start.7 = (bf16[144,1024]{1,0:T(8,128)(2,1)S(1)}, bf16[144,1024]{1,0:T(8,128)(2,1)S(1)}, u32[]{:S(2)}, u32[]{:S(2)}) collective-permute-start(bf16[144,1024]{1,0:T(8,128)(2,1)S(1)} %get-tuple-element.60), channel_id=1, source_target_pairs={{0,8},{4,12},{8,0},{12,4},{16,24},{20,28},{24,16},{28,20},{1,9},{5... | collective-permute-start | bytes 884744 | tf_op jit(solution)/shard_map/ppermute | solution.py:111
  17.5 6.4 %copy-start.7 = (f32[32]{0:T(128)S(1)}, f32[32]{0:T(128)}, u32[]{:S(2)}) copy-start(f32[32]{0:T(128)} %decay_ref.3) | copy-start | bytes 388
  17.5 20.6 %collective-permute-start.8 = (bf16[144,1024]{1,0:T(8,128)(2,1)S(1)}, bf16[144,1024]{1,0:T(8,128)(2,1)S(1)}, u32[]{:S(2)}, u32[]{:S(2)}) collective-permute-start(bf16[144,1024]{1,0:T(8,128)(2,1)S(1)} %get-tuple-element.61), channel_id=1, source_target_pairs={{0,12},{4,8},{8,4},{12,0},{16,28},{20,24},{24,20},{28,16},{1,13},{... | collective-permute-start | bytes 884744 | tf_op jit(solution)/shard_map/ppermute | solution.py:111
  35.5 14.7 %collective-permute-start.17 = (bf16[4,128,256]{2,1,0:T(8,128)(2,1)S(1)}, bf16[4,128,256]{2,1,0:T(8,128)(2,1)S(1)}, u32[]{:S(2)}, u32[]{:S(2)}) collective-permute-start(bf16[4,128,256]{2,1,0:T(8,128)(2,1)S(1)} %get-tuple-element.53.rest_0_), channel_id=1, source_target_pairs={{0,16},{4,20},{8,24},{12,28},{16,0},{20,4},{24,8},{28,12},{1,17},{... | collective-permute-start | bytes 786440 | tf_op jit(solution)/shard_map/ppermute | solution.py:555
  49.8 13.3 %copy-start.3 = (bf16[2,64,4096]{2,1,0:T(8,128)(2,1)S(1)}, bf16[2,64,4096]{2,1,0:T(8,128)(2,1)}, u32[]{:S(2)}) copy-start(bf16[2,64,4096]{2,1,0:T(8,128)(2,1)} %query_ref.1) | copy-start | bytes 3145732
  49.8 11.7 %collective-permute-start.9 = (bf16[4,128,256]{2,1,0:T(8,128)(2,1)S(1)}, bf16[4,128,256]{2,1,0:T(8,128)(2,1)S(1)}, u32[]{:S(2)}, u32[]{:S(2)}) collective-permute-start(bf16[4,128,256]{2,1,0:T(8,128)(2,1)S(1)} %get-tuple-element.71), channel_id=1, source_target_pairs={{0,16},{4,20},{8,24},{12,28},{16,0},{20,4},{24,8},{28,12},{1,17},{... | collective-permute-start | bytes 786440 | tf_op jit(solution)/shard_map/ppermute | solution.py:555
  50.5 14.5 %collective-permute-start.18 = (bf16[4,128,256]{2,1,0:T(8,128)(2,1)S(1)}, bf16[4,128,256]{2,1,0:T(8,128)(2,1)S(1)}, u32[]{:S(2)}, u32[]{:S(2)}) collective-permute-start(bf16[4,128,256]{2,1,0:T(8,128)(2,1)S(1)} %compose_0.1), channel_id=1, source_target_pairs={{0,1},{2,3},{4,5},{6,7},{8,9},{10,11},{12,13},{14,15},{16,17},{18,... | collective-permute-start | bytes 786440 | tf_op jit(solution)/shard_map/ppermute | solution.py:413
  61.8 5.4 %collective-permute-start.10 = (bf16[4,128,256]{2,1,0:T(8,128)(2,1)S(1)}, bf16[4,128,256]{2,1,0:T(8,128)(2,1)S(1)}, u32[]{:S(2)}, u32[]{:S(2)}) collective-permute-start(bf16[4,128,256]{2,1,0:T(8,128)(2,1)S(1)} %compose_1.1), channel_id=1, source_target_pairs={{0,1},{2,3},{4,5},{6,7},{8,9},{10,11},{12,13},{14,15},{16,17},{18,... | collective-permute-start | bytes 786440 | tf_op jit(solution)/shard_map/ppermute | solution.py:413
  63.4 18.5 %collective-permute-start.3 = (bf16[128,1024]{1,0:T(8,128)(2,1)S(1)}, bf16[128,1024]{1,0:T(8,128)(2,1)S(1)}, u32[]{:S(2)}, u32[]{:S(2)}) collective-permute-start(bf16[128,1024]{1,0:T(8,128)(2,1)S(1)} %get-tuple-element.55), channel_id=1, source_target_pairs={{0,4},{4,0},{8,12},{12,8},{16,20},{20,16},{24,28},{28,24},{1,5},{5... | collective-permute-start | bytes 786440 | tf_op jit(solution)/shard_map/ppermute | solution.py:111
  65.0 16.9 %collective-permute-start.4 = (bf16[128,1024]{1,0:T(8,128)(2,1)S(1)}, bf16[128,1024]{1,0:T(8,128)(2,1)S(1)}, u32[]{:S(2)}, u32[]{:S(2)}) collective-permute-start(bf16[128,1024]{1,0:T(8,128)(2,1)S(1)} %get-tuple-element.56), channel_id=1, source_target_pairs={{0,8},{4,12},{8,0},{12,4},{16,24},{20,28},{24,16},{28,20},{1,9},{5... | collective-permute-start | bytes 786440 | tf_op jit(solution)/shard_map/ppermute | solution.py:111
  65.2 2.8 %collective-permute-start.20 = (bf16[4,128,128]{2,1,0:T(8,128)(2,1)S(1)}, bf16[4,128,128]{2,1,0:T(8,128)(2,1)S(1)}, u32[]{:S(2)}, u32[]{:S(2)}) collective-permute-start(bf16[4,128,128]{2,1,0:T(8,128)(2,1)S(1)} %add_convert_fusion), channel_id=1, source_target_pairs={{1,3},{5,7},{9,11},{13,15},{17,19},{21,23},{25,27},{29,31}} | collective-permute-start | bytes 393224 | tf_op jit(solution)/shard_map/ppermute | solution.py:413
  65.8 6.3 %collective-permute-start.19 = (bf16[4,128,128]{2,1,0:T(8,128)(2,1)S(1)}, bf16[4,128,128]{2,1,0:T(8,128)(2,1)S(1)}, u32[]{:S(2)}, u32[]{:S(2)}) collective-permute-start(bf16[4,128,128]{2,1,0:T(8,128)(2,1)S(1)} %add_convert_fusion), channel_id=1, source_target_pairs={{1,2},{5,6},{9,10},{13,14},{17,18},{21,22},{25,26},{29,30}} | collective-permute-start | bytes 393224 | tf_op jit(solution)/shard_map/ppermute | solution.py:413
  67.3 6.7 %collective-permute-start.12 = (bf16[4,128,128]{2,1,0:T(8,128)(2,1)S(1)}, bf16[4,128,128]{2,1,0:T(8,128)(2,1)S(1)}, u32[]{:S(2)}, u32[]{:S(2)}) collective-permute-start(bf16[4,128,128]{2,1,0:T(8,128)(2,1)S(1)} %add_convert_fusion.1), channel_id=1, source_target_pairs={{1,3},{5,7},{9,11},{13,15},{17,19},{21,23},{25,27},{29,31}} | collective-permute-start | bytes 393224 | tf_op jit(solution)/shard_map/ppermute | solution.py:413
  68.0 13.9 %collective-permute-start.5 = (bf16[128,1024]{1,0:T(8,128)(2,1)S(1)}, bf16[128,1024]{1,0:T(8,128)(2,1)S(1)}, u32[]{:S(2)}, u32[]{:S(2)}) collective-permute-start(bf16[128,1024]{1,0:T(8,128)(2,1)S(1)} %get-tuple-element.57), channel_id=1, source_target_pairs={{0,12},{4,8},{8,4},{12,0},{16,28},{20,24},{24,20},{28,16},{1,13},{... | collective-permute-start | bytes 786440 | tf_op jit(solution)/shard_map/ppermute | solution.py:111
  72.1 6.3 %collective-permute-start.11 = (bf16[4,128,128]{2,1,0:T(8,128)(2,1)S(1)}, bf16[4,128,128]{2,1,0:T(8,128)(2,1)S(1)}, u32[]{:S(2)}, u32[]{:S(2)}) collective-permute-start(bf16[4,128,128]{2,1,0:T(8,128)(2,1)S(1)} %add_convert_fusion.1), channel_id=1, source_target_pairs={{1,2},{5,6},{9,10},{13,14},{17,18},{21,22},{25,26},{29,30}} | collective-permute-start | bytes 393224 | tf_op jit(solution)/shard_map/ppermute | solution.py:413
  74.0 12.6 %collective-permute-start.21 = (bf16[4,128,128]{2,1,0:T(8,128)(2,1)S(1)}, bf16[4,128,128]{2,1,0:T(8,128)(2,1)S(1)}, u32[]{:S(2)}, u32[]{:S(2)}) collective-permute-start(bf16[4,128,128]{2,1,0:T(8,128)(2,1)S(1)} %get-tuple-element.88), channel_id=1, source_target_pairs={{0,16},{4,20},{8,24},{12,28},{16,0},{20,4},{24,8},{28,12},{1,17},{... | collective-permute-start | bytes 393224 | tf_op jit(solution)/shard_map/ppermute | solution.py:555
  78.8 16.5 %collective-permute-start.13 = (bf16[4,128,128]{2,1,0:T(8,128)(2,1)S(1)}, bf16[4,128,128]{2,1,0:T(8,128)(2,1)S(1)}, u32[]{:S(2)}, u32[]{:S(2)}) collective-permute-start(bf16[4,128,128]{2,1,0:T(8,128)(2,1)S(1)} %get-tuple-element.73), channel_id=1, source_target_pairs={{0,16},{4,20},{8,24},{12,28},{16,0},{20,4},{24,8},{28,12},{1,17},{... | collective-permute-start | bytes 393224 | tf_op jit(solution)/shard_map/ppermute | solution.py:555
  91.7 9.4 %collective-permute-start.22 = (bf16[64,1024]{1,0:T(8,128)(2,1)S(1)}, bf16[64,1024]{1,0:T(8,128)(2,1)S(1)}, u32[]{:S(2)}, u32[]{:S(2)}) collective-permute-start(bf16[64,1024]{1,0:T(8,128)(2,1)S(1)} %get-tuple-element.90), channel_id=1, source_target_pairs={{0,4},{4,0},{8,12},{12,8},{16,20},{20,16},{24,28},{28,24},{1,5},{5... | collective-permute-start | bytes 393224 | tf_op jit(solution)/shard_map/ppermute | solution.py:111
  91.8 12.2 %collective-permute-start.23 = (bf16[64,1024]{1,0:T(8,128)(2,1)S(1)}, bf16[64,1024]{1,0:T(8,128)(2,1)S(1)}, u32[]{:S(2)}, u32[]{:S(2)}) collective-permute-start(bf16[64,1024]{1,0:T(8,128)(2,1)S(1)} %get-tuple-element.91), channel_id=1, source_target_pairs={{0,8},{4,12},{8,0},{12,4},{16,24},{20,28},{24,16},{28,20},{1,9},{5... | collective-permute-start | bytes 393224 | tf_op jit(solution)/shard_map/ppermute | solution.py:111
  92.1 11.9 %collective-permute-start.24 = (bf16[64,1024]{1,0:T(8,128)(2,1)S(1)}, bf16[64,1024]{1,0:T(8,128)(2,1)S(1)}, u32[]{:S(2)}, u32[]{:S(2)}) collective-permute-start(bf16[64,1024]{1,0:T(8,128)(2,1)S(1)} %get-tuple-element.92), channel_id=1, source_target_pairs={{0,12},{4,8},{8,4},{12,0},{16,28},{20,24},{24,20},{28,16},{1,13},{... | collective-permute-start | bytes 393224 | tf_op jit(solution)/shard_map/ppermute | solution.py:111
  95.3 8.7 %copy-start = (bf16[2,64,4096]{2,1,0:T(8,128)(2,1)S(1)}, bf16[2,64,4096]{2,1,0:T(8,128)(2,1)}, u32[]{:S(2)}) copy-start(bf16[2,64,4096]{2,1,0:T(8,128)(2,1)} %rest_4_.7) | copy-start | bytes 3145732
  95.3 8.7 %copy-start.5 = (f32[4096]{0:T(1024)S(1)}, f32[4096]{0:T(1024)}, u32[]{:S(2)}) copy-start(f32[4096]{0:T(1024)} %param.23) | copy-start | bytes 49156
  100.4 5.0 %collective-permute-start.14 = (bf16[64,1024]{1,0:T(8,128)(2,1)S(1)}, bf16[64,1024]{1,0:T(8,128)(2,1)S(1)}, u32[]{:S(2)}, u32[]{:S(2)}) collective-permute-start(bf16[64,1024]{1,0:T(8,128)(2,1)S(1)} %get-tuple-element.75), channel_id=1, source_target_pairs={{0,4},{4,0},{8,12},{12,8},{16,20},{20,16},{24,28},{28,24},{1,5},{5... | collective-permute-start | bytes 393224 | tf_op jit(solution)/shard_map/ppermute | solution.py:111
  100.6 5.0 %collective-permute-start.15 = (bf16[64,1024]{1,0:T(8,128)(2,1)S(1)}, bf16[64,1024]{1,0:T(8,128)(2,1)S(1)}, u32[]{:S(2)}, u32[]{:S(2)}) collective-permute-start(bf16[64,1024]{1,0:T(8,128)(2,1)S(1)} %get-tuple-element.76), channel_id=1, source_target_pairs={{0,8},{4,12},{8,0},{12,4},{16,24},{20,28},{24,16},{28,20},{1,9},{5... | collective-permute-start | bytes 393224 | tf_op jit(solution)/shard_map/ppermute | solution.py:111
  101.1 7.2 %collective-permute-start.16 = (bf16[64,1024]{1,0:T(8,128)(2,1)S(1)}, bf16[64,1024]{1,0:T(8,128)(2,1)S(1)}, u32[]{:S(2)}, u32[]{:S(2)}) collective-permute-start(bf16[64,1024]{1,0:T(8,128)(2,1)S(1)} %get-tuple-element.77), channel_id=1, source_target_pairs={{0,12},{4,8},{8,4},{12,0},{16,28},{20,24},{24,20},{28,16},{1,13},{... | collective-permute-start | bytes 393224 | tf_op jit(solution)/shard_map/ppermute | solution.py:111

commit v2 on v1

--- a/solution.py
+++ b/solution.py
@@ -16,14 +16,16 @@
 ANY = pl.BlockSpec(memory_space=pl.ANY)
 VMEM = pl.BlockSpec(memory_space=pltpu.VMEM)
 SMEM = pl.BlockSpec(memory_space=pltpu.SMEM)
+PACK_MIB = 48
+SCALE = 0.1
 
 
 def params(mib=48):
     return pltpu.CompilerParams(vmem_limit_bytes=mib * 1024 * 1024)
 
 
-def misc_rows(total_heads):
-    return -(-(total_heads + 2) // 16) * 16
+def misc_rows(heads):
+    return -(-(heads + 2) // 16) * 16
 
 
 def cost(flops, nbytes):
@@ -51,9 +53,17 @@
 
 
 def pack_kv_kernel(sub, batch, heads, key_ref, value_ref, latent_ref, beta_ref, mark_ref, kind_ref, *rest):
-    outs, (extra, sem) = rest[:sub], rest[sub:]
+    outs, (latent, beta, mark, kind, turned, sem, small_sem) = rest[-sub - 7 : -7], rest[-7:]
     lo = lax.rem(lax.axis_index("head"), sub)
     rows, width = key_ref.shape[1], key_ref.shape[2] // sub
+    small = [
+        pltpu.make_async_copy(source, target, small_sem.at[i])
+        for i, (source, target) in enumerate(
+            ((latent_ref.at[batch], latent), (beta_ref.at[batch], beta), (mark_ref, mark), (kind_ref, kind))
+        )
+    ]
+    for c in small:
+        c.start()
     copies = []
     for k in range(sub):
         col = pl.multiple_of((lo ^ k) * width, width)
@@ -64,25 +74,24 @@
                 )
             )
             copies[-1].start()
-    extra[...] = jnp.zeros_like(extra)
+    for c in small:
+        c.wait()
     lanes = width // 128
-    wide = jnp.concatenate(
-        [
-            beta_ref[batch].astype(f32),
-            mark_ref[batch].astype(f32),
-            kind_ref[batch].astype(f32),
-            jnp.zeros((rows, 128 - heads - 2), f32),
-        ],
-        axis=1,
-    )
-    turned = jnp.transpose(jnp.concatenate([wide, jnp.zeros((128 - rows, 128), f32)], axis=0)).astype(bf16)
-    chunks = [latent_ref[batch, 16 * j : 16 * j + 16] for j in range(rows // 16)]
-    chunks += [turned[16 * j : 16 * j + 16] for j in range(misc_rows(heads) // 16)]
-    for c, chunk in enumerate(chunks):
-        extra[16 * (c // lanes) : 16 * (c // lanes) + 16, (c % lanes) * 128 : (c % lanes + 1) * 128] = chunk
+    total = beta.shape[1]
+    misc = misc_rows(heads)
+    wide = jnp.concatenate([beta[...].astype(f32), jnp.zeros((rows, 128 - total), f32)], axis=1)
+    turned[...] = jnp.transpose(jnp.concatenate([wide, jnp.zeros((128 - rows, 128), f32)], axis=0))
+    tokens = jnp.concatenate([mark[batch : batch + 1].astype(f32), kind[batch : batch + 1].astype(f32)], axis=0)
+    tokens = jnp.concatenate([tokens, jnp.zeros((2, 128 - rows), f32)], axis=1)
     for k in range(sub):
-        copies.append(pltpu.make_async_copy(extra, outs[k].at[pl.ds(2 * rows, extra.shape[0])], sem.at[k, 2]))
-        copies[-1].start()
+        own = turned[pl.ds(pl.multiple_of((lo ^ k) * heads, heads), heads), :]
+        values = jnp.concatenate([own, tokens, jnp.zeros((misc - heads - 2, 128), f32)], axis=0).astype(bf16)
+        chunks = [latent[16 * j : 16 * j + 16] for j in range(rows // 16)]
+        chunks += [values[16 * j : 16 * j + 16] for j in range(misc // 16)]
+        chunks += [jnp.zeros((16, 128), bf16)] * (-len(chunks) % lanes)
+        for c, chunk in enumerate(chunks):
+            at = 2 * rows + 16 * (c // lanes)
+            outs[k][at : at + 16, (c % lanes) * 128 : (c % lanes + 1) * 128] = chunk
     for c in copies:
         c.wait()
 
@@ -113,15 +122,19 @@
     return [pieces[0]] + [got[k] for k in range(1, len(pieces))]
 
 
-def state_kernel(sub, outer, blocks, heads, tok, hp, decay_ref, *rest):
+def place(outer, first, share, hp):
+    at = pl.program_id(0) * hp
+    hi = lax.div(lax.axis_index("head"), lax.axis_size("head") // outer)
+    return (hi ^ (first + lax.div(at, share))) * share + lax.rem(at, share)
+
+
+def state_kernel(sub, outer, first, blocks, heads, tok, hp, decay_ref, *rest):
     pieces = rest[:sub]
     up_ref, bias_ref = rest[sub : sub + 2]
-    w_ref, u_ref, shrink_ref, growth_ref, opre_ref, mpre_ref, mask_ref, alive_ref = rest[sub + 2 : sub + 10]
-    parts = rest[sub + 10 : sub + 10 + outer]
-    buf, up, levels, kinds, lasts, betas, gates, spans, sem, part_sem = rest[sub + 10 + outer :]
+    w_ref, u_ref, shrink_ref, growth_ref, opre_ref, mpre_ref, span_ref, mask_ref, alive_ref = rest[-17:-8]
+    buf, up, levels, kinds, lasts, values, gates, sem = rest[-8:]
     me = lax.rem(lax.axis_index("head"), sub)
-    hi = lax.div(lax.axis_index("head"), sub)
-    total_heads = heads * sub
+    start = place(outer, first, heads // outer, hp)
     width = heads * DK
     per = BLOCK // tok
     row = lax.broadcasted_iota(jnp.int32, (BLOCK, BLOCK), 0)
@@ -148,30 +161,29 @@
         for c in copies:
             c.wait()
         lanes = width // 128
-        misc = misc_rows(total_heads)
+        misc = misc_rows(heads)
 
         def chunk(source, c):
             at = 2 * tok + 16 * (c // lanes)
             return buf[source, at : at + 16, (c % lanes) * 128 : (c % lanes + 1) * 128]
 
         for n in range(blocks):
-            tall = []
-            for s in range(n * per, (n + 1) * per):
-                values = [chunk(s, tok // 16 + j).astype(f32) for j in range(misc // 16)]
-                values.append(jnp.zeros((128 - misc, 128), f32))
-                tall.append(jnp.transpose(jnp.concatenate(values, axis=0))[:tok])
-            tall = jnp.concatenate(tall, axis=0)
-            sig = jax.nn.sigmoid(tall)
-            for h in range(heads):
-                mine = jnp.sum(jnp.where(col == me * heads + h, sig, 0.0), axis=1, keepdims=True)
-                betas[h, n] = jnp.broadcast_to(mine, (BLOCK, BLOCK))
-            mark = jnp.broadcast_to(tall[:, total_heads : total_heads + 1], (BLOCK, BLOCK))
-            own = dot(low_b, mark)
-            other = dot(jnp.transpose(mark), up_b)
+            tall = jnp.concatenate(
+                [
+                    jnp.concatenate([chunk(s, tok // 16 + j).astype(f32) for j in range(misc // 16)], axis=0)[:, :tok]
+                    for s in range(n * per, (n + 1) * per)
+                ],
+                axis=1,
+            )
+            values[n] = jax.nn.sigmoid(tall)
+            mark = tall[heads : heads + 1]
+            two = jnp.transpose(jnp.concatenate([tall[heads : heads + 2], jnp.zeros((6, BLOCK), f32)], axis=0))
+            own = dot(low_b, jnp.broadcast_to(two[:, 0:1], (BLOCK, BLOCK)))
+            other = dot(jnp.broadcast_to(mark, (BLOCK, BLOCK)), up_b)
             mask_ref[n] = jnp.where(own == other, low, 0.0)
             alive_ref[n] = (own == 0).astype(f32)
             lasts[n] = (own == other[:, BLOCK - 1 : BLOCK]).astype(f32)
-            kinds[n] = jnp.broadcast_to(tall[:, total_heads + 1 : total_heads + 2], (BLOCK, BLOCK))
+            kinds[n] = jnp.broadcast_to(two[:, 1:2], (BLOCK, BLOCK))
             gates[n] = jnp.concatenate(
                 [chunk(s, j) for s in range(n * per, (n + 1) * per) for j in range(tok // 16)], axis=0
             )
@@ -180,8 +192,12 @@
     lower = (row > col).astype(f32)
     items = [(i, n) for i in range(hp) for n in range(blocks)]
     strict_all, rhs_all, tail_all, carry_all = {}, {}, {}, {}
+    betas = []
+    for n in range(blocks):
+        mine = values[n, pl.ds(start, hp), :]
+        betas.append(jnp.transpose(jnp.concatenate([mine, jnp.zeros((8 - hp % 8, BLOCK), f32)], axis=0)))
     for i in range(hp):
-        h = step * hp + i
+        h = start + i
         at = pl.ds(pl.multiple_of(h * DK, DK), DK)
         bias_at = pl.ds(pl.multiple_of(me * width + h * DK, DK), DK)
         audio, text = bias_ref[0:1, bias_at], bias_ref[1:2, bias_at]
@@ -201,7 +217,7 @@
             last = total[BLOCK - 1 : BLOCK]
             tail = unit * (jnp.exp2(last - total) * lasts[n])
             carry = jnp.exp2(last) * alive_ref[n, BLOCK - 1 : BLOCK]
-            beta = betas[h, n]
+            beta = jnp.broadcast_to(betas[n][:, i : i + 1], (BLOCK, BLOCK))
             growth_ref[i, n] = growth
             shrink_ref[i, n, :, :DK] = shrunk
             shrink_ref[i, n, :, DK:] = shrunk_rest
@@ -251,19 +267,7 @@
             offset[i] = carry_all[i, n] * offset[i] + offs[i, n] - joint[:, :DK]
             move[i] = carry_all[i, n] * move[i] - joint[:, DK:]
     for i in range(hp):
-        spans[step * hp + i] = jnp.concatenate([offset[i], move[i]], axis=1).astype(bf16)
-
-    @pl.when(step == pl.num_programs(0) - 1)
-    def _():
-        share = heads // outer
-        copies = [
-            pltpu.make_async_copy(spans.at[pl.ds((hi ^ j) * share, share)], parts[j], part_sem.at[j])
-            for j in range(outer)
-        ]
-        for c in copies:
-            c.start()
-        for c in copies:
-            c.wait()
+        span_ref[i] = jnp.concatenate([offset[i], move[i]], axis=1).astype(bf16)
 
 
 def joined(later, earlier):
@@ -278,7 +282,7 @@
 
 
 def compose_kernel(outer, share, *rest):
-    parts, out_ref, order = rest[:outer], rest[outer], rest[outer + 1]
+    parts, out_ref, order = rest[:outer], rest[-2], rest[-1]
     ordered(outer, parts, order)
     for h in range(share):
         whole = (order[0, h, :, :DK], order[0, h, :, DK:])
@@ -286,6 +290,16 @@
             whole = joined((order[o, h, :, :DK], order[o, h, :, DK:]), whole)
         out_ref[h, :, :DK] = whole[0]
         out_ref[h, :, DK:] = whole[1]
+
+
+def relay_kernel(share, whole_ref, got_ref, out_ref):
+    for h in range(share):
+        whole = joined(
+            (whole_ref[h, :, :DK], whole_ref[h, :, DK:]), (got_ref[h, :, :DK], got_ref[h, :, DK:])
+        )
+        out_ref[h, :, :DK] = whole[0]
+        if out_ref.shape[2] > DK:
+            out_ref[h, :, DK:] = whole[1]
 
 
 def seed_kernel(outer, share, raw, *rest):
@@ -313,27 +327,18 @@
         outs[j][...] = seeds[hi ^ j]
 
 
-def output_kernel(sub, outer, blocks, heads, tok, batch, hp, *rest):
+def query_kernel(sub, outer, first, blocks, heads, tok, batch, hp, *rest):
     pieces = rest[:sub]
-    w_ref, u_ref, shrink_ref, growth_ref, opre_ref, mpre_ref, mask_ref, alive_ref = rest[sub : sub + 8]
-    seeds = rest[sub + 8 : sub + 8 + outer]
-    outs = rest[sub + 8 + outer : 2 * sub + 8 + outer]
-    buf, obuf, begin, sem, osem, seed_sem = rest[2 * sub + 8 + outer :]
-    step = pl.program_id(0)
+    w_ref, u_ref, shrink_ref, growth_ref, mask_ref, alive_ref = rest[sub : sub + 6]
+    base_ref, rows_ref, buf, sem = rest[-4:]
     lo = lax.rem(lax.axis_index("head"), sub)
-    hi = lax.div(lax.axis_index("head"), sub)
     per = BLOCK // tok
 
-    @pl.when(step == 0)
+    @pl.when(pl.program_id(0) == 0)
     def _():
-        share = heads // outer
         copies = [
             pltpu.make_async_copy(pieces[k].at[pl.ds(batch * tok, tok)], buf.at[lo ^ k], sem.at[k])
             for k in range(sub)
-        ]
-        copies += [
-            pltpu.make_async_copy(seeds[j], begin.at[pl.ds((hi ^ j) * share, share)], seed_sem.at[j])
-            for j in range(outer)
         ]
         for c in copies:
             c.start()
@@ -341,11 +346,8 @@
             c.wait()
 
     items = [(i, n) for i in range(hp) for n in range(blocks)]
-    at = [pl.ds(pl.multiple_of((step * hp + i) * DK, DK), DK) for i in range(hp)]
-    start = [begin[step * hp + i].astype(f32) for i in range(hp)]
-    states = {
-        (i, n): start[i] if n == 0 else opre_ref[i, n - 1] + dot(mpre_ref[i, n - 1], start[i]) for i, n in items
-    }
+    start = place(outer, first, heads // outer, hp)
+    at = [pl.ds(pl.multiple_of((start + i) * DK, DK), DK) for i in range(hp)]
     grown, mix = {}, {}
     for i, n in items:
         query = buf[n * per : (n + 1) * per, :, at[i]].reshape(BLOCK, DK).astype(f32)
@@ -356,24 +358,34 @@
         mix[i, n] = mask_ref[n] * dot(
             jnp.concatenate([gh, gh, gl], axis=1), jnp.concatenate([shrunk, shrunk[:, :DK]], axis=1), NT
         )
-    fresh = {(i, n): u_ref[i, n] - dot(w_ref[i, n], states[i, n]) for i, n in items}
     for i, n in items:
-        fh, fl = split(fresh[i, n])
         mh, ml = split(mix[i, n])
-        live = (grown[i, n] * alive_ref[n]).astype(bf16)
-        core = dot(
-            jnp.concatenate([live, mh, mh, ml], axis=1),
-            jnp.concatenate([states[i, n].astype(bf16), fh, fl, fh], axis=0),
-        )
-        obuf[n * per : (n + 1) * per, :, at[i]] = core.astype(bf16).reshape(per, tok, DK)
-
-    @pl.when(step == pl.num_programs(0) - 1)
-    def _():
-        copies = [pltpu.make_async_copy(obuf.at[lo ^ k], outs[k], osem.at[k]) for k in range(sub)]
-        for c in copies:
-            c.start()
-        for c in copies:
-            c.wait()
+        uh, ul = split(u_ref[i, n])
+        both = dot(mh, jnp.concatenate([uh, w_ref[i, n]], axis=1))
+        rest_part = dot(jnp.concatenate([mh, ml], axis=1), jnp.concatenate([ul, uh], axis=0))
+        base_ref[i, n] = both[:, :DK] + rest_part
+        rows_ref[i, n] = (grown[i, n] * alive_ref[n] - both[:, DK:]).astype(bf16)
+
+
+def output_kernel(sub, outer, sets, blocks, heads, tok, *rest):
+    seeds, rest = rest[:outer], rest[outer:]
+    outs, obuf = rest[-sub - 1 : -1], rest[-1]
+    lo = lax.rem(lax.axis_index("head"), sub)
+    hi = lax.div(lax.axis_index("head"), sub)
+    share = heads // outer
+    per = BLOCK // tok
+    for part, (first, shares) in enumerate(sets):
+        base_ref, rows_ref, opre_ref, mpre_ref = rest[4 * part : 4 * part + 4]
+        for r in range(shares * share):
+            j, i = first + r // share, r % share
+            at = pl.ds(pl.multiple_of(((hi ^ j) * share + i) * DK, DK), DK)
+            seed = seeds[j][i]
+            for n in range(blocks):
+                state = seed if n == 0 else opre_ref[r, n - 1] + dot(mpre_ref[r, n - 1], seed)
+                core = base_ref[r, n] + dot(rows_ref[r, n], state)
+                obuf[n * per : (n + 1) * per, :, at] = core.astype(bf16).reshape(per, tok, DK)
+    for k in range(sub):
+        outs[k][...] = obuf[lo ^ k]
 
 
 def finish_kernel(sub, heads, *rest):
@@ -402,7 +414,7 @@
     size = 1
     while size < count:
         final = 2 * size >= count
-        payload = whole[..., :DK] if final else whole
+        payload = whole[..., :DK] if final and size == 1 else whole
         got = None
         for t in range(size):
             pairs = [
@@ -430,14 +442,17 @@
                 ],
                 axis=2,
             )
-        moved = product(whole[..., DK:], got)
-        whole = jnp.concatenate(
-            [
-                (whole[..., :DK].astype(f32) + moved[..., :DK]).astype(bf16),
-                jnp.where(right, moved[..., DK:].astype(bf16), whole[..., DK:]),
-            ],
-            axis=2,
-        )
+        share = whole.shape[0]
+        last = 4 * size >= count
+        whole = pl.pallas_call(
+            functools.partial(relay_kernel, share),
+            out_shape=jax.ShapeDtypeStruct((share, DK, DK if last else 2 * DK), bf16),
+            in_specs=[VMEM] * 2,
+            out_specs=VMEM,
+            compiler_params=params(),
+            cost_estimate=cost(0, 0),
+            name=f"relay_{size}",
+        )(whole, got)
         size *= 2
     if early is None:
         early = jnp.concatenate([jnp.zeros_like(unit_mat), unit_mat], axis=2)
@@ -468,25 +483,34 @@
     width = heads * DK
     blocks = tok * sub // BLOCK
     sds = jax.ShapeDtypeStruct
-    extra_rows = 16 * -(-(tok // 16 + misc_rows(total_heads) // 16) // (width // 128))
+    extra_rows = 16 * -(-(tok // 16 + misc_rows(heads) // 16) // (width // 128))
     piece_rows = 2 * tok + extra_rows
-    mark3, kind3 = boundary[..., None], modality[..., None]
-
-    def pack_kv(batch):
+
+    def pack_kv(batch, *after):
         return pl.pallas_call(
-            functools.partial(pack_kv_kernel, sub, batch, total_heads),
+            functools.partial(pack_kv_kernel, sub, batch, heads),
             out_shape=[sds((piece_rows, width), bf16)] * sub,
-            in_specs=[ANY, ANY] + [VMEM] * 4,
-            out_specs=[ANY] * sub,
-            scratch_shapes=[pltpu.VMEM((extra_rows, width), bf16), pltpu.SemaphoreType.DMA((sub, 3))],
-            compiler_params=params(),
-            cost_estimate=cost(0, 4 * sub * piece_rows * width),
+            in_specs=[ANY] * (6 + len(after)),
+            out_specs=[VMEM] * sub,
+            scratch_shapes=[
+                pltpu.VMEM(gate_latent.shape[1:], bf16),
+                pltpu.VMEM(beta_raw.shape[1:], bf16),
+                pltpu.VMEM(boundary.shape, jnp.int32),
+                pltpu.VMEM(modality.shape, jnp.int32),
+                pltpu.VMEM((128, 128), f32),
+                pltpu.SemaphoreType.DMA((sub, 3)),
+                pltpu.SemaphoreType.DMA((4,)),
+            ],
+            compiler_params=params(PACK_MIB),
+            cost_estimate=cost(0, 0),
             name=f"pack_kv_{batch}",
-        )(key_rows, value_rows, gate_latent, beta_raw, mark3, kind3)
-
-    kv = [exchange(pack_kv(b)) for b in range(batches)]
-    hp = max(1, 8 // blocks)
-    while heads % hp:
+        )(key_rows, value_rows, gate_latent, beta_raw, boundary, modality, *after)
+
+    kv = []
+    for b in range(batches):
+        kv.append(exchange(pack_kv(b, *([] if b == 0 else [kv[-1][-1]]))))
+    hp = min(share, max(1, 8 // blocks))
+    while share % hp:
         hp -= 1
     before_rows = max(1, blocks - 1)
 
@@ -497,75 +521,108 @@
     wide_head = by_head(blocks, DK, 2 * DK)
     pre_head = by_head(before_rows, DK, DK)
     whole = pl.BlockSpec((blocks, BLOCK, BLOCK), lambda i: (0, 0, 0))
-    square = (heads, blocks, DK, DK)
     levels = BLOCK.bit_length() - 1
-    local, seeds = [], []
-    q_here = None
-    for b in range(batches):
-        made = pl.pallas_call(
-            functools.partial(state_kernel, sub, outer, blocks, heads, tok, hp),
-            grid=(heads // hp,),
-            out_shape=[
-                sds(square, bf16),
-                sds(square, f32),
-                sds((heads, blocks, DK, 2 * DK), bf16),
-                sds(square, f32),
-                sds((heads, before_rows, DK, DK), f32),
-                sds((heads, before_rows, DK, DK), bf16),
-                sds((blocks, BLOCK, BLOCK), f32),
-                sds((blocks, BLOCK, BLOCK), f32),
-            ]
-            + [sds((share, DK, 2 * DK), bf16)] * outer,
-            in_specs=[SMEM] + [ANY] * sub + [ANY, VMEM],
-            out_specs=[per_head, per_head, wide_head, per_head, pre_head, pre_head, whole, whole] + [ANY] * outer,
+    local_dims = [
+        ((blocks, DK, DK), bf16),
+        ((blocks, DK, DK), f32),
+        ((blocks, DK, 2 * DK), bf16),
+        ((blocks, DK, DK), f32),
+        ((before_rows, DK, DK), f32),
+        ((before_rows, DK, DK), bf16),
+        ((DK, 2 * DK), bf16),
+    ]
+    count = lax.axis_size("head")
+
+    def state_maps(b, first, shares, *after):
+        here = shares * share
+        return pl.pallas_call(
+            functools.partial(state_kernel, sub, outer, first, blocks, heads, tok, hp),
+            grid=(here // hp,),
+            out_shape=[sds((here, *dims), kind) for dims, kind in local_dims] + [sds((blocks, BLOCK, BLOCK), f32)] * 2,
+            in_specs=[SMEM] + [ANY] * sub + [ANY, VMEM] + [ANY] * len(after),
+            out_specs=[by_head(*dims) for dims, _ in local_dims] + [whole, whole],
             scratch_shapes=[
                 pltpu.VMEM((sub, piece_rows, width), bf16),
                 pltpu.VMEM((DK, width), bf16),
                 pltpu.VMEM((levels, BLOCK, BLOCK), bf16),
                 pltpu.VMEM((blocks, BLOCK, BLOCK), f32),
                 pltpu.VMEM((blocks, BLOCK, BLOCK), f32),
-                pltpu.VMEM((heads, blocks, BLOCK, BLOCK), f32),
+                pltpu.VMEM((blocks, misc_rows(heads), BLOCK), f32),
                 pltpu.VMEM((blocks, BLOCK, BLOCK), bf16),
-                pltpu.VMEM((heads, DK, 2 * DK), bf16),
                 pltpu.SemaphoreType.DMA((sub + 1,)),
-                pltpu.SemaphoreType.DMA((outer,)),
             ],
             compiler_params=params(),
-            cost_estimate=cost(heads * blocks * 24 * 2 * 128**3 * 4, 8 * 2**20),
-            name=f"state_maps_{b}",
-        )(decay_log, *kv[b], gate_up, dt_bias)
-        local.append(made[:8])
+            cost_estimate=cost(SCALE * here * blocks * 2e8, 0),
+            name=f"state_maps_{b}_{first}",
+        )(decay_log, *kv[b], gate_up, dt_bias, *after)
+
+    def swap(parts):
+        return [parts[0]] + [
+            lax.ppermute(parts[j], "head", [(i, i ^ (j * sub)) for i in range(count)]) for j in range(1, outer)
+        ]
+
+    sets = ([(1, outer - 1)] if outer > 1 else []) + [(0, 1)]
+    local, split_maps = [], []
+    q_here = None
+    for b in range(batches):
+        made = []
+        for first, shares in sets:
+            after = [kv[b + 1][0]] if first == sets[0][0] and b + 1 < batches else []
+            made.append(state_maps(b, first, shares, *after))
+        local.append(made)
+        sent = []
+        if outer > 1:
+            spans = made[0][6]
+            sent = [spans] if outer == 2 else [spans[j * share : (j + 1) * share] for j in range(outer - 1)]
+        split_maps.append(swap([made[-1][6]] + sent))
         if q_here is None:
             q_here = exchange(
                 pl.pallas_call(
                     functools.partial(pack_q_kernel, sub, batches),
                     out_shape=[sds((batches * tok, width), bf16)] * sub,
                     in_specs=[ANY, ANY],
-                    out_specs=[ANY] * sub,
+                    out_specs=[VMEM] * sub,
                     scratch_shapes=[pltpu.SemaphoreType.DMA((sub, batches))],
                     compiler_params=params(),
-                    cost_estimate=cost(0, 4 * sub * batches * tok * width),
+                    cost_estimate=cost(0, 0),
                     name="pack_q",
-                )(query_rows, made[-1])
+                )(query_rows, kv[-1][-1])
             )
-        count = lax.axis_size("head")
-
-        def swap(parts):
-            return [parts[0]] + [
-                lax.ppermute(parts[j], "head", [(i, i ^ (j * sub)) for i in range(count)]) for j in range(1, outer)
-            ]
-
-        parts = swap(made[8:])
+    queries = []
+    for b in range(batches):
+        made = []
+        for (first, shares), here in zip(sets, local[b]):
+            made.append(
+                pl.pallas_call(
+                    functools.partial(query_kernel, sub, outer, first, blocks, heads, tok, b, hp),
+                    grid=(shares * share // hp,),
+                    out_shape=[
+                        sds((shares * share, blocks, DK, DK), f32),
+                        sds((shares * share, blocks, DK, DK), bf16),
+                    ],
+                    in_specs=[ANY] * sub + [per_head, per_head, wide_head, per_head] + [whole] * 2,
+                    out_specs=[per_head] * 2,
+                    scratch_shapes=[pltpu.VMEM((sub, tok, width), bf16), pltpu.SemaphoreType.DMA((sub,))],
+                    compiler_params=params(),
+                    cost_estimate=cost(SCALE * shares * share * blocks * 1e8, 0),
+                    name=f"query_parts_{b}_{first}",
+                )(*q_here, *here[:4], *here[7:9])
+            )
+        queries.append(made)
+    back = []
+    for b in range(batches):
+        parts = split_maps[b]
+        after = [made[1] for made in queries[-1]] if b == batches - 1 else []
         total = pl.pallas_call(
             functools.partial(compose_kernel, outer, share),
             out_shape=sds((share, DK, 2 * DK), bf16),
-            in_specs=[VMEM] * outer,
+            in_specs=[VMEM] * outer + [ANY] * len(after),
             out_specs=VMEM,
             scratch_shapes=[pltpu.VMEM((outer, share, DK, 2 * DK), bf16)],
             compiler_params=params(),
-            cost_estimate=cost(share * outer * 4 * 128**3, 2**20),
+            cost_estimate=cost(0, 0),
             name=f"compose_{b}",
-        )(*parts)
+        )(*parts, *after)
         early, incoming, raw = before(total)
         mine = pl.pallas_call(
             functools.partial(seed_kernel, outer, share, raw),
@@ -577,33 +634,22 @@
                 pltpu.VMEM((outer, share, DK, DK), bf16),
             ],
             compiler_params=params(),
-            cost_estimate=cost(share * outer * 4 * 128**3, 2**20),
+            cost_estimate=cost(0, 0),
             name=f"seeds_{b}",
         )(*parts, early, incoming)
-        seeds.append(swap(mine))
-    back = []
-    for b in range(batches):
+        operands = []
+        for made, here in zip(queries[b], local[b]):
+            operands += [*made, *here[4:6]]
         outs = pl.pallas_call(
-            functools.partial(output_kernel, sub, outer, blocks, heads, tok, b, hp),
-            grid=(heads // hp,),
+            functools.partial(output_kernel, sub, outer, sets, blocks, heads, tok),
             out_shape=[sds((tok, width), bf16)] * sub,
-            in_specs=[ANY] * sub
-            + [per_head, per_head, wide_head, per_head, pre_head, pre_head]
-            + [whole] * 2
-            + [ANY] * outer,
-            out_specs=[ANY] * sub,
-            scratch_shapes=[
-                pltpu.VMEM((sub, tok, width), bf16),
-                pltpu.VMEM((sub, tok, width), bf16),
-                pltpu.VMEM((heads, DK, DK), bf16),
-                pltpu.SemaphoreType.DMA((sub,)),
-                pltpu.SemaphoreType.DMA((sub,)),
-                pltpu.SemaphoreType.DMA((outer,)),
-            ],
+            in_specs=[VMEM] * (len(operands) + outer),
+            out_specs=[VMEM] * sub,
+            scratch_shapes=[pltpu.VMEM((sub, tok, width), bf16)],
             compiler_params=params(),
-            cost_estimate=cost(heads * blocks * 10 * 2 * 128**3 * 4, 8 * 2**20),
+            cost_estimate=cost(SCALE * heads * blocks * 2e7, 0),
             name=f"span_outputs_{b}",
-        )(*q_here, *local[b], *seeds[b])
+        )(*swap(mine), *operands)
         back.append(exchange(outs))
 
     mixed = None
@@ -619,7 +665,7 @@
             out_specs=rows,
             input_output_aliases={} if b == 0 else {sub + 2: 0},
             compiler_params=params(),
-            cost_estimate=cost(20 * tok * columns, 8 * tok * columns),
+            cost_estimate=cost(0, 0),
             name=f"finish_{b}",
         )(*back[b], out_gate, norm_gain[None, :], *([] if b == 0 else [mixed]))
     return mixed

time: 110 us -> 96.1 us (0.87)
  waiting for transfers between devices: 28.9 us -> 17.6 us
  Pallas kernels: 38.6 us -> 35.8 us
  local copies, waits for them, and re-layouts: 5.49 us -> 3.97 us
    ppermute x4, waiting for transfers between devices: 14.4 us -> 0.01 us  [swap(): lax.ppermute(parts[j], 'head', [(i, i ^ j * sub) for i in range(count)])]
    ppermute x15, starting transfers between devices: 20 us -> 24.4 us  [exchange(): lax.ppermute(pieces[k], 'head', [(i, i ^ k) for i in range(count)])]
    ppermute x15, waiting for transfers between devices: 11.1 us -> 14.8 us  [exchange(): lax.ppermute(pieces[k], 'head', [(i, i ^ k) for i in range(count)])]
    ppermute x4, starting transfers between devices: 9.23 us -> 6.03 us  [swap(): lax.ppermute(parts[j], 'head', [(i, i ^ j * sub) for i in range(count)])]
    pallas_call x6 -> x14, Pallas kernels: 34.6 us -> 31.8 us  [the longest x4 21.4 us: state_maps(): pl.pallas_call(functools.partial(state_kernel, sub, outer, first, blocks,...]
    unnamed x21 -> x23, local copies, waits for them, and re-layouts: 5.29 us -> 3.97 us
  transfers between devices with their start and end apart: 25 -> 25, of which waited for: 9 -> 8; matrix products, arithmetic and copies ran while one was open for 0% -> 0% of each run, Pallas kernels for 34% -> 36%
where the time goes in v2:
time: 96.1 us; the launch traced here: 94.7 us
  starting transfers between devices  36.9 us (38%)
  Pallas kernels  35.8 us (37%)
  waiting for transfers between devices  17.6 us (18%)
  local copies, waits for them, and re-layouts  3.97 us (4%)
    ppermute x15, starting transfers between devices, exchange(): lax.ppermute(pieces[k], 'head', [(i, i ^ k) for i in range(count)])  24.4 us
    pallas_call x4, Pallas kernels, state_maps(): pl.pallas_call(functools.partial(state_kernel, sub, outer, first, blocks,...  21.4 us
    ppermute x15, waiting for transfers between devices, exchange(): lax.ppermute(pieces[k], 'head', [(i, i ^ k) for i in range(count)])  14.8 us
    ppermute x6, starting transfers between devices, before(): part = lax.ppermute(payload, 'seq', pairs)  6.53 us
    pallas_call x4, Pallas kernels, per_device(): pl.pallas_call(functools.partial(query_kernel, sub, outer, first, blocks,...  6.2 us
    ppermute x4, starting transfers between devices, swap(): lax.ppermute(parts[j], 'head', [(i, i ^ j * sub) for i in range(count)])  6.03 us
    unnamed x23, local copies, waits for them, and re-layouts  3.97 us
    pallas_call x2, Pallas kernels, per_device(): pl.pallas_call(functools.partial(output_kernel, sub, outer, sets, blocks,...  2.82 us
  transfers between devices with their start and end apart: 25, of which 8 were waited for; matrix products, arithmetic and copies ran while one was open for 0% of the time, Pallas kernels for 36%

profile of v2, /device:TPU:2, one launch (start us, length us, event | category | flops | bytes accessed | tf_op | source)
XLA Modules:
  0.0 94.7 jit_solution(2337395400717886743)
XLA Ops:
  0.0 0.8 copy.15.beta_ref
  0.9 1.2 %copy-done.2 = bf16[2,64,4096]{2,1,0:T(8,128)(2,1)S(1)} copy-done((bf16[2,64,4096]{2,1,0:T(8,128)(2,1)S(1)}, bf16[2,64,4096]{2,1,0:T(8,128)(2,1)}, u32[]{:S(2)}) %copy-start.2) | copy-done | bytes 1048600
  2.1 1.2 %copy-done.3 = bf16[2,64,4096]{2,1,0:T(8,128)(2,1)S(1)} copy-done((bf16[2,64,4096]{2,1,0:T(8,128)(2,1)S(1)}, bf16[2,64,4096]{2,1,0:T(8,128)(2,1)}, u32[]{:S(2)}) %copy-start.3) | copy-done | bytes 1048600
  3.3 0.5 pack_kv_0.1
  3.8 2.6 %collective-permute-start = (bf16[144,1024]{1,0:T(8,128)(2,1)S(1)}, bf16[144,1024]{1,0:T(8,128)(2,1)S(1)}, u32[]{:S(2)}, u32[]{:S(2)}) collective-permute-start(bf16[144,1024]{1,0:T(8,128)(2,1)S(1)} %get-tuple-element.73), channel_id=1, source_target_pairs={{0,12},{4,8},{8,4},{12,0},{16,28},{20,24},{24,20},{28,16},{1,13},{... | collective-permute-start | bytes 884744 | tf_op jit(solution)/shard_map/ppermute | solution.py:120
  6.4 0.5 collective-permute-start.15
  6.9 0.4 collective-permute-start.16
  7.4 7.3 %collective-permute-done.rest_0_.rest_3_ = bf16[144,1024]{1,0:T(8,128)(2,1)S(1)} collective-permute-done((bf16[144,1024]{1,0:T(8,128)(2,1)S(1)}, bf16[144,1024]{1,0:T(8,128)(2,1)S(1)}, u32[]{:S(2)}, u32[]{:S(2)}) %collective-permute-start) | collective-permute-done | bytes 294944 | tf_op jit(solution)/shard_map/ppermute | solution.py:120
  14.7 0.5 pack_kv_1.1
  15.2 2.6 %collective-permute-start.3 = (bf16[144,1024]{1,0:T(8,128)(2,1)S(1)}, bf16[144,1024]{1,0:T(8,128)(2,1)S(1)}, u32[]{:S(2)}, u32[]{:S(2)}) collective-permute-start(bf16[144,1024]{1,0:T(8,128)(2,1)S(1)} %get-tuple-element.77), channel_id=1, source_target_pairs={{0,12},{4,8},{8,4},{12,0},{16,28},{20,24},{24,20},{28,16},{1,13},{... | collective-permute-start | bytes 884744 | tf_op jit(solution)/shard_map/ppermute | solution.py:120
  17.8 0.5 collective-permute-start.1
  18.3 0.4 collective-permute-start.2
  18.8 2.3 %collective-permute-done.15.rest_1_ = bf16[144,1024]{1,0:T(8,128)(2,1)S(1)} collective-permute-done((bf16[144,1024]{1,0:T(8,128)(2,1)S(1)}, bf16[144,1024]{1,0:T(8,128)(2,1)S(1)}, u32[]{:S(2)}, u32[]{:S(2)}) %collective-permute-start.15) | collective-permute-done | bytes 294944 | tf_op jit(solution)/shard_map/ppermute | solution.py:120
  21.1 0.6 copy-done.8
  21.8 5.3 %state_maps_0_1.1 = (bf16[4,2,128,128]{3,2,1,0:T(8,128)(2,1)S(1)}, f32[4,2,128,128]{3,2,1,0:T(8,128)S(1)}, bf16[4,2,128,256]{3,2,1,0:T(8,128)(2,1)S(1)}, f32[4,2...) custom-call(f32[32]{0:T(128)S(1)} %copy-done.8, ...), custom_call_target="tpu_custom_call" | custom-call | flops 160000000 | tf_op jit(solution)/shard_map/state_maps_0_1/pallas_call | solution.py:538
  27.1 2.6 %collective-permute-start.17 = (bf16[4,128,256]{2,1,0:T(8,128)(2,1)S(1)}, bf16[4,128,256]{2,1,0:T(8,128)(2,1)S(1)}, u32[]{:S(2)}, u32[]{:S(2)}) collective-permute-start(bf16[4,128,256]{2,1,0:T(8,128)(2,1)S(1)} %get-tuple-element.114), channel_id=1, source_target_pairs={{0,16},{4,20},{8,24},{12,28},{16,0},{20,4},{24,8},{28,12},{1,17},{... | collective-permute-start | bytes 786440 | tf_op jit(solution)/shard_map/ppermute | solution.py:561
  30.0 1.6 %collective-permute-start.5 = (bf16[128,1024]{1,0:T(8,128)(2,1)S(1)}, bf16[128,1024]{1,0:T(8,128)(2,1)S(1)}, u32[]{:S(2)}, u32[]{:S(2)}) collective-permute-start(bf16[128,1024]{1,0:T(8,128)(2,1)S(1)} %get-tuple-element.81), channel_id=1, source_target_pairs={{0,4},{4,0},{8,12},{12,8},{16,20},{20,16},{24,28},{28,24},{1,5},{5... | collective-permute-start | bytes 786440 | tf_op jit(solution)/shard_map/ppermute | solution.py:120
  31.6 5.7 %collective-permute-start.6 = (bf16[128,1024]{1,0:T(8,128)(2,1)S(1)}, bf16[128,1024]{1,0:T(8,128)(2,1)S(1)}, u32[]{:S(2)}, u32[]{:S(2)}) collective-permute-start(bf16[128,1024]{1,0:T(8,128)(2,1)S(1)} %get-tuple-element.82), channel_id=1, source_target_pairs={{0,8},{4,12},{8,0},{12,4},{16,24},{20,28},{24,16},{28,20},{1,9},{5... | collective-permute-start | bytes 786440 | tf_op jit(solution)/shard_map/ppermute | solution.py:120
  37.3 0.8 collective-permute-done.2.rest_2_
  38.1 5.3 %state_maps_1_1.1 = (bf16[4,2,128,128]{3,2,1,0:T(8,128)(2,1)S(1)}, f32[4,2,128,128]{3,2,1,0:T(8,128)S(1)}, bf16[4,2,128,256]{3,2,1,0:T(8,128)(2,1)S(1)}, f32[4,2...) custom-call(f32[32]{0:T(128)S(1)} %copy-done.8, ...), custom_call_target="tpu_custom_call" | custom-call | flops 160000000 | tf_op jit(solution)/shard_map/state_maps_1_1/pallas_call | solution.py:538
  43.5 5.5 %state_maps_0_0.1 = (bf16[4,2,128,128]{3,2,1,0:T(8,128)(2,1)S(1)}, f32[4,2,128,128]{3,2,1,0:T(8,128)S(1)}, bf16[4,2,128,256]{3,2,1,0:T(8,128)(2,1)S(1)}, f32[4,2...) custom-call(f32[32]{0:T(128)S(1)} %copy-done.8, ...), custom_call_target="tpu_custom_call" | custom-call | flops 160000000 | tf_op jit(solution)/shard_map/state_maps_0_0/pallas_call | solution.py:538
  49.3 1.3 %collective-permute-start.18 = (bf16[4,128,256]{2,1,0:T(8,128)(2,1)S(1)}, bf16[4,128,256]{2,1,0:T(8,128)(2,1)S(1)}, u32[]{:S(2)}, u32[]{:S(2)}) collective-permute-start(bf16[4,128,256]{2,1,0:T(8,128)(2,1)S(1)} %compose_0.1.whole_ref), channel_id=1, source_target_pairs={{0,1},{2,3},{4,5},{6,7},{8,9},{10,11},{12,13},{14,15},{16,17},{18,... | collective-permute-start | bytes 786440 | tf_op jit(solution)/shard_map/ppermute | solution.py:425
  50.6 5.3 %state_maps_1_0.1 = (bf16[4,2,128,128]{3,2,1,0:T(8,128)(2,1)S(1)}, f32[4,2,128,128]{3,2,1,0:T(8,128)S(1)}, bf16[4,2,128,256]{3,2,1,0:T(8,128)(2,1)S(1)}, f32[4,2...) custom-call(f32[32]{0:T(128)S(1)} %copy-done.8, ...), custom_call_target="tpu_custom_call" | custom-call | flops 160000000 | tf_op jit(solution)/shard_map/state_maps_1_0/pallas_call | solution.py:538
  55.9 1.6 %query_parts_1_1.1 = (f32[4,2,128,128]{3,2,1,0:T(8,128)S(1)}, bf16[4,2,128,128]{3,2,1,0:T(8,128)(2,1)S(1)}) custom-call(bf16[128,1024]{1,0:T(8,128)(2,1)S(1)} %get-tuple-element.80.rest_0_, bf16[128,1024]{1,0:T(8,128)(2,1)S(1)} %collective-permute-done.5.rest_1_, bf16[128,1024]{1,0:T(8,128)(2,1)S(1)} %collective-permute-done.6.rest_2_, ...), custom_call_target="tpu_custom_call" | custom-call | flops 80000000 | tf_op jit(solution)/shard_map/query_parts_1_1/pallas_call | solution.py:596
  57.5 1.6 %query_parts_1_0.1 = (f32[4,2,128,128]{3,2,1,0:T(8,128)S(1)}, bf16[4,2,128,128]{3,2,1,0:T(8,128)(2,1)S(1)}) custom-call(bf16[128,1024]{1,0:T(8,128)(2,1)S(1)} %get-tuple-element.80.rest_0_, bf16[128,1024]{1,0:T(8,128)(2,1)S(1)} %collective-permute-done.5.rest_1_, bf16[128,1024]{1,0:T(8,128)(2,1)S(1)} %collective-permute-done.6.rest_2_, ...), custom_call_target="tpu_custom_call" | custom-call | flops 80000000 | tf_op jit(solution)/shard_map/query_parts_1_0/pallas_call | solution.py:596
  59.3 1.3 %collective-permute-start.8 = (bf16[4,128,256]{2,1,0:T(8,128)(2,1)S(1)}, bf16[4,128,256]{2,1,0:T(8,128)(2,1)S(1)}, u32[]{:S(2)}, u32[]{:S(2)}) collective-permute-start(bf16[4,128,256]{2,1,0:T(8,128)(2,1)S(1)} %compose_1.1.whole_ref), channel_id=1, source_target_pairs={{0,1},{2,3},{4,5},{6,7},{8,9},{10,11},{12,13},{14,15},{16,17},{18,... | collective-permute-start | bytes 786440 | tf_op jit(solution)/shard_map/ppermute | solution.py:425
  60.9 0.7 collective-permute-start.20
  61.6 1.3 %collective-permute-start.19 = (bf16[4,128,128]{2,1,0:T(8,128)(2,1)S(1)}, bf16[4,128,128]{2,1,0:T(8,128)(2,1)S(1)}, u32[]{:S(2)}, u32[]{:S(2)}) collective-permute-start(bf16[4,128,128]{2,1,0:T(8,128)(2,1)S(1)} %relay_1.3), channel_id=1, source_target_pairs={{1,2},{5,6},{9,10},{13,14},{17,18},{21,22},{25,26},{29,30}} | collective-permute-start | bytes 393224 | tf_op jit(solution)/shard_map/ppermute | solution.py:425
  63.1 0.7 collective-permute-start.10
  63.8 1.3 %collective-permute-start.9 = (bf16[4,128,128]{2,1,0:T(8,128)(2,1)S(1)}, bf16[4,128,128]{2,1,0:T(8,128)(2,1)S(1)}, u32[]{:S(2)}, u32[]{:S(2)}) collective-permute-start(bf16[4,128,128]{2,1,0:T(8,128)(2,1)S(1)} %relay_1.2), channel_id=1, source_target_pairs={{1,2},{5,6},{9,10},{13,14},{17,18},{21,22},{25,26},{29,30}} | collective-permute-start | bytes 393224 | tf_op jit(solution)/shard_map/ppermute | solution.py:425
  65.1 2.8 %collective-permute-done.19 = bf16[4,128,128]{2,1,0:T(8,128)(2,1)S(1)} collective-permute-done((bf16[4,128,128]{2,1,0:T(8,128)(2,1)S(1)}, bf16[4,128,128]{2,1,0:T(8,128)(2,1)S(1)}, u32[]{:S(2)}, u32[]{:S(2)}) %collective-permute-start.19) | collective-permute-done | bytes 131104 | tf_op jit(solution)/shard_map/ppermute | solution.py:425
  67.9 0.4 seeds_0.1
  68.3 3.0 %collective-permute-start.21 = (bf16[4,128,128]{2,1,0:T(8,128)(2,1)S(1)}, bf16[4,128,128]{2,1,0:T(8,128)(2,1)S(1)}, u32[]{:S(2)}, u32[]{:S(2)}) collective-permute-start(bf16[4,128,128]{2,1,0:T(8,128)(2,1)S(1)} %get-tuple-element.116), channel_id=1, source_target_pairs={{0,16},{4,20},{8,24},{12,28},{16,0},{20,4},{24,8},{28,12},{1,17},{... | collective-permute-start | bytes 393224 | tf_op jit(solution)/shard_map/ppermute | solution.py:561
  71.2 1.5 %query_parts_0_1.1 = (f32[4,2,128,128]{3,2,1,0:T(8,128)S(1)}, bf16[4,2,128,128]{3,2,1,0:T(8,128)(2,1)S(1)}) custom-call(bf16[128,1024]{1,0:T(8,128)(2,1)S(1)} %get-tuple-element.80.rest_0_, bf16[128,1024]{1,0:T(8,128)(2,1)S(1)} %collective-permute-done.5.rest_1_, bf16[128,1024]{1,0:T(8,128)(2,1)S(1)} %collective-permute-done.6.rest_2_, ...), custom_call_target="tpu_custom_call" | custom-call | flops 80000000 | tf_op jit(solution)/shard_map/query_parts_0_1/pallas_call | solution.py:596
  72.7 1.6 %query_parts_0_0.1 = (f32[4,2,128,128]{3,2,1,0:T(8,128)S(1)}, bf16[4,2,128,128]{3,2,1,0:T(8,128)(2,1)S(1)}) custom-call(bf16[128,1024]{1,0:T(8,128)(2,1)S(1)} %get-tuple-element.80.rest_0_, bf16[128,1024]{1,0:T(8,128)(2,1)S(1)} %collective-permute-done.5.rest_1_, bf16[128,1024]{1,0:T(8,128)(2,1)S(1)} %collective-permute-done.6.rest_2_, ...), custom_call_target="tpu_custom_call" | custom-call | flops 80000000 | tf_op jit(solution)/shard_map/query_parts_0_0/pallas_call | solution.py:596
  74.4 0.4 seeds_1.1
  74.8 0.3 collective-permute-start.11
  75.1 1.4 %span_outputs_0.1 = (bf16[64,1024]{1,0:T(8,128)(2,1)S(1)}, bf16[64,1024]{1,0:T(8,128)(2,1)S(1)}, bf16[64,1024]{1,0:T(8,128)(2,1)S(1)}, bf16[64,1024]{1,0:T(8,128)(2,1)S(1)}) custom-call(bf16[4,128,128]{2,1,0:T(8,128)(2,1)S(1)} %get-tuple-element.115.rest_0_, bf16[4,128,128]{2,1,0:T(8,128)(2,1)S(1)} %collective-permute-done.21.rest_1_, ...), custom_call_target="tpu_custom_call" | custom-call | flops 32000000 | tf_op jit(solution)/shard_map/span_outputs_0/pallas_call | solution.py:643
  76.5 0.8 collective-permute-start.22
  77.3 5.4 %collective-permute-start.23 = (bf16[64,1024]{1,0:T(8,128)(2,1)S(1)}, bf16[64,1024]{1,0:T(8,128)(2,1)S(1)}, u32[]{:S(2)}, u32[]{:S(2)}) collective-permute-start(bf16[64,1024]{1,0:T(8,128)(2,1)S(1)} %get-tuple-element.139), channel_id=1, source_target_pairs={{0,8},{4,12},{8,0},{12,4},{16,24},{20,28},{24,16},{28,20},{1,9},{5... | collective-permute-start | bytes 393224 | tf_op jit(solution)/shard_map/ppermute | solution.py:120
  82.7 1.4 %span_outputs_1.1 = (bf16[64,1024]{1,0:T(8,128)(2,1)S(1)}, bf16[64,1024]{1,0:T(8,128)(2,1)S(1)}, bf16[64,1024]{1,0:T(8,128)(2,1)S(1)}, bf16[64,1024]{1,0:T(8,128)(2,1)S(1)}) custom-call(bf16[4,128,128]{2,1,0:T(8,128)(2,1)S(1)} %get-tuple-element.98.rest_0_, bf16[4,128,128]{2,1,0:T(8,128)(2,1)S(1)} %collective-permute-done.11.rest_1_, ...), custom_call_target="tpu_custom_call" | custom-call | flops 32000000 | tf_op jit(solution)/shard_map/span_outputs_1/pallas_call | solution.py:643
  84.1 1.5 %collective-permute-start.12 = (bf16[64,1024]{1,0:T(8,128)(2,1)S(1)}, bf16[64,1024]{1,0:T(8,128)(2,1)S(1)}, u32[]{:S(2)}, u32[]{:S(2)}) collective-permute-start(bf16[64,1024]{1,0:T(8,128)(2,1)S(1)} %get-tuple-element.107), channel_id=1, source_target_pairs={{0,4},{4,0},{8,12},{12,8},{16,20},{20,16},{24,28},{28,24},{1,5},{5... | collective-permute-start | bytes 393224 | tf_op jit(solution)/shard_map/ppermute | solution.py:120
  85.6 2.0 %collective-permute-start.13 = (bf16[64,1024]{1,0:T(8,128)(2,1)S(1)}, bf16[64,1024]{1,0:T(8,128)(2,1)S(1)}, u32[]{:S(2)}, u32[]{:S(2)}) collective-permute-start(bf16[64,1024]{1,0:T(8,128)(2,1)S(1)} %get-tuple-element.108), channel_id=1, source_target_pairs={{0,8},{4,12},{8,0},{12,4},{16,24},{20,28},{24,16},{28,20},{1,9},{5... | collective-permute-start | bytes 393224 | tf_op jit(solution)/shard_map/ppermute | solution.py:120
  87.6 0.3 collective-permute-start.14
  87.9 1.4 %collective-permute-done.24.rest_3_ = bf16[64,1024]{1,0:T(8,128)(2,1)S(1)} collective-permute-done((bf16[64,1024]{1,0:T(8,128)(2,1)S(1)}, bf16[64,1024]{1,0:T(8,128)(2,1)S(1)}, u32[]{:S(2)}, u32[]{:S(2)}) %collective-permute-start.24) | collective-permute-done | bytes 131104 | tf_op jit(solution)/shard_map/ppermute | solution.py:120
  89.3 1.2 %finish_0.1.rest_6_ = bf16[2,64,4096]{2,1,0:T(8,128)(2,1)} custom-call(bf16[64,1024]{1,0:T(8,128)(2,1)S(1)} %get-tuple-element.137.rest_0_, bf16[64,1024]{1,0:T(8,128)(2,1)S(1)} %collective-permute-done.22.rest_1_, bf16[64,1024]{1,0:T(8,128)(2,1)S(1)} %collective-permute-done.23.rest_2_, bf16[64,1024]{1,0:T(8,128)(2,1)S(1)} %collective-permute-done.24.rest_3_, ...), custom_call_target="tpu_custom_call" | custom-call | tf_op jit(solution)/shard_map/finish_0/pallas_call | solution.py:658
  90.7 2.8 %collective-permute-done.14.rest_3_ = bf16[64,1024]{1,0:T(8,128)(2,1)S(1)} collective-permute-done((bf16[64,1024]{1,0:T(8,128)(2,1)S(1)}, bf16[64,1024]{1,0:T(8,128)(2,1)S(1)}, u32[]{:S(2)}, u32[]{:S(2)}) %collective-permute-start.14) | collective-permute-done | bytes 131104 | tf_op jit(solution)/shard_map/ppermute | solution.py:120
  93.5 1.2 %finish_1.1 = bf16[2,64,4096]{2,1,0:T(8,128)(2,1)} custom-call(bf16[64,1024]{1,0:T(8,128)(2,1)S(1)} %get-tuple-element.106.rest_0_, bf16[64,1024]{1,0:T(8,128)(2,1)S(1)} %collective-permute-done.12.rest_1_, bf16[64,1024]{1,0:T(8,128)(2,1)S(1)} %collective-permute-done.13.rest_2_, ...), custom_call_target="tpu_custom_call", output_to_operand_aliasing={{}: (6, {})} | custom-call | tf_op jit(solution)/shard_map/finish_1/pallas_call | solution.py:658
  (48 shorter events, 1.6 us)
Async XLA Ops:
  0.0 0.9 copy-start.10
  0.0 0.9 copy-start.9
  0.0 0.9 copy-start.6
  0.9 1.2 %copy-start.2 = (bf16[2,64,4096]{2,1,0:T(8,128)(2,1)S(1)}, bf16[2,64,4096]{2,1,0:T(8,128)(2,1)}, u32[]{:S(2)}) copy-start(bf16[2,64,4096]{2,1,0:T(8,128)(2,1)} %key_ref.3) | copy-start | bytes 3145732
  2.1 1.2 %copy-start.3 = (bf16[2,64,4096]{2,1,0:T(8,128)(2,1)S(1)}, bf16[2,64,4096]{2,1,0:T(8,128)(2,1)}, u32[]{:S(2)}) copy-start(bf16[2,64,4096]{2,1,0:T(8,128)(2,1)} %value_ref.3) | copy-start | bytes 3145732
  3.8 10.9 %collective-permute-start = (bf16[144,1024]{1,0:T(8,128)(2,1)S(1)}, bf16[144,1024]{1,0:T(8,128)(2,1)S(1)}, u32[]{:S(2)}, u32[]{:S(2)}) collective-permute-start(bf16[144,1024]{1,0:T(8,128)(2,1)S(1)} %get-tuple-element.73), channel_id=1, source_target_pairs={{0,12},{4,8},{8,4},{12,0},{16,28},{20,24},{24,20},{28,16},{1,13},{... | collective-permute-start | bytes 884744 | tf_op jit(solution)/shard_map/ppermute | solution.py:120
  6.4 14.7 %collective-permute-start.15 = (bf16[144,1024]{1,0:T(8,128)(2,1)S(1)}, bf16[144,1024]{1,0:T(8,128)(2,1)S(1)}, u32[]{:S(2)}, u32[]{:S(2)}) collective-permute-start(bf16[144,1024]{1,0:T(8,128)(2,1)S(1)} %get-tuple-element.111), channel_id=1, source_target_pairs={{0,4},{4,0},{8,12},{12,8},{16,20},{20,16},{24,28},{28,24},{1,5},{5... | collective-permute-start | bytes 884744 | tf_op jit(solution)/shard_map/ppermute | solution.py:120
  6.9 14.2 %copy-start = (bf16[128,4096]{1,0:T(8,128)(2,1)S(1)}, bf16[128,4096]{1,0:T(8,128)(2,1)}, u32[]{:S(2)}) copy-start(bf16[128,4096]{1,0:T(8,128)(2,1)} %rest_4_.9) | copy-start | bytes 3145732
  6.9 14.2 %copy-start.5 = (f32[2,4096]{1,0:T(2,128)S(1)}, f32[2,4096]{1,0:T(2,128)}, u32[]{:S(2)}) copy-start(f32[2,4096]{1,0:T(2,128)} %rest_5_.7) | copy-start | bytes 98308
  6.9 14.2 %collective-permute-start.16 = (bf16[144,1024]{1,0:T(8,128)(2,1)S(1)}, bf16[144,1024]{1,0:T(8,128)(2,1)S(1)}, u32[]{:S(2)}, u32[]{:S(2)}) collective-permute-start(bf16[144,1024]{1,0:T(8,128)(2,1)S(1)} %get-tuple-element.112), channel_id=1, source_target_pairs={{0,8},{4,12},{8,0},{12,4},{16,24},{20,28},{24,16},{28,20},{1,9},{5... | collective-permute-start | bytes 884744 | tf_op jit(solution)/shard_map/ppermute | solution.py:120
  15.2 14.5 %collective-permute-start.3 = (bf16[144,1024]{1,0:T(8,128)(2,1)S(1)}, bf16[144,1024]{1,0:T(8,128)(2,1)S(1)}, u32[]{:S(2)}, u32[]{:S(2)}) collective-permute-start(bf16[144,1024]{1,0:T(8,128)(2,1)S(1)} %get-tuple-element.77), channel_id=1, source_target_pairs={{0,12},{4,8},{8,4},{12,0},{16,28},{20,24},{24,20},{28,16},{1,13},{... | collective-permute-start | bytes 884744 | tf_op jit(solution)/shard_map/ppermute | solution.py:120
  17.8 19.5 %collective-permute-start.1 = (bf16[144,1024]{1,0:T(8,128)(2,1)S(1)}, bf16[144,1024]{1,0:T(8,128)(2,1)S(1)}, u32[]{:S(2)}, u32[]{:S(2)}) collective-permute-start(bf16[144,1024]{1,0:T(8,128)(2,1)S(1)} %get-tuple-element.75), channel_id=1, source_target_pairs={{0,4},{4,0},{8,12},{12,8},{16,20},{20,16},{24,28},{28,24},{1,5},{5... | collective-permute-start | bytes 884744 | tf_op jit(solution)/shard_map/ppermute | solution.py:120
  18.3 19.8 %collective-permute-start.2 = (bf16[144,1024]{1,0:T(8,128)(2,1)S(1)}, bf16[144,1024]{1,0:T(8,128)(2,1)S(1)}, u32[]{:S(2)}, u32[]{:S(2)}) collective-permute-start(bf16[144,1024]{1,0:T(8,128)(2,1)S(1)} %get-tuple-element.76), channel_id=1, source_target_pairs={{0,8},{4,12},{8,0},{12,4},{16,24},{20,28},{24,16},{28,20},{1,9},{5... | collective-permute-start | bytes 884744 | tf_op jit(solution)/shard_map/ppermute | solution.py:120
  21.1 0.7 copy-start.8
  21.8 8.0 %copy-start.4 = (bf16[2,64,4096]{2,1,0:T(8,128)(2,1)S(1)}, bf16[2,64,4096]{2,1,0:T(8,128)(2,1)}, u32[]{:S(2)}) copy-start(bf16[2,64,4096]{2,1,0:T(8,128)(2,1)} %query_ref.1) | copy-start | bytes 3145732
  27.1 21.9 %collective-permute-start.17 = (bf16[4,128,256]{2,1,0:T(8,128)(2,1)S(1)}, bf16[4,128,256]{2,1,0:T(8,128)(2,1)S(1)}, u32[]{:S(2)}, u32[]{:S(2)}) collective-permute-start(bf16[4,128,256]{2,1,0:T(8,128)(2,1)S(1)} %get-tuple-element.114), channel_id=1, source_target_pairs={{0,16},{4,20},{8,24},{12,28},{16,0},{20,4},{24,8},{28,12},{1,17},{... | collective-permute-start | bytes 786440 | tf_op jit(solution)/shard_map/ppermute | solution.py:561
  30.0 25.9 %collective-permute-start.5 = (bf16[128,1024]{1,0:T(8,128)(2,1)S(1)}, bf16[128,1024]{1,0:T(8,128)(2,1)S(1)}, u32[]{:S(2)}, u32[]{:S(2)}) collective-permute-start(bf16[128,1024]{1,0:T(8,128)(2,1)S(1)} %get-tuple-element.81), channel_id=1, source_target_pairs={{0,4},{4,0},{8,12},{12,8},{16,20},{20,16},{24,28},{28,24},{1,5},{5... | collective-permute-start | bytes 786440 | tf_op jit(solution)/shard_map/ppermute | solution.py:120
  31.6 24.3 %collective-permute-start.6 = (bf16[128,1024]{1,0:T(8,128)(2,1)S(1)}, bf16[128,1024]{1,0:T(8,128)(2,1)S(1)}, u32[]{:S(2)}, u32[]{:S(2)}) collective-permute-start(bf16[128,1024]{1,0:T(8,128)(2,1)S(1)} %get-tuple-element.82), channel_id=1, source_target_pairs={{0,8},{4,12},{8,0},{12,4},{16,24},{20,28},{24,16},{28,20},{1,9},{5... | collective-permute-start | bytes 786440 | tf_op jit(solution)/shard_map/ppermute | solution.py:120
  37.3 18.6 %collective-permute-start.7 = (bf16[128,1024]{1,0:T(8,128)(2,1)S(1)}, bf16[128,1024]{1,0:T(8,128)(2,1)S(1)}, u32[]{:S(2)}, u32[]{:S(2)}) collective-permute-start(bf16[128,1024]{1,0:T(8,128)(2,1)S(1)} %get-tuple-element.83), channel_id=1, source_target_pairs={{0,12},{4,8},{8,4},{12,0},{16,28},{20,24},{24,20},{28,16},{1,13},{... | collective-permute-start | bytes 786440 | tf_op jit(solution)/shard_map/ppermute | solution.py:120
  43.4 15.6 %collective-permute-start.4 = (bf16[4,128,256]{2,1,0:T(8,128)(2,1)S(1)}, bf16[4,128,256]{2,1,0:T(8,128)(2,1)S(1)}, u32[]{:S(2)}, u32[]{:S(2)}) collective-permute-start(bf16[4,128,256]{2,1,0:T(8,128)(2,1)S(1)} %get-tuple-element.79), channel_id=1, source_target_pairs={{0,16},{4,20},{8,24},{12,28},{16,0},{20,4},{24,8},{28,12},{1,17},{... | collective-permute-start | bytes 786440 | tf_op jit(solution)/shard_map/ppermute | solution.py:561
  49.3 11.4 %collective-permute-start.18 = (bf16[4,128,256]{2,1,0:T(8,128)(2,1)S(1)}, bf16[4,128,256]{2,1,0:T(8,128)(2,1)S(1)}, u32[]{:S(2)}, u32[]{:S(2)}) collective-permute-start(bf16[4,128,256]{2,1,0:T(8,128)(2,1)S(1)} %compose_0.1.whole_ref), channel_id=1, source_target_pairs={{0,1},{2,3},{4,5},{6,7},{8,9},{10,11},{12,13},{14,15},{16,17},{18,... | collective-permute-start | bytes 786440 | tf_op jit(solution)/shard_map/ppermute | solution.py:425
  59.3 3.5 %collective-permute-start.8 = (bf16[4,128,256]{2,1,0:T(8,128)(2,1)S(1)}, bf16[4,128,256]{2,1,0:T(8,128)(2,1)S(1)}, u32[]{:S(2)}, u32[]{:S(2)}) collective-permute-start(bf16[4,128,256]{2,1,0:T(8,128)(2,1)S(1)} %compose_1.1.whole_ref), channel_id=1, source_target_pairs={{0,1},{2,3},{4,5},{6,7},{8,9},{10,11},{12,13},{14,15},{16,17},{18,... | collective-permute-start | bytes 786440 | tf_op jit(solution)/shard_map/ppermute | solution.py:425
  60.9 4.2 %collective-permute-start.20 = (bf16[4,128,128]{2,1,0:T(8,128)(2,1)S(1)}, bf16[4,128,128]{2,1,0:T(8,128)(2,1)S(1)}, u32[]{:S(2)}, u32[]{:S(2)}) collective-permute-start(bf16[4,128,128]{2,1,0:T(8,128)(2,1)S(1)} %relay_1.3), channel_id=1, source_target_pairs={{1,3},{5,7},{9,11},{13,15},{17,19},{21,23},{25,27},{29,31}} | collective-permute-start | bytes 393224 | tf_op jit(solution)/shard_map/ppermute | solution.py:425
  61.6 6.3 %collective-permute-start.19 = (bf16[4,128,128]{2,1,0:T(8,128)(2,1)S(1)}, bf16[4,128,128]{2,1,0:T(8,128)(2,1)S(1)}, u32[]{:S(2)}, u32[]{:S(2)}) collective-permute-start(bf16[4,128,128]{2,1,0:T(8,128)(2,1)S(1)} %relay_1.3), channel_id=1, source_target_pairs={{1,2},{5,6},{9,10},{13,14},{17,18},{21,22},{25,26},{29,30}} | collective-permute-start | bytes 393224 | tf_op jit(solution)/shard_map/ppermute | solution.py:425
  63.1 11.2 %collective-permute-start.10 = (bf16[4,128,128]{2,1,0:T(8,128)(2,1)S(1)}, bf16[4,128,128]{2,1,0:T(8,128)(2,1)S(1)}, u32[]{:S(2)}, u32[]{:S(2)}) collective-permute-start(bf16[4,128,128]{2,1,0:T(8,128)(2,1)S(1)} %relay_1.2), channel_id=1, source_target_pairs={{1,3},{5,7},{9,11},{13,15},{17,19},{21,23},{25,27},{29,31}} | collective-permute-start | bytes 393224 | tf_op jit(solution)/shard_map/ppermute | solution.py:425
  63.8 10.6 %collective-permute-start.9 = (bf16[4,128,128]{2,1,0:T(8,128)(2,1)S(1)}, bf16[4,128,128]{2,1,0:T(8,128)(2,1)S(1)}, u32[]{:S(2)}, u32[]{:S(2)}) collective-permute-start(bf16[4,128,128]{2,1,0:T(8,128)(2,1)S(1)} %relay_1.2), channel_id=1, source_target_pairs={{1,2},{5,6},{9,10},{13,14},{17,18},{21,22},{25,26},{29,30}} | collective-permute-start | bytes 393224 | tf_op jit(solution)/shard_map/ppermute | solution.py:425
  68.3 6.8 %collective-permute-start.21 = (bf16[4,128,128]{2,1,0:T(8,128)(2,1)S(1)}, bf16[4,128,128]{2,1,0:T(8,128)(2,1)S(1)}, u32[]{:S(2)}, u32[]{:S(2)}) collective-permute-start(bf16[4,128,128]{2,1,0:T(8,128)(2,1)S(1)} %get-tuple-element.116), channel_id=1, source_target_pairs={{0,16},{4,20},{8,24},{12,28},{16,0},{20,4},{24,8},{28,12},{1,17},{... | collective-permute-start | bytes 393224 | tf_op jit(solution)/shard_map/ppermute | solution.py:561
  74.8 7.9 %collective-permute-start.11 = (bf16[4,128,128]{2,1,0:T(8,128)(2,1)S(1)}, bf16[4,128,128]{2,1,0:T(8,128)(2,1)S(1)}, u32[]{:S(2)}, u32[]{:S(2)}) collective-permute-start(bf16[4,128,128]{2,1,0:T(8,128)(2,1)S(1)} %get-tuple-element.99), channel_id=1, source_target_pairs={{0,16},{4,20},{8,24},{12,28},{16,0},{20,4},{24,8},{28,12},{1,17},{... | collective-permute-start | bytes 393224 | tf_op jit(solution)/shard_map/ppermute | solution.py:561
  76.5 11.1 %collective-permute-start.22 = (bf16[64,1024]{1,0:T(8,128)(2,1)S(1)}, bf16[64,1024]{1,0:T(8,128)(2,1)S(1)}, u32[]{:S(2)}, u32[]{:S(2)}) collective-permute-start(bf16[64,1024]{1,0:T(8,128)(2,1)S(1)} %get-tuple-element.138), channel_id=1, source_target_pairs={{0,4},{4,0},{8,12},{12,8},{16,20},{20,16},{24,28},{28,24},{1,5},{5... | collective-permute-start | bytes 393224 | tf_op jit(solution)/shard_map/ppermute | solution.py:120
  77.3 10.7 %collective-permute-start.23 = (bf16[64,1024]{1,0:T(8,128)(2,1)S(1)}, bf16[64,1024]{1,0:T(8,128)(2,1)S(1)}, u32[]{:S(2)}, u32[]{:S(2)}) collective-permute-start(bf16[64,1024]{1,0:T(8,128)(2,1)S(1)} %get-tuple-element.139), channel_id=1, source_target_pairs={{0,8},{4,12},{8,0},{12,4},{16,24},{20,28},{24,16},{28,20},{1,9},{5... | collective-permute-start | bytes 393224 | tf_op jit(solution)/shard_map/ppermute | solution.py:120
  82.6 6.7 %collective-permute-start.24 = (bf16[64,1024]{1,0:T(8,128)(2,1)S(1)}, bf16[64,1024]{1,0:T(8,128)(2,1)S(1)}, u32[]{:S(2)}, u32[]{:S(2)}) collective-permute-start(bf16[64,1024]{1,0:T(8,128)(2,1)S(1)} %get-tuple-element.140), channel_id=1, source_target_pairs={{0,12},{4,8},{8,4},{12,0},{16,28},{20,24},{24,20},{28,16},{1,13},{... | collective-permute-start | bytes 393224 | tf_op jit(solution)/shard_map/ppermute | solution.py:120
  82.7 6.7 %copy-start.1 = (bf16[2,64,4096]{2,1,0:T(8,128)(2,1)S(1)}, bf16[2,64,4096]{2,1,0:T(8,128)(2,1)}, u32[]{:S(2)}) copy-start(bf16[2,64,4096]{2,1,0:T(8,128)(2,1)} %rest_4_.11) | copy-start | bytes 3145732
  82.7 6.7 %copy-start.7 = (f32[4096]{0:T(1024)S(1)}, f32[4096]{0:T(1024)}, u32[]{:S(2)}) copy-start(f32[4096]{0:T(1024)} %param.23) | copy-start | bytes 49156
  84.1 6.5 %collective-permute-start.12 = (bf16[64,1024]{1,0:T(8,128)(2,1)S(1)}, bf16[64,1024]{1,0:T(8,128)(2,1)S(1)}, u32[]{:S(2)}, u32[]{:S(2)}) collective-permute-start(bf16[64,1024]{1,0:T(8,128)(2,1)S(1)} %get-tuple-element.107), channel_id=1, source_target_pairs={{0,4},{4,0},{8,12},{12,8},{16,20},{20,16},{24,28},{28,24},{1,5},{5... | collective-permute-start | bytes 393224 | tf_op jit(solution)/shard_map/ppermute | solution.py:120
  85.6 5.1 %collective-permute-start.13 = (bf16[64,1024]{1,0:T(8,128)(2,1)S(1)}, bf16[64,1024]{1,0:T(8,128)(2,1)S(1)}, u32[]{:S(2)}, u32[]{:S(2)}) collective-permute-start(bf16[64,1024]{1,0:T(8,128)(2,1)S(1)} %get-tuple-element.108), channel_id=1, source_target_pairs={{0,8},{4,12},{8,0},{12,4},{16,24},{20,28},{24,16},{28,20},{1,9},{5... | collective-permute-start | bytes 393224 | tf_op jit(solution)/shard_map/ppermute | solution.py:120
  87.6 5.9 %collective-permute-start.14 = (bf16[64,1024]{1,0:T(8,128)(2,1)S(1)}, bf16[64,1024]{1,0:T(8,128)(2,1)S(1)}, u32[]{:S(2)}, u32[]{:S(2)}) collective-permute-start(bf16[64,1024]{1,0:T(8,128)(2,1)S(1)} %get-tuple-element.109), channel_id=1, source_target_pairs={{0,12},{4,8},{8,4},{12,0},{16,28},{20,24},{24,20},{28,16},{1,13},{... | collective-permute-start | bytes 393224 | tf_op jit(solution)/shard_map/ppermute | solution.py:120

commit v3 on v2

--- a/solution.py
+++ b/solution.py
@@ -16,7 +16,6 @@
 ANY = pl.BlockSpec(memory_space=pl.ANY)
 VMEM = pl.BlockSpec(memory_space=pltpu.VMEM)
 SMEM = pl.BlockSpec(memory_space=pltpu.SMEM)
-PACK_MIB = 48
 SCALE = 0.1
 
 
@@ -52,46 +51,52 @@
 NT = ((1,), (1,))
 
 
-def pack_kv_kernel(sub, batch, heads, key_ref, value_ref, latent_ref, beta_ref, mark_ref, kind_ref, *rest):
-    outs, (latent, beta, mark, kind, turned, sem, small_sem) = rest[-sub - 7 : -7], rest[-7:]
+def pack_kv_kernel(sub, outer, batches, heads, first, extras, key_ref, value_ref, latent_ref, beta_ref, mark_ref, kind_ref, *rest):
+    outs, (latent, beta, mark, kind, wide, sem, small_sem) = rest[-sub - 7 : -7], rest[-7:]
     lo = lax.rem(lax.axis_index("head"), sub)
-    rows, width = key_ref.shape[1], key_ref.shape[2] // sub
-    small = [
-        pltpu.make_async_copy(source, target, small_sem.at[i])
-        for i, (source, target) in enumerate(
-            ((latent_ref.at[batch], latent), (beta_ref.at[batch], beta), (mark_ref, mark), (kind_ref, kind))
-        )
-    ]
-    for c in small:
-        c.start()
+    hi = lax.div(lax.axis_index("head"), sub)
+    rows, width = key_ref.shape[1], outs[0].shape[1]
+    part = heads // outer * DK
     copies = []
     for k in range(sub):
-        col = pl.multiple_of((lo ^ k) * width, width)
-        for i, ref in enumerate((key_ref, value_ref)):
-            copies.append(
-                pltpu.make_async_copy(
-                    ref.at[batch, :, pl.ds(col, width)], outs[k].at[pl.ds(i * rows, rows)], sem.at[k, i]
-                )
+        for j in range(width // part):
+            col = pl.multiple_of(((lo ^ k) * outer + (hi ^ ((first + j) % outer))) * part, part)
+            for n, batch in enumerate(batches):
+                for i, ref in enumerate((key_ref, value_ref)):
+                    copies.append(
+                        pltpu.make_async_copy(
+                            ref.at[batch, :, pl.ds(col, part)],
+                            outs[k].at[pl.ds((2 * n + i) * rows, rows), pl.ds(j * part, part)],
+                            sem.at[k, j, 2 * n + i],
+                        )
+                    )
+                    copies[-1].start()
+    if extras:
+        (batch,) = batches
+        small = [
+            pltpu.make_async_copy(source, target, small_sem.at[i])
+            for i, (source, target) in enumerate(
+                ((latent_ref.at[batch], latent), (beta_ref.at[batch], beta), (mark_ref, mark), (kind_ref, kind))
             )
-            copies[-1].start()
-    for c in small:
-        c.wait()
-    lanes = width // 128
-    total = beta.shape[1]
-    misc = misc_rows(heads)
-    wide = jnp.concatenate([beta[...].astype(f32), jnp.zeros((rows, 128 - total), f32)], axis=1)
-    turned[...] = jnp.transpose(jnp.concatenate([wide, jnp.zeros((128 - rows, 128), f32)], axis=0))
-    tokens = jnp.concatenate([mark[batch : batch + 1].astype(f32), kind[batch : batch + 1].astype(f32)], axis=0)
-    tokens = jnp.concatenate([tokens, jnp.zeros((2, 128 - rows), f32)], axis=1)
-    for k in range(sub):
-        own = turned[pl.ds(pl.multiple_of((lo ^ k) * heads, heads), heads), :]
-        values = jnp.concatenate([own, tokens, jnp.zeros((misc - heads - 2, 128), f32)], axis=0).astype(bf16)
-        chunks = [latent[16 * j : 16 * j + 16] for j in range(rows // 16)]
-        chunks += [values[16 * j : 16 * j + 16] for j in range(misc // 16)]
-        chunks += [jnp.zeros((16, 128), bf16)] * (-len(chunks) % lanes)
-        for c, chunk in enumerate(chunks):
-            at = 2 * rows + 16 * (c // lanes)
-            outs[k][at : at + 16, (c % lanes) * 128 : (c % lanes + 1) * 128] = chunk
+        ]
+        for c in small:
+            c.start()
+        for c in small:
+            c.wait()
+        lanes = width // 128
+        misc = misc_rows(heads)
+        wide[...] = beta[...].astype(f32)
+        tokens = jnp.concatenate([mark[batch : batch + 1].astype(f32), kind[batch : batch + 1].astype(f32)], axis=0)
+        for k in range(sub):
+            own = wide[pl.ds(pl.multiple_of((lo ^ k) * heads, heads), heads), :]
+            values = jnp.concatenate([own, tokens, jnp.zeros((misc - heads - 2, rows), f32)], axis=0)
+            values = jnp.concatenate([values, jnp.zeros((misc, 128 - rows), f32)], axis=1).astype(bf16)
+            chunks = [latent[16 * j : 16 * j + 16] for j in range(rows // 16)]
+            chunks += [values[16 * j : 16 * j + 16] for j in range(misc // 16)]
+            chunks += [jnp.zeros((16, 128), bf16)] * (-len(chunks) % lanes)
+            for c, chunk in enumerate(chunks):
+                at = 2 * rows + 16 * (c // lanes)
+                outs[k][at : at + 16, (c % lanes) * 128 : (c % lanes + 1) * 128] = chunk
     for c in copies:
         c.wait()
 
@@ -128,11 +133,24 @@
     return (hi ^ (first + lax.div(at, share))) * share + lax.rem(at, share)
 
 
-def state_kernel(sub, outer, first, blocks, heads, tok, hp, decay_ref, *rest):
-    pieces = rest[:sub]
-    up_ref, bias_ref = rest[sub : sub + 2]
-    w_ref, u_ref, shrink_ref, growth_ref, opre_ref, mpre_ref, span_ref, mask_ref, alive_ref = rest[-17:-8]
-    buf, up, levels, kinds, lasts, values, gates, sem = rest[-8:]
+def reorder(parts, place, bits):
+    for bit in range(bits):
+        flipped = lax.rem(lax.div(place, 2**bit), 2) == 1
+        parts = [jnp.where(flipped, parts[i ^ 2**bit], parts[i]) for i in range(len(parts))]
+    return parts
+
+
+def token_rows(pieces, slot, lo, tok, load):
+    per = BLOCK // tok
+    parts = [load(pieces[slot * per + r]) for r in range(per)]
+    return jnp.concatenate(reorder(parts, lax.rem(lo, per), per.bit_length() - 1), axis=0)
+
+
+def state_kernel(sub, outer, first, lane, blocks, heads, tok, hp, decay_ref, *rest):
+    pieces, extras = rest[:sub], rest[sub : 2 * sub]
+    up_ref, bias_ref = rest[2 * sub : 2 * sub + 2]
+    w_ref, u_ref, shrink_ref, growth_ref, opre_ref, mpre_ref, span_ref, mask_ref, alive_ref = rest[-14:-5]
+    levels, kinds, lasts, values, gates = rest[-5:]
     me = lax.rem(lax.axis_index("head"), sub)
     start = place(outer, first, heads // outer, hp)
     width = heads * DK
@@ -148,33 +166,25 @@
 
     @pl.when(step == 0)
     def _():
-        copies = [pltpu.make_async_copy(pieces[k], buf.at[me ^ k], sem.at[k]) for k in range(sub)]
-        copies.append(
-            pltpu.make_async_copy(up_ref.at[:, pl.ds(pl.multiple_of(me * width, width), width)], up, sem.at[sub])
-        )
-        for c in copies:
-            c.start()
         for level in range(count):
             size = 2**level
             here = (row // size == col // size + 1) & ((row // size) % 2 == 1)
             levels[level] = here.astype(bf16)
-        for c in copies:
-            c.wait()
-        lanes = width // 128
+        lanes = extras[0].shape[1] // 128
         misc = misc_rows(heads)
 
-        def chunk(source, c):
+        def chunk(piece, c):
             at = 2 * tok + 16 * (c // lanes)
-            return buf[source, at : at + 16, (c % lanes) * 128 : (c % lanes + 1) * 128]
+            return piece[at : at + 16, (c % lanes) * 128 : (c % lanes + 1) * 128]
 
         for n in range(blocks):
-            tall = jnp.concatenate(
-                [
-                    jnp.concatenate([chunk(s, tok // 16 + j).astype(f32) for j in range(misc // 16)], axis=0)[:, :tok]
-                    for s in range(n * per, (n + 1) * per)
-                ],
-                axis=1,
-            )
+            parts = [
+                jnp.concatenate(
+                    [chunk(extras[n * per + r], tok // 16 + j).astype(f32) for j in range(misc // 16)], axis=0
+                )[:, :tok]
+                for r in range(per)
+            ]
+            tall = jnp.concatenate(reorder(parts, lax.rem(me, per), per.bit_length() - 1), axis=1)
             values[n] = jax.nn.sigmoid(tall)
             mark = tall[heads : heads + 1]
             two = jnp.transpose(jnp.concatenate([tall[heads : heads + 2], jnp.zeros((6, BLOCK), f32)], axis=0))
@@ -184,13 +194,14 @@
             alive_ref[n] = (own == 0).astype(f32)
             lasts[n] = (own == other[:, BLOCK - 1 : BLOCK]).astype(f32)
             kinds[n] = jnp.broadcast_to(two[:, 1:2], (BLOCK, BLOCK))
-            gates[n] = jnp.concatenate(
-                [chunk(s, j) for s in range(n * per, (n + 1) * per) for j in range(tok // 16)], axis=0
+            gates[n] = token_rows(
+                extras, n, me, tok, lambda p: jnp.concatenate([chunk(p, j) for j in range(tok // 16)], axis=0)
             )
 
     low2 = jnp.concatenate([low_b, low_b], axis=1)
     lower = (row > col).astype(f32)
     items = [(i, n) for i in range(hp) for n in range(blocks)]
+    every = range(blocks)
     strict_all, rhs_all, tail_all, carry_all = {}, {}, {}, {}
     betas = []
     for n in range(blocks):
@@ -198,18 +209,18 @@
         betas.append(jnp.transpose(jnp.concatenate([mine, jnp.zeros((8 - hp % 8, BLOCK), f32)], axis=0)))
     for i in range(hp):
         h = start + i
-        at = pl.ds(pl.multiple_of(h * DK, DK), DK)
+        at = pl.ds(pl.multiple_of(lane + (step * hp + i) * DK, DK), DK)
         bias_at = pl.ds(pl.multiple_of(me * width + h * DK, DK), DK)
         audio, text = bias_ref[0:1, bias_at], bias_ref[1:2, bias_at]
         rate = -LOG2E * jnp.exp(jnp.full((1, DK), decay_ref[me * heads + h], f32))
         for n in range(blocks):
-            gate = dot(gates[n], up[:, at]).astype(bf16).astype(f32)
+            gate = dot(gates[n], up_ref[:, bias_at]).astype(bf16).astype(f32)
             pre = gate + jnp.where(kinds[n] == 1.0, text, audio)
             soft = jnp.maximum(pre, 0.0) + jnp.log(1.0 + jnp.exp(-jnp.abs(pre)))
             high, rest_part = split(rate * soft)
             total = dot(low2, jnp.concatenate([high, rest_part], axis=0))
-            key = buf[n * per : (n + 1) * per, 0:tok, at].reshape(BLOCK, DK).astype(f32)
-            value = buf[n * per : (n + 1) * per, tok : 2 * tok, at].reshape(BLOCK, DK).astype(f32)
+            key = token_rows(pieces, n, me, tok, lambda p: p[0:tok, at]).astype(f32)
+            value = token_rows(pieces, n, me, tok, lambda p: p[tok : 2 * tok, at]).astype(f32)
             unit = key * lax.rsqrt(jnp.sum(key * key, axis=1, keepdims=True) + norm_eps)
             growth = jnp.exp2(total)
             grown = unit * growth
@@ -255,10 +266,16 @@
         uh, ul = split(both[t][:, DK:])
         th, tl = split(tail_all[t])
         joint = dot(th, jnp.concatenate([w, uh], axis=1))
-        fade[t] = joint[:, :DK]
+        fade[t] = joint[:, :DK].astype(bf16)
         offs[t] = joint[:, DK:] + dot(jnp.concatenate([th, tl], axis=1), jnp.concatenate([ul, uh], axis=0))
+    bits = blocks.bit_length() - 1
+    for i in range(hp):
+        for made in (fade, offs, carry_all):
+            in_time = reorder([made[i, n] for n in every], lax.div(me, per), bits)
+            for n in every:
+                made[i, n] = in_time[n]
     offset = {i: offs[i, 0] for i in range(hp)}
-    move = {i: jnp.where(row == col, carry_all[i, 0], 0.0) - fade[i, 0] for i in range(hp)}
+    move = {i: jnp.where(row == col, carry_all[i, 0], 0.0) - fade[i, 0].astype(f32) for i in range(hp)}
     for n in range(1, blocks):
         for i in range(hp):
             opre_ref[i, n - 1] = offset[i]
@@ -292,7 +309,8 @@
         out_ref[h, :, DK:] = whole[1]
 
 
-def relay_kernel(share, whole_ref, got_ref, out_ref):
+def relay_kernel(share, whole_ref, got_ref, *rest):
+    out_ref = rest[-1]
     for h in range(share):
         whole = joined(
             (whole_ref[h, :, :DK], whole_ref[h, :, DK:]), (got_ref[h, :, :DK], got_ref[h, :, DK:])
@@ -305,8 +323,7 @@
 def seed_kernel(outer, share, raw, *rest):
     parts = rest[:outer]
     early_ref, in_ref = rest[outer : outer + 2]
-    outs = rest[outer + 2 : 2 * outer + 2]
-    order, seeds = rest[2 * outer + 2 :]
+    outs, (order, seeds) = rest[-outer - 2 : -2], rest[-2:]
     hi = lax.div(lax.axis_index("head"), lax.axis_size("head") // outer)
     ordered(outer, parts, order)
     row = lax.broadcasted_iota(jnp.int32, (DK, DK), 0)
@@ -330,27 +347,14 @@
 def query_kernel(sub, outer, first, blocks, heads, tok, batch, hp, *rest):
     pieces = rest[:sub]
     w_ref, u_ref, shrink_ref, growth_ref, mask_ref, alive_ref = rest[sub : sub + 6]
-    base_ref, rows_ref, buf, sem = rest[-4:]
+    base_ref, rows_ref = rest[-2:]
     lo = lax.rem(lax.axis_index("head"), sub)
-    per = BLOCK // tok
-
-    @pl.when(pl.program_id(0) == 0)
-    def _():
-        copies = [
-            pltpu.make_async_copy(pieces[k].at[pl.ds(batch * tok, tok)], buf.at[lo ^ k], sem.at[k])
-            for k in range(sub)
-        ]
-        for c in copies:
-            c.start()
-        for c in copies:
-            c.wait()
-
     items = [(i, n) for i in range(hp) for n in range(blocks)]
     start = place(outer, first, heads // outer, hp)
     at = [pl.ds(pl.multiple_of((start + i) * DK, DK), DK) for i in range(hp)]
     grown, mix = {}, {}
     for i, n in items:
-        query = buf[n * per : (n + 1) * per, :, at[i]].reshape(BLOCK, DK).astype(f32)
+        query = token_rows(pieces, n, lo, tok, lambda p: p[batch * tok : (batch + 1) * tok, at[i]]).astype(f32)
         unit = query * (lax.rsqrt(jnp.sum(query * query, axis=1, keepdims=True) + norm_eps) * DK ** (-0.5))
         grown[i, n] = unit * growth_ref[i, n]
         gh, gl = split(grown[i, n])
@@ -369,7 +373,7 @@
 
 def output_kernel(sub, outer, sets, blocks, heads, tok, *rest):
     seeds, rest = rest[:outer], rest[outer:]
-    outs, obuf = rest[-sub - 1 : -1], rest[-1]
+    outs = rest[-sub:]
     lo = lax.rem(lax.axis_index("head"), sub)
     hi = lax.div(lax.axis_index("head"), sub)
     share = heads // outer
@@ -380,12 +384,15 @@
             j, i = first + r // share, r % share
             at = pl.ds(pl.multiple_of(((hi ^ j) * share + i) * DK, DK), DK)
             seed = seeds[j][i]
+            states = [seed] + [
+                (opre_ref[r, n] + dot(mpre_ref[r, n], seed)).astype(bf16) for n in range(blocks - 1)
+            ]
+            states = reorder(states, lax.div(lo, per), blocks.bit_length() - 1)
             for n in range(blocks):
-                state = seed if n == 0 else opre_ref[r, n - 1] + dot(mpre_ref[r, n - 1], seed)
-                core = base_ref[r, n] + dot(rows_ref[r, n], state)
-                obuf[n * per : (n + 1) * per, :, at] = core.astype(bf16).reshape(per, tok, DK)
-    for k in range(sub):
-        outs[k][...] = obuf[lo ^ k]
+                core = (base_ref[r, n] + dot(rows_ref[r, n], states[n])).astype(bf16)
+                rows = reorder([core[t * tok : (t + 1) * tok] for t in range(per)], lax.rem(lo, per), per.bit_length() - 1)
+                for t in range(per):
+                    outs[n * per + t][:, at] = rows[t]
 
 
 def finish_kernel(sub, heads, *rest):
@@ -405,7 +412,7 @@
     return jnp.einsum("hij,hjk->hik", a, b, preferred_element_type=f32)
 
 
-def before(span):
+def before(span, *after):
     count = lax.axis_size("seq")
     place = lax.axis_index("seq")
     unit_mat = jnp.broadcast_to(jnp.eye(DK, dtype=bf16), span.shape[:1] + (DK, DK))
@@ -447,12 +454,12 @@
         whole = pl.pallas_call(
             functools.partial(relay_kernel, share),
             out_shape=jax.ShapeDtypeStruct((share, DK, DK if last else 2 * DK), bf16),
-            in_specs=[VMEM] * 2,
+            in_specs=[VMEM] * 2 + [ANY] * len(after),
             out_specs=VMEM,
-            compiler_params=params(),
+            compiler_params=params(16),
             cost_estimate=cost(0, 0),
             name=f"relay_{size}",
-        )(whole, got)
+        )(whole, got, *after)
         size *= 2
     if early is None:
         early = jnp.concatenate([jnp.zeros_like(unit_mat), unit_mat], axis=2)
@@ -483,32 +490,32 @@
     width = heads * DK
     blocks = tok * sub // BLOCK
     sds = jax.ShapeDtypeStruct
-    extra_rows = 16 * -(-(tok // 16 + misc_rows(heads) // 16) // (width // 128))
-    piece_rows = 2 * tok + extra_rows
-
-    def pack_kv(batch, *after):
+    by_head_t = jnp.swapaxes(beta_raw, 1, 2)
+    sets = ([(1, outer - 1)] if outer > 1 else []) + [(0, 1)]
+    misc = tok // 16 + misc_rows(heads) // 16
+
+    def pack_kv(of, first, shares, extras, *after):
+        lanes = shares * share
+        rows = 2 * tok * len(of) + (16 * -(-misc // lanes) if extras else 0)
         return pl.pallas_call(
-            functools.partial(pack_kv_kernel, sub, batch, heads),
-            out_shape=[sds((piece_rows, width), bf16)] * sub,
+            functools.partial(pack_kv_kernel, sub, outer, of, heads, first, extras),
+            out_shape=[sds((rows, lanes * DK), bf16)] * sub,
             in_specs=[ANY] * (6 + len(after)),
             out_specs=[VMEM] * sub,
             scratch_shapes=[
                 pltpu.VMEM(gate_latent.shape[1:], bf16),
-                pltpu.VMEM(beta_raw.shape[1:], bf16),
+                pltpu.VMEM(by_head_t.shape[1:], bf16),
                 pltpu.VMEM(boundary.shape, jnp.int32),
                 pltpu.VMEM(modality.shape, jnp.int32),
-                pltpu.VMEM((128, 128), f32),
-                pltpu.SemaphoreType.DMA((sub, 3)),
+                pltpu.VMEM(by_head_t.shape[1:], f32),
+                pltpu.SemaphoreType.DMA((sub, shares, 2 * len(of))),
                 pltpu.SemaphoreType.DMA((4,)),
             ],
-            compiler_params=params(PACK_MIB),
+            compiler_params=params(16 if after else 60),
             cost_estimate=cost(0, 0),
-            name=f"pack_kv_{batch}",
-        )(key_rows, value_rows, gate_latent, beta_raw, boundary, modality, *after)
-
-    kv = []
-    for b in range(batches):
-        kv.append(exchange(pack_kv(b, *([] if b == 0 else [kv[-1][-1]]))))
+            name=f"pack_kv_{of[0]}_{first}",
+        )(key_rows, value_rows, gate_latent, by_head_t, boundary, modality, *after)
+
     hp = min(share, max(1, 8 // blocks))
     while share % hp:
         hp -= 1
@@ -533,87 +540,65 @@
     ]
     count = lax.axis_size("head")
 
-    def state_maps(b, first, shares, *after):
+    def state_maps(b, part, *after):
+        first, shares = sets[part]
+        pieces = extras = kv[b]
+        lane = sum(earlier for _, earlier in sets[:part]) * share * DK
         here = shares * share
         return pl.pallas_call(
-            functools.partial(state_kernel, sub, outer, first, blocks, heads, tok, hp),
+            functools.partial(state_kernel, sub, outer, first, lane, blocks, heads, tok, hp),
             grid=(here // hp,),
             out_shape=[sds((here, *dims), kind) for dims, kind in local_dims] + [sds((blocks, BLOCK, BLOCK), f32)] * 2,
-            in_specs=[SMEM] + [ANY] * sub + [ANY, VMEM] + [ANY] * len(after),
+            in_specs=[SMEM] + [VMEM] * (2 * sub + 2) + [ANY] * len(after),
             out_specs=[by_head(*dims) for dims, _ in local_dims] + [whole, whole],
             scratch_shapes=[
-                pltpu.VMEM((sub, piece_rows, width), bf16),
-                pltpu.VMEM((DK, width), bf16),
                 pltpu.VMEM((levels, BLOCK, BLOCK), bf16),
                 pltpu.VMEM((blocks, BLOCK, BLOCK), f32),
                 pltpu.VMEM((blocks, BLOCK, BLOCK), f32),
                 pltpu.VMEM((blocks, misc_rows(heads), BLOCK), f32),
                 pltpu.VMEM((blocks, BLOCK, BLOCK), bf16),
-                pltpu.SemaphoreType.DMA((sub + 1,)),
             ],
             compiler_params=params(),
             cost_estimate=cost(SCALE * here * blocks * 2e8, 0),
             name=f"state_maps_{b}_{first}",
-        )(decay_log, *kv[b], gate_up, dt_bias, *after)
+        )(decay_log, *pieces, *extras, gate_up, dt_bias, *after)
 
     def swap(parts):
         return [parts[0]] + [
             lax.ppermute(parts[j], "head", [(i, i ^ (j * sub)) for i in range(count)]) for j in range(1, outer)
         ]
 
-    sets = ([(1, outer - 1)] if outer > 1 else []) + [(0, 1)]
-    local, split_maps = [], []
-    q_here = None
-    for b in range(batches):
-        made = []
-        for first, shares in sets:
-            after = [kv[b + 1][0]] if first == sets[0][0] and b + 1 < batches else []
-            made.append(state_maps(b, first, shares, *after))
-        local.append(made)
-        sent = []
-        if outer > 1:
-            spans = made[0][6]
-            sent = [spans] if outer == 2 else [spans[j * share : (j + 1) * share] for j in range(outer - 1)]
-        split_maps.append(swap([made[-1][6]] + sent))
-        if q_here is None:
-            q_here = exchange(
-                pl.pallas_call(
-                    functools.partial(pack_q_kernel, sub, batches),
-                    out_shape=[sds((batches * tok, width), bf16)] * sub,
-                    in_specs=[ANY, ANY],
-                    out_specs=[VMEM] * sub,
-                    scratch_shapes=[pltpu.SemaphoreType.DMA((sub, batches))],
-                    compiler_params=params(),
-                    cost_estimate=cost(0, 0),
-                    name="pack_q",
-                )(query_rows, kv[-1][-1])
-            )
-    queries = []
-    for b in range(batches):
-        made = []
-        for (first, shares), here in zip(sets, local[b]):
-            made.append(
-                pl.pallas_call(
-                    functools.partial(query_kernel, sub, outer, first, blocks, heads, tok, b, hp),
-                    grid=(shares * share // hp,),
-                    out_shape=[
-                        sds((shares * share, blocks, DK, DK), f32),
-                        sds((shares * share, blocks, DK, DK), bf16),
-                    ],
-                    in_specs=[ANY] * sub + [per_head, per_head, wide_head, per_head] + [whole] * 2,
-                    out_specs=[per_head] * 2,
-                    scratch_shapes=[pltpu.VMEM((sub, tok, width), bf16), pltpu.SemaphoreType.DMA((sub,))],
-                    compiler_params=params(),
-                    cost_estimate=cost(SCALE * shares * share * blocks * 1e8, 0),
-                    name=f"query_parts_{b}_{first}",
-                )(*q_here, *here[:4], *here[7:9])
-            )
-        queries.append(made)
-    back = []
-    for b in range(batches):
-        parts = split_maps[b]
-        after = [made[1] for made in queries[-1]] if b == batches - 1 else []
-        total = pl.pallas_call(
+    def pack_q(*after):
+        return pl.pallas_call(
+            functools.partial(pack_q_kernel, sub, batches),
+            out_shape=[sds((batches * tok, width), bf16)] * sub,
+            in_specs=[ANY] * (1 + len(after)),
+            out_specs=[VMEM] * sub,
+            scratch_shapes=[pltpu.SemaphoreType.DMA((sub, batches))],
+            compiler_params=params(16),
+            cost_estimate=cost(0, 0),
+            name="pack_q",
+        )(query_rows, *after)
+
+    def query_parts(b, part, *after):
+        first, shares = sets[part]
+        here = local[b][part]
+        return pl.pallas_call(
+            functools.partial(query_kernel, sub, outer, first, blocks, heads, tok, b, hp),
+            grid=(shares * share // hp,),
+            out_shape=[
+                sds((shares * share, blocks, DK, DK), f32),
+                sds((shares * share, blocks, DK, DK), bf16),
+            ],
+            in_specs=[VMEM] * sub + [per_head, per_head, wide_head, per_head] + [whole] * 2 + [ANY] * len(after),
+            out_specs=[per_head] * 2,
+            compiler_params=params(),
+            cost_estimate=cost(SCALE * shares * share * blocks * 1e8, 0),
+            name=f"query_parts_{b}_{first}",
+        )(*q_here, *here[:4], *here[7:9], *after)
+
+    def compose(b, parts, *after):
+        return pl.pallas_call(
             functools.partial(compose_kernel, outer, share),
             out_shape=sds((share, DK, 2 * DK), bf16),
             in_specs=[VMEM] * outer + [ANY] * len(after),
@@ -623,34 +608,77 @@
             cost_estimate=cost(0, 0),
             name=f"compose_{b}",
         )(*parts, *after)
-        early, incoming, raw = before(total)
-        mine = pl.pallas_call(
+
+    def seeds(b, parts, early, incoming, raw, *after):
+        return pl.pallas_call(
             functools.partial(seed_kernel, outer, share, raw),
             out_shape=[sds((share, DK, DK), bf16)] * outer,
-            in_specs=[VMEM] * (outer + 2),
+            in_specs=[VMEM] * (outer + 2) + [ANY] * len(after),
             out_specs=[VMEM] * outer,
             scratch_shapes=[
                 pltpu.VMEM((outer, share, DK, 2 * DK), bf16),
                 pltpu.VMEM((outer, share, DK, DK), bf16),
             ],
-            compiler_params=params(),
+            compiler_params=params(16),
             cost_estimate=cost(0, 0),
             name=f"seeds_{b}",
-        )(*parts, early, incoming)
+        )(*parts, early, incoming, *after)
+
+    def outputs(b, queries, given):
         operands = []
-        for made, here in zip(queries[b], local[b]):
+        for made, here in zip(queries, local[b]):
             operands += [*made, *here[4:6]]
-        outs = pl.pallas_call(
+        return pl.pallas_call(
             functools.partial(output_kernel, sub, outer, sets, blocks, heads, tok),
             out_shape=[sds((tok, width), bf16)] * sub,
             in_specs=[VMEM] * (len(operands) + outer),
             out_specs=[VMEM] * sub,
-            scratch_shapes=[pltpu.VMEM((sub, tok, width), bf16)],
             compiler_params=params(),
             cost_estimate=cost(SCALE * heads * blocks * 2e7, 0),
             name=f"span_outputs_{b}",
-        )(*swap(mine), *operands)
-        back.append(exchange(outs))
+        )(*given, *operands)
+
+    def swapped(made):
+        sent = []
+        if outer > 1:
+            spans = made[0][6]
+            sent = [spans] if outer == 2 else [spans[j * share : (j + 1) * share] for j in range(outer - 1)]
+        return swap([made[-1][6]] + sent)
+
+    parts_here = range(len(sets))
+    jobs = [(b, part) for part in parts_here for b in range(batches)]
+    local = [[None] * len(sets) for _ in range(batches)]
+    queries = [[] for _ in range(batches)]
+    moved, totals, begins, outs, back, relays = {}, {}, {}, {}, [], {}
+    token = None
+    kv = []
+    for b in range(batches):
+        packed = pack_kv([b], sets[0][0], outer, True, *([] if token is None else [token]))
+        kv.append(exchange(packed))
+        token = kv[b][-1]
+    packed_q = pack_q(token)
+    q_here = exchange(packed_q)
+    token = packed[0]
+    for b, part in jobs:
+        local[b][part] = state_maps(b, part, token)
+    for b in range(batches):
+        moved[b] = swapped(local[b])
+    def chain(b, *after):
+        totals[b] = compose(b, moved[b], *after)
+        relays[b] = before(totals[b])
+        begins[b] = seeds(b, moved[b], *relays[b])
+
+    last = batches - 1
+    for part in parts_here:
+        queries[last].append(query_parts(last, part))
+    for b in range(batches):
+        chain(b, *([made[1] for made in queries[last]] if b == last else []))
+    for b in range(last):
+        for part in parts_here:
+            queries[b].append(query_parts(b, part))
+    for b in range(batches):
+        outs[b] = outputs(b, queries[b], swap(begins[b]))
+        back.append(exchange(outs[b]))
 
     mixed = None
     for b in range(batches):

time: 96.1 us -> 93.4 us (0.972)
  waiting for transfers between devices: 17.6 us -> 21.8 us
  local copies, waits for them, and re-layouts: 3.97 us -> 0.68 us
  starting transfers between devices: 36.9 us -> 34.7 us
  Pallas kernels: 35.8 us -> 34.8 us
    ppermute x4, waiting for transfers between devices: 0.01 us -> 3.73 us  [swap(): lax.ppermute(parts[j], 'head', [(i, i ^ j * sub) for i in range(count)])]
    unnamed x23 -> x26, local copies, waits for them, and re-layouts: 3.97 us -> 0.68 us
    ppermute x15, starting transfers between devices: 24.4 us -> 21.5 us  [exchange(): lax.ppermute(pieces[k], 'head', [(i, i ^ k) for i in range(count)])]
    pallas_call x17, Pallas kernels: 32.8 us -> 31.9 us  [the longest x4 20.4 us: state_maps(): pl.pallas_call(functools.partial(state_kernel, sub, outer, first, lane, b...]
  transfers between devices with their start and end apart: 25 -> 25, of which waited for: 8 -> 8; matrix products, arithmetic and copies ran while one was open for 0% -> 0% of each run, Pallas kernels for 36% -> 33%
where the time goes in v3:
time: 93.4 us; the launch traced here: 92.4 us
  Pallas kernels  34.8 us (37%)
  starting transfers between devices  34.7 us (37%)
  waiting for transfers between devices  21.8 us (23%)
    ppermute x15, starting transfers between devices, exchange(): lax.ppermute(pieces[k], 'head', [(i, i ^ k) for i in range(count)])  21.5 us
    pallas_call x4, Pallas kernels, state_maps(): pl.pallas_call(functools.partial(state_kernel, sub, outer, first, lane, b...  20.4 us
    ppermute x15, waiting for transfers between devices, exchange(): lax.ppermute(pieces[k], 'head', [(i, i ^ k) for i in range(count)])  15.3 us
    ppermute x6, starting transfers between devices, before(): part = lax.ppermute(payload, 'seq', pairs)  6.71 us
    ppermute x4, starting transfers between devices, swap(): lax.ppermute(parts[j], 'head', [(i, i ^ j * sub) for i in range(count)])  6.45 us
    ppermute x4, waiting for transfers between devices, swap(): lax.ppermute(parts[j], 'head', [(i, i ^ j * sub) for i in range(count)])  3.73 us
    pallas_call x4, Pallas kernels, query_parts(): pl.pallas_call(functools.partial(query_kernel, sub, outer, first, blocks,...  3.37 us
    pallas_call x2, Pallas kernels, pack_kv(): pl.pallas_call(functools.partial(pack_kv_kernel, sub, outer, of, heads, f...  3.08 us
  transfers between devices with their start and end apart: 25, of which 8 were waited for; matrix products, arithmetic and copies ran while one was open for 0% of the time, Pallas kernels for 33%

profile of v3, /device:TPU:2, one launch (start us, length us, event | category | flops | bytes accessed | tf_op | source)
XLA Modules:
  0.0 92.4 jit_solution(11179709261561198031)
XLA Ops:
  0.0 2.6 %pack_kv_0_1.1 = (bf16[144,1024]{1,0:T(8,128)(2,1)}, bf16[144,1024]{1,0:T(8,128)(2,1)}, bf16[144,1024]{1,0:T(8,128)(2,1)}, bf16[144,1024]{1,0:T(8,128)(2,1)}) custom-call(bf16[2,64,4096]{2,1,0:T(8,128)(2,1)} %key_ref.3, bf16[2,64,4096]{2,1,0:T(8,128)(2,1)} %value_ref.3, bf16[2,64,128]{2,1,0:T(8,128)(2,1)} %latent_ref.3, bf16[2,32,64]{2,1,0:T(8,128)(2,1)} %bitcast.2, ...), custom_call_target="tpu_custom_call" | custom-call | tf_op jit(solution)/shard_map/pack_kv_0_1/pallas_call | solution.py:500
  2.6 2.6 %collective-permute-start = (bf16[144,1024]{1,0:T(8,128)(2,1)}, bf16[144,1024]{1,0:T(8,128)(2,1)S(1)}, u32[]{:S(2)}, u32[]{:S(2)}) collective-permute-start(bf16[144,1024]{1,0:T(8,128)(2,1)} %get-tuple-element.73), channel_id=1, source_target_pairs={{0,12},{4,8},{8,4},{12,0},{16,28},{20,24},{24,20},{28,16},{1,13},{... | collective-permute-start | bytes 884744 | tf_op jit(solution)/shard_map/ppermute | solution.py:125
  5.2 0.5 collective-permute-start.15
  5.7 0.4 collective-permute-start.16
  6.2 7.5 %collective-permute-done.rest_0_.rest_3_.rest_7_ = bf16[144,1024]{1,0:T(8,128)(2,1)S(1)} collective-permute-done((bf16[144,1024]{1,0:T(8,128)(2,1)}, bf16[144,1024]{1,0:T(8,128)(2,1)S(1)}, u32[]{:S(2)}, u32[]{:S(2)}) %collective-permute-start) | collective-permute-done | bytes 294944 | tf_op jit(solution)/shard_map/ppermute | solution.py:125
  13.8 0.5 pack_kv_1_1.1
  14.3 2.6 %collective-permute-start.3 = (bf16[144,1024]{1,0:T(8,128)(2,1)S(1)}, bf16[144,1024]{1,0:T(8,128)(2,1)S(1)}, u32[]{:S(2)}, u32[]{:S(2)}) collective-permute-start(bf16[144,1024]{1,0:T(8,128)(2,1)S(1)} %get-tuple-element.77), channel_id=1, source_target_pairs={{0,12},{4,8},{8,4},{12,0},{16,28},{20,24},{24,20},{28,16},{1,13},{... | collective-permute-start | bytes 884744 | tf_op jit(solution)/shard_map/ppermute | solution.py:125
  16.8 0.5 collective-permute-start.1
  17.4 0.4 collective-permute-start.2
  17.8 2.3 %collective-permute-done.15.rest_1_.rest_5_ = bf16[144,1024]{1,0:T(8,128)(2,1)S(1)} collective-permute-done((bf16[144,1024]{1,0:T(8,128)(2,1)}, bf16[144,1024]{1,0:T(8,128)(2,1)S(1)}, u32[]{:S(2)}, u32[]{:S(2)}) %collective-permute-start.15) | collective-permute-done | bytes 294944 | tf_op jit(solution)/shard_map/ppermute | solution.py:125
  20.1 0.6 copy-done.10
  20.8 4.9 %state_maps_0_1.1 = (bf16[4,2,128,128]{3,2,1,0:T(8,128)(2,1)S(1)}, f32[4,2,128,128]{3,2,1,0:T(8,128)S(1)}, bf16[4,2,128,256]{3,2,1,0:T(8,128)(2,1)S(1)}, f32[4,2...) custom-call(f32[32]{0:T(128)S(1)} %copy-done.10, ...), custom_call_target="tpu_custom_call" | custom-call | flops 160000000 | tf_op jit(solution)/shard_map/state_maps_0_1/pallas_call | solution.py:548
  25.7 2.7 %collective-permute-start.17 = (bf16[4,128,256]{2,1,0:T(8,128)(2,1)S(1)}, bf16[4,128,256]{2,1,0:T(8,128)(2,1)S(1)}, u32[]{:S(2)}, u32[]{:S(2)}) collective-permute-start(bf16[4,128,256]{2,1,0:T(8,128)(2,1)S(1)} %get-tuple-element.114), channel_id=1, source_target_pairs={{0,16},{4,20},{8,24},{12,28},{16,0},{20,4},{24,8},{28,12},{1,17},{... | collective-permute-start | bytes 786440 | tf_op jit(solution)/shard_map/ppermute | solution.py:568
  28.4 1.0 %pack_q.1 = (bf16[128,1024]{1,0:T(8,128)(2,1)S(1)}, bf16[128,1024]{1,0:T(8,128)(2,1)}, bf16[128,1024]{1,0:T(8,128)(2,1)S(1)}, bf16[128,1024]{1,0:T(8,128)(2,1)S(1)}) custom-call(bf16[2,64,4096]{2,1,0:T(8,128)(2,1)S(1)} %copy-done.5, bf16[144,1024]{1,0:T(8,128)(2,1)S(1)} %collective-permute-done.3.rest_3_.rest_7_.rest_0_), custom_call_target="tpu_custom_call" | custom-call | tf_op jit(solution)/shard_map/pack_q/pallas_call | solution.py:572
  29.3 1.6 %collective-permute-start.5 = (bf16[128,1024]{1,0:T(8,128)(2,1)}, bf16[128,1024]{1,0:T(8,128)(2,1)S(1)}, u32[]{:S(2)}, u32[]{:S(2)}) collective-permute-start(bf16[128,1024]{1,0:T(8,128)(2,1)} %get-tuple-element.81), channel_id=1, source_target_pairs={{0,4},{4,0},{8,12},{12,8},{16,20},{20,16},{24,28},{28,24},{1,5},{5... | collective-permute-start | bytes 786440 | tf_op jit(solution)/shard_map/ppermute | solution.py:125
  30.9 5.7 %collective-permute-start.6 = (bf16[128,1024]{1,0:T(8,128)(2,1)S(1)}, bf16[128,1024]{1,0:T(8,128)(2,1)S(1)}, u32[]{:S(2)}, u32[]{:S(2)}) collective-permute-start(bf16[128,1024]{1,0:T(8,128)(2,1)S(1)} %get-tuple-element.82), channel_id=1, source_target_pairs={{0,8},{4,12},{8,0},{12,4},{16,24},{20,28},{24,16},{28,20},{1,9},{5... | collective-permute-start | bytes 786440 | tf_op jit(solution)/shard_map/ppermute | solution.py:125
  36.6 0.9 collective-permute-done.2.rest_2_.rest_6_
  37.5 5.6 %state_maps_1_1.1 = (bf16[4,2,128,128]{3,2,1,0:T(8,128)(2,1)S(1)}, f32[4,2,128,128]{3,2,1,0:T(8,128)S(1)}, bf16[4,2,128,256]{3,2,1,0:T(8,128)(2,1)S(1)}, f32[4,2...) custom-call(f32[32]{0:T(128)S(1)} %copy-done.10, ...), custom_call_target="tpu_custom_call" | custom-call | flops 160000000 | tf_op jit(solution)/shard_map/state_maps_1_1/pallas_call | solution.py:548
  43.1 4.9 %state_maps_0_0.1 = (bf16[4,2,128,128]{3,2,1,0:T(8,128)(2,1)S(1)}, f32[4,2,128,128]{3,2,1,0:T(8,128)S(1)}, bf16[4,2,128,256]{3,2,1,0:T(8,128)(2,1)S(1)}, f32[4,2...) custom-call(f32[32]{0:T(128)S(1)} %copy-done.10, ...), custom_call_target="tpu_custom_call" | custom-call | flops 160000000 | tf_op jit(solution)/shard_map/state_maps_0_0/pallas_call | solution.py:548
  48.1 0.3 compose_0.1.whole_ref
  48.3 1.5 %collective-permute-start.18 = (bf16[4,128,256]{2,1,0:T(8,128)(2,1)S(1)}, bf16[4,128,256]{2,1,0:T(8,128)(2,1)S(1)}, u32[]{:S(2)}, u32[]{:S(2)}) collective-permute-start(bf16[4,128,256]{2,1,0:T(8,128)(2,1)S(1)} %compose_0.1.whole_ref), channel_id=1, source_target_pairs={{0,1},{2,3},{4,5},{6,7},{8,9},{10,11},{12,13},{14,15},{16,17},{18,... | collective-permute-start | bytes 786440 | tf_op jit(solution)/shard_map/ppermute | solution.py:432
  49.8 4.9 %state_maps_1_0.1 = (bf16[4,2,128,128]{3,2,1,0:T(8,128)(2,1)S(1)}, f32[4,2,128,128]{3,2,1,0:T(8,128)S(1)}, bf16[4,2,128,256]{3,2,1,0:T(8,128)(2,1)S(1)}, f32[4,2...) custom-call(f32[32]{0:T(128)S(1)} %copy-done.10, ...), custom_call_target="tpu_custom_call" | custom-call | flops 160000000 | tf_op jit(solution)/shard_map/state_maps_1_0/pallas_call | solution.py:548
  54.8 0.8 query_parts_1_1.1
  55.7 0.8 query_parts_1_0.1
  56.5 0.3 compose_1.1.whole_ref
  56.8 1.3 %collective-permute-start.8 = (bf16[4,128,256]{2,1,0:T(8,128)(2,1)S(1)}, bf16[4,128,256]{2,1,0:T(8,128)(2,1)S(1)}, u32[]{:S(2)}, u32[]{:S(2)}) collective-permute-start(bf16[4,128,256]{2,1,0:T(8,128)(2,1)S(1)} %compose_1.1.whole_ref), channel_id=1, source_target_pairs={{0,1},{2,3},{4,5},{6,7},{8,9},{10,11},{12,13},{14,15},{16,17},{18,... | collective-permute-start | bytes 786440 | tf_op jit(solution)/shard_map/ppermute | solution.py:432
  58.3 0.7 collective-permute-start.20
  59.0 1.3 %collective-permute-start.19 = (bf16[4,128,128]{2,1,0:T(8,128)(2,1)S(1)}, bf16[4,128,128]{2,1,0:T(8,128)(2,1)S(1)}, u32[]{:S(2)}, u32[]{:S(2)}) collective-permute-start(bf16[4,128,128]{2,1,0:T(8,128)(2,1)S(1)} %relay_1.3), channel_id=1, source_target_pairs={{1,2},{5,6},{9,10},{13,14},{17,18},{21,22},{25,26},{29,30}} | collective-permute-start | bytes 393224 | tf_op jit(solution)/shard_map/ppermute | solution.py:432
  60.5 0.7 collective-permute-start.10
  61.2 1.3 %collective-permute-start.9 = (bf16[4,128,128]{2,1,0:T(8,128)(2,1)S(1)}, bf16[4,128,128]{2,1,0:T(8,128)(2,1)S(1)}, u32[]{:S(2)}, u32[]{:S(2)}) collective-permute-start(bf16[4,128,128]{2,1,0:T(8,128)(2,1)S(1)} %relay_1.2), channel_id=1, source_target_pairs={{1,2},{5,6},{9,10},{13,14},{17,18},{21,22},{25,26},{29,30}} | collective-permute-start | bytes 393224 | tf_op jit(solution)/shard_map/ppermute | solution.py:432
  62.5 2.8 %collective-permute-done.19 = bf16[4,128,128]{2,1,0:T(8,128)(2,1)S(1)} collective-permute-done((bf16[4,128,128]{2,1,0:T(8,128)(2,1)S(1)}, bf16[4,128,128]{2,1,0:T(8,128)(2,1)S(1)}, u32[]{:S(2)}, u32[]{:S(2)}) %collective-permute-start.19) | collective-permute-done | bytes 131104 | tf_op jit(solution)/shard_map/ppermute | solution.py:432
  65.3 0.4 seeds_0.1
  65.7 3.0 %collective-permute-start.21 = (bf16[4,128,128]{2,1,0:T(8,128)(2,1)S(1)}, bf16[4,128,128]{2,1,0:T(8,128)(2,1)S(1)}, u32[]{:S(2)}, u32[]{:S(2)}) collective-permute-start(bf16[4,128,128]{2,1,0:T(8,128)(2,1)S(1)} %get-tuple-element.116), channel_id=1, source_target_pairs={{0,16},{4,20},{8,24},{12,28},{16,0},{20,4},{24,8},{28,12},{1,17},{... | collective-permute-start | bytes 393224 | tf_op jit(solution)/shard_map/ppermute | solution.py:568
  68.7 0.8 query_parts_0_1.1
  69.5 0.8 query_parts_0_0.1
  70.4 0.4 seeds_1.1
  70.8 0.8 collective-permute-start.11
  71.6 3.7 %collective-permute-done.21.rest_1_ = bf16[4,128,128]{2,1,0:T(8,128)(2,1)S(1)} collective-permute-done((bf16[4,128,128]{2,1,0:T(8,128)(2,1)S(1)}, bf16[4,128,128]{2,1,0:T(8,128)(2,1)S(1)}, u32[]{:S(2)}, u32[]{:S(2)}) %collective-permute-start.21) | collective-permute-done | bytes 131104 | tf_op jit(solution)/shard_map/ppermute | solution.py:568
  75.3 1.4 %span_outputs_0.1 = (bf16[64,1024]{1,0:T(8,128)(2,1)S(1)}, bf16[64,1024]{1,0:T(8,128)(2,1)S(1)}, bf16[64,1024]{1,0:T(8,128)(2,1)S(1)}, bf16[64,1024]{1,0:T(8,128)(2,1)S(1)}) custom-call(bf16[4,128,128]{2,1,0:T(8,128)(2,1)S(1)} %get-tuple-element.115.rest_0_, bf16[4,128,128]{2,1,0:T(8,128)(2,1)S(1)} %collective-permute-done.21.rest_1_, ...), custom_call_target="tpu_custom_call" | custom-call | flops 32000000 | tf_op jit(solution)/shard_map/span_outputs_0/pallas_call | solution.py:631
  76.7 1.3 %collective-permute-start.22 = (bf16[64,1024]{1,0:T(8,128)(2,1)S(1)}, bf16[64,1024]{1,0:T(8,128)(2,1)S(1)}, u32[]{:S(2)}, u32[]{:S(2)}) collective-permute-start(bf16[64,1024]{1,0:T(8,128)(2,1)S(1)} %get-tuple-element.138), channel_id=1, source_target_pairs={{0,4},{4,0},{8,12},{12,8},{16,20},{20,16},{24,28},{28,24},{1,5},{5... | collective-permute-start | bytes 393224 | tf_op jit(solution)/shard_map/ppermute | solution.py:125
  78.0 2.2 %collective-permute-start.23 = (bf16[64,1024]{1,0:T(8,128)(2,1)S(1)}, bf16[64,1024]{1,0:T(8,128)(2,1)S(1)}, u32[]{:S(2)}, u32[]{:S(2)}) collective-permute-start(bf16[64,1024]{1,0:T(8,128)(2,1)S(1)} %get-tuple-element.139), channel_id=1, source_target_pairs={{0,8},{4,12},{8,0},{12,4},{16,24},{20,28},{24,16},{28,20},{1,9},{5... | collective-permute-start | bytes 393224 | tf_op jit(solution)/shard_map/ppermute | solution.py:125
  80.3 1.4 %span_outputs_1.1 = (bf16[64,1024]{1,0:T(8,128)(2,1)S(1)}, bf16[64,1024]{1,0:T(8,128)(2,1)S(1)}, bf16[64,1024]{1,0:T(8,128)(2,1)S(1)}, bf16[64,1024]{1,0:T(8,128)(2,1)S(1)}) custom-call(bf16[4,128,128]{2,1,0:T(8,128)(2,1)S(1)} %get-tuple-element.98.rest_0_, bf16[4,128,128]{2,1,0:T(8,128)(2,1)S(1)} %collective-permute-done.11.rest_1_, ...), custom_call_target="tpu_custom_call" | custom-call | flops 32000000 | tf_op jit(solution)/shard_map/span_outputs_1/pallas_call | solution.py:631
  81.7 1.5 %collective-permute-start.12 = (bf16[64,1024]{1,0:T(8,128)(2,1)S(1)}, bf16[64,1024]{1,0:T(8,128)(2,1)S(1)}, u32[]{:S(2)}, u32[]{:S(2)}) collective-permute-start(bf16[64,1024]{1,0:T(8,128)(2,1)S(1)} %get-tuple-element.107), channel_id=1, source_target_pairs={{0,4},{4,0},{8,12},{12,8},{16,20},{20,16},{24,28},{28,24},{1,5},{5... | collective-permute-start | bytes 393224 | tf_op jit(solution)/shard_map/ppermute | solution.py:125
  83.2 2.0 %collective-permute-start.13 = (bf16[64,1024]{1,0:T(8,128)(2,1)S(1)}, bf16[64,1024]{1,0:T(8,128)(2,1)S(1)}, u32[]{:S(2)}, u32[]{:S(2)}) collective-permute-start(bf16[64,1024]{1,0:T(8,128)(2,1)S(1)} %get-tuple-element.108), channel_id=1, source_target_pairs={{0,8},{4,12},{8,0},{12,4},{16,24},{20,28},{24,16},{28,20},{1,9},{5... | collective-permute-start | bytes 393224 | tf_op jit(solution)/shard_map/ppermute | solution.py:125
  85.3 2.2 %collective-permute-done.24.rest_3_ = bf16[64,1024]{1,0:T(8,128)(2,1)S(1)} collective-permute-done((bf16[64,1024]{1,0:T(8,128)(2,1)S(1)}, bf16[64,1024]{1,0:T(8,128)(2,1)S(1)}, u32[]{:S(2)}, u32[]{:S(2)}) %collective-permute-start.24) | collective-permute-done | bytes 131104 | tf_op jit(solution)/shard_map/ppermute | solution.py:125
  87.6 1.2 %finish_0.1.rest_6_ = bf16[2,64,4096]{2,1,0:T(8,128)(2,1)} custom-call(bf16[64,1024]{1,0:T(8,128)(2,1)S(1)} %get-tuple-element.137.rest_0_, bf16[64,1024]{1,0:T(8,128)(2,1)S(1)} %collective-permute-done.22.rest_1_, bf16[64,1024]{1,0:T(8,128)(2,1)S(1)} %collective-permute-done.23.rest_2_, bf16[64,1024]{1,0:T(8,128)(2,1)S(1)} %collective-permute-done.24.rest_3_, ...), custom_call_target="tpu_custom_call" | custom-call | tf_op jit(solution)/shard_map/finish_0/pallas_call | solution.py:686
  88.9 2.3 %collective-permute-done.14.rest_3_ = bf16[64,1024]{1,0:T(8,128)(2,1)S(1)} collective-permute-done((bf16[64,1024]{1,0:T(8,128)(2,1)S(1)}, bf16[64,1024]{1,0:T(8,128)(2,1)S(1)}, u32[]{:S(2)}, u32[]{:S(2)}) %collective-permute-start.14) | collective-permute-done | bytes 131104 | tf_op jit(solution)/shard_map/ppermute | solution.py:125
  91.1 1.2 %finish_1.1 = bf16[2,64,4096]{2,1,0:T(8,128)(2,1)} custom-call(bf16[64,1024]{1,0:T(8,128)(2,1)S(1)} %get-tuple-element.106.rest_0_, bf16[64,1024]{1,0:T(8,128)(2,1)S(1)} %collective-permute-done.12.rest_1_, bf16[64,1024]{1,0:T(8,128)(2,1)S(1)} %collective-permute-done.13.rest_2_, ...), custom_call_target="tpu_custom_call", output_to_operand_aliasing={{}: (6, {})} | custom-call | tf_op jit(solution)/shard_map/finish_1/pallas_call | solution.py:686
  (51 shorter events, 0.7 us)
Async XLA Ops:
  0.0 13.7 %copy-start.3 = (bf16[2,64,4096]{2,1,0:T(8,128)(2,1)S(1)}, bf16[2,64,4096]{2,1,0:T(8,128)(2,1)}, u32[]{:S(2)}) copy-start(bf16[2,64,4096]{2,1,0:T(8,128)(2,1)} %key_ref.3) | copy-start | bytes 3145732
  0.0 13.7 %copy-start.4 = (bf16[2,64,4096]{2,1,0:T(8,128)(2,1)S(1)}, bf16[2,64,4096]{2,1,0:T(8,128)(2,1)}, u32[]{:S(2)}) copy-start(bf16[2,64,4096]{2,1,0:T(8,128)(2,1)} %value_ref.3) | copy-start | bytes 3145732
  0.0 13.7 %copy-start.7 = (bf16[2,64,128]{2,1,0:T(8,128)(2,1)S(1)}, bf16[2,64,128]{2,1,0:T(8,128)(2,1)}, u32[]{:S(2)}) copy-start(bf16[2,64,128]{2,1,0:T(8,128)(2,1)} %latent_ref.3) | copy-start | bytes 98308
  0.0 13.7 %copy-start.8 = (bf16[2,64,32]{1,2,0:T(8,128)(2,1)S(1)}, bf16[2,64,32]{1,2,0:T(8,128)(2,1)}, u32[]{:S(2)}) copy-start(bf16[2,64,32]{1,2,0:T(8,128)(2,1)} %param.15) | copy-start | bytes 24580
  2.6 11.1 %collective-permute-start = (bf16[144,1024]{1,0:T(8,128)(2,1)}, bf16[144,1024]{1,0:T(8,128)(2,1)S(1)}, u32[]{:S(2)}, u32[]{:S(2)}) collective-permute-start(bf16[144,1024]{1,0:T(8,128)(2,1)} %get-tuple-element.73), channel_id=1, source_target_pairs={{0,12},{4,8},{8,4},{12,0},{16,28},{20,24},{24,20},{28,16},{1,13},{... | collective-permute-start | bytes 884744 | tf_op jit(solution)/shard_map/ppermute | solution.py:125
  5.2 8.5 %copy-start.12 = (s32[2,64]{1,0:T(2,128)S(1)}, s32[2,64]{1,0:T(2,128)}, u32[]{:S(2)}) copy-start(s32[2,64]{1,0:T(2,128)} %kind_ref.3) | copy-start | bytes 1540
  5.2 8.5 %copy-start.11 = (s32[2,64]{1,0:T(2,128)S(1)}, s32[2,64]{1,0:T(2,128)}, u32[]{:S(2)}) copy-start(s32[2,64]{1,0:T(2,128)} %mark_ref.3) | copy-start | bytes 1540
  5.2 14.9 %collective-permute-start.15 = (bf16[144,1024]{1,0:T(8,128)(2,1)}, bf16[144,1024]{1,0:T(8,128)(2,1)S(1)}, u32[]{:S(2)}, u32[]{:S(2)}) collective-permute-start(bf16[144,1024]{1,0:T(8,128)(2,1)} %get-tuple-element.111), channel_id=1, source_target_pairs={{0,4},{4,0},{8,12},{12,8},{16,20},{20,16},{24,28},{28,24},{1,5},{5... | collective-permute-start | bytes 884744 | tf_op jit(solution)/shard_map/ppermute | solution.py:125
  5.7 14.4 %copy-start = (bf16[128,4096]{1,0:T(8,128)(2,1)S(1)}, bf16[128,4096]{1,0:T(8,128)(2,1)}, u32[]{:S(2)}) copy-start(bf16[128,4096]{1,0:T(8,128)(2,1)} %rest_8_.7) | copy-start | bytes 3145732
  5.7 14.4 %copy-start.1 = (bf16[144,1024]{1,0:T(8,128)(2,1)S(1)}, bf16[144,1024]{1,0:T(8,128)(2,1)}, u32[]{:S(2)}) copy-start(bf16[144,1024]{1,0:T(8,128)(2,1)} %get-tuple-element.110.rest_0_.rest_4_) | copy-start | bytes 884740
  5.7 14.4 %copy-start.6 = (f32[2,4096]{1,0:T(2,128)S(1)}, f32[2,4096]{1,0:T(2,128)}, u32[]{:S(2)}) copy-start(f32[2,4096]{1,0:T(2,128)} %rest_9_.7) | copy-start | bytes 98308
  5.7 14.4 %collective-permute-start.16 = (bf16[144,1024]{1,0:T(8,128)(2,1)}, bf16[144,1024]{1,0:T(8,128)(2,1)S(1)}, u32[]{:S(2)}, u32[]{:S(2)}) collective-permute-start(bf16[144,1024]{1,0:T(8,128)(2,1)} %get-tuple-element.112), channel_id=1, source_target_pairs={{0,8},{4,12},{8,0},{12,4},{16,24},{20,28},{24,16},{28,20},{1,9},{5... | collective-permute-start | bytes 884744 | tf_op jit(solution)/shard_map/ppermute | solution.py:125
  14.3 14.1 %collective-permute-start.3 = (bf16[144,1024]{1,0:T(8,128)(2,1)S(1)}, bf16[144,1024]{1,0:T(8,128)(2,1)S(1)}, u32[]{:S(2)}, u32[]{:S(2)}) collective-permute-start(bf16[144,1024]{1,0:T(8,128)(2,1)S(1)} %get-tuple-element.77), channel_id=1, source_target_pairs={{0,12},{4,8},{8,4},{12,0},{16,28},{20,24},{24,20},{28,16},{1,13},{... | collective-permute-start | bytes 884744 | tf_op jit(solution)/shard_map/ppermute | solution.py:125
  16.8 19.8 %collective-permute-start.1 = (bf16[144,1024]{1,0:T(8,128)(2,1)S(1)}, bf16[144,1024]{1,0:T(8,128)(2,1)S(1)}, u32[]{:S(2)}, u32[]{:S(2)}) collective-permute-start(bf16[144,1024]{1,0:T(8,128)(2,1)S(1)} %get-tuple-element.75), channel_id=1, source_target_pairs={{0,4},{4,0},{8,12},{12,8},{16,20},{20,16},{24,28},{28,24},{1,5},{5... | collective-permute-start | bytes 884744 | tf_op jit(solution)/shard_map/ppermute | solution.py:125
  17.4 20.1 %collective-permute-start.2 = (bf16[144,1024]{1,0:T(8,128)(2,1)S(1)}, bf16[144,1024]{1,0:T(8,128)(2,1)S(1)}, u32[]{:S(2)}, u32[]{:S(2)}) collective-permute-start(bf16[144,1024]{1,0:T(8,128)(2,1)S(1)} %get-tuple-element.76), channel_id=1, source_target_pairs={{0,8},{4,12},{8,0},{12,4},{16,24},{20,28},{24,16},{28,20},{1,9},{5... | collective-permute-start | bytes 884744 | tf_op jit(solution)/shard_map/ppermute | solution.py:125
  20.1 0.7 copy-start.10
  20.8 7.6 %copy-start.5 = (bf16[2,64,4096]{2,1,0:T(8,128)(2,1)S(1)}, bf16[2,64,4096]{2,1,0:T(8,128)(2,1)}, u32[]{:S(2)}) copy-start(bf16[2,64,4096]{2,1,0:T(8,128)(2,1)} %query_ref.1) | copy-start | bytes 3145732
  25.7 22.4 %collective-permute-start.17 = (bf16[4,128,256]{2,1,0:T(8,128)(2,1)S(1)}, bf16[4,128,256]{2,1,0:T(8,128)(2,1)S(1)}, u32[]{:S(2)}, u32[]{:S(2)}) collective-permute-start(bf16[4,128,256]{2,1,0:T(8,128)(2,1)S(1)} %get-tuple-element.114), channel_id=1, source_target_pairs={{0,16},{4,20},{8,24},{12,28},{16,0},{20,4},{24,8},{28,12},{1,17},{... | collective-permute-start | bytes 786440 | tf_op jit(solution)/shard_map/ppermute | solution.py:568
  29.3 25.4 %collective-permute-start.5 = (bf16[128,1024]{1,0:T(8,128)(2,1)}, bf16[128,1024]{1,0:T(8,128)(2,1)S(1)}, u32[]{:S(2)}, u32[]{:S(2)}) collective-permute-start(bf16[128,1024]{1,0:T(8,128)(2,1)} %get-tuple-element.81), channel_id=1, source_target_pairs={{0,4},{4,0},{8,12},{12,8},{16,20},{20,16},{24,28},{28,24},{1,5},{5... | collective-permute-start | bytes 786440 | tf_op jit(solution)/shard_map/ppermute | solution.py:125
  30.9 23.9 %collective-permute-start.6 = (bf16[128,1024]{1,0:T(8,128)(2,1)S(1)}, bf16[128,1024]{1,0:T(8,128)(2,1)S(1)}, u32[]{:S(2)}, u32[]{:S(2)}) collective-permute-start(bf16[128,1024]{1,0:T(8,128)(2,1)S(1)} %get-tuple-element.82), channel_id=1, source_target_pairs={{0,8},{4,12},{8,0},{12,4},{16,24},{20,28},{24,16},{28,20},{1,9},{5... | collective-permute-start | bytes 786440 | tf_op jit(solution)/shard_map/ppermute | solution.py:125
  36.6 18.2 %collective-permute-start.7 = (bf16[128,1024]{1,0:T(8,128)(2,1)S(1)}, bf16[128,1024]{1,0:T(8,128)(2,1)S(1)}, u32[]{:S(2)}, u32[]{:S(2)}) collective-permute-start(bf16[128,1024]{1,0:T(8,128)(2,1)S(1)} %get-tuple-element.83), channel_id=1, source_target_pairs={{0,12},{4,8},{8,4},{12,0},{16,28},{20,24},{24,20},{28,16},{1,13},{... | collective-permute-start | bytes 786440 | tf_op jit(solution)/shard_map/ppermute | solution.py:125
  43.1 13.4 %collective-permute-start.4 = (bf16[4,128,256]{2,1,0:T(8,128)(2,1)}, bf16[4,128,256]{2,1,0:T(8,128)(2,1)S(1)}, u32[]{:S(2)}, u32[]{:S(2)}) collective-permute-start(bf16[4,128,256]{2,1,0:T(8,128)(2,1)} %get-tuple-element.79), channel_id=1, source_target_pairs={{0,16},{4,20},{8,24},{12,28},{16,0},{20,4},{24,8},{28,12},{1,17},{... | collective-permute-start | bytes 786440 | tf_op jit(solution)/shard_map/ppermute | solution.py:568
  48.3 9.8 %collective-permute-start.18 = (bf16[4,128,256]{2,1,0:T(8,128)(2,1)S(1)}, bf16[4,128,256]{2,1,0:T(8,128)(2,1)S(1)}, u32[]{:S(2)}, u32[]{:S(2)}) collective-permute-start(bf16[4,128,256]{2,1,0:T(8,128)(2,1)S(1)} %compose_0.1.whole_ref), channel_id=1, source_target_pairs={{0,1},{2,3},{4,5},{6,7},{8,9},{10,11},{12,13},{14,15},{16,17},{18,... | collective-permute-start | bytes 786440 | tf_op jit(solution)/shard_map/ppermute | solution.py:432
  56.8 3.5 %collective-permute-start.8 = (bf16[4,128,256]{2,1,0:T(8,128)(2,1)S(1)}, bf16[4,128,256]{2,1,0:T(8,128)(2,1)S(1)}, u32[]{:S(2)}, u32[]{:S(2)}) collective-permute-start(bf16[4,128,256]{2,1,0:T(8,128)(2,1)S(1)} %compose_1.1.whole_ref), channel_id=1, source_target_pairs={{0,1},{2,3},{4,5},{6,7},{8,9},{10,11},{12,13},{14,15},{16,17},{18,... | collective-permute-start | bytes 786440 | tf_op jit(solution)/shard_map/ppermute | solution.py:432
  58.3 4.2 %collective-permute-start.20 = (bf16[4,128,128]{2,1,0:T(8,128)(2,1)S(1)}, bf16[4,128,128]{2,1,0:T(8,128)(2,1)S(1)}, u32[]{:S(2)}, u32[]{:S(2)}) collective-permute-start(bf16[4,128,128]{2,1,0:T(8,128)(2,1)S(1)} %relay_1.3), channel_id=1, source_target_pairs={{1,3},{5,7},{9,11},{13,15},{17,19},{21,23},{25,27},{29,31}} | collective-permute-start | bytes 393224 | tf_op jit(solution)/shard_map/ppermute | solution.py:432
  59.0 6.3 %collective-permute-start.19 = (bf16[4,128,128]{2,1,0:T(8,128)(2,1)S(1)}, bf16[4,128,128]{2,1,0:T(8,128)(2,1)S(1)}, u32[]{:S(2)}, u32[]{:S(2)}) collective-permute-start(bf16[4,128,128]{2,1,0:T(8,128)(2,1)S(1)} %relay_1.3), channel_id=1, source_target_pairs={{1,2},{5,6},{9,10},{13,14},{17,18},{21,22},{25,26},{29,30}} | collective-permute-start | bytes 393224 | tf_op jit(solution)/shard_map/ppermute | solution.py:432
  60.5 9.8 %collective-permute-start.10 = (bf16[4,128,128]{2,1,0:T(8,128)(2,1)S(1)}, bf16[4,128,128]{2,1,0:T(8,128)(2,1)S(1)}, u32[]{:S(2)}, u32[]{:S(2)}) collective-permute-start(bf16[4,128,128]{2,1,0:T(8,128)(2,1)S(1)} %relay_1.2), channel_id=1, source_target_pairs={{1,3},{5,7},{9,11},{13,15},{17,19},{21,23},{25,27},{29,31}} | collective-permute-start | bytes 393224 | tf_op jit(solution)/shard_map/ppermute | solution.py:432
  61.2 9.2 %collective-permute-start.9 = (bf16[4,128,128]{2,1,0:T(8,128)(2,1)S(1)}, bf16[4,128,128]{2,1,0:T(8,128)(2,1)S(1)}, u32[]{:S(2)}, u32[]{:S(2)}) collective-permute-start(bf16[4,128,128]{2,1,0:T(8,128)(2,1)S(1)} %relay_1.2), channel_id=1, source_target_pairs={{1,2},{5,6},{9,10},{13,14},{17,18},{21,22},{25,26},{29,30}} | collective-permute-start | bytes 393224 | tf_op jit(solution)/shard_map/ppermute | solution.py:432
  65.7 9.6 %collective-permute-start.21 = (bf16[4,128,128]{2,1,0:T(8,128)(2,1)S(1)}, bf16[4,128,128]{2,1,0:T(8,128)(2,1)S(1)}, u32[]{:S(2)}, u32[]{:S(2)}) collective-permute-start(bf16[4,128,128]{2,1,0:T(8,128)(2,1)S(1)} %get-tuple-element.116), channel_id=1, source_target_pairs={{0,16},{4,20},{8,24},{12,28},{16,0},{20,4},{24,8},{28,12},{1,17},{... | collective-permute-start | bytes 393224 | tf_op jit(solution)/shard_map/ppermute | solution.py:568
  70.8 9.5 %collective-permute-start.11 = (bf16[4,128,128]{2,1,0:T(8,128)(2,1)S(1)}, bf16[4,128,128]{2,1,0:T(8,128)(2,1)S(1)}, u32[]{:S(2)}, u32[]{:S(2)}) collective-permute-start(bf16[4,128,128]{2,1,0:T(8,128)(2,1)S(1)} %get-tuple-element.99), channel_id=1, source_target_pairs={{0,16},{4,20},{8,24},{12,28},{16,0},{20,4},{24,8},{28,12},{1,17},{... | collective-permute-start | bytes 393224 | tf_op jit(solution)/shard_map/ppermute | solution.py:568
  76.7 8.5 %collective-permute-start.22 = (bf16[64,1024]{1,0:T(8,128)(2,1)S(1)}, bf16[64,1024]{1,0:T(8,128)(2,1)S(1)}, u32[]{:S(2)}, u32[]{:S(2)}) collective-permute-start(bf16[64,1024]{1,0:T(8,128)(2,1)S(1)} %get-tuple-element.138), channel_id=1, source_target_pairs={{0,4},{4,0},{8,12},{12,8},{16,20},{20,16},{24,28},{28,24},{1,5},{5... | collective-permute-start | bytes 393224 | tf_op jit(solution)/shard_map/ppermute | solution.py:125
  78.0 7.3 %collective-permute-start.23 = (bf16[64,1024]{1,0:T(8,128)(2,1)S(1)}, bf16[64,1024]{1,0:T(8,128)(2,1)S(1)}, u32[]{:S(2)}, u32[]{:S(2)}) collective-permute-start(bf16[64,1024]{1,0:T(8,128)(2,1)S(1)} %get-tuple-element.139), channel_id=1, source_target_pairs={{0,8},{4,12},{8,0},{12,4},{16,24},{20,28},{24,16},{28,20},{1,9},{5... | collective-permute-start | bytes 393224 | tf_op jit(solution)/shard_map/ppermute | solution.py:125
  80.3 7.3 %collective-permute-start.24 = (bf16[64,1024]{1,0:T(8,128)(2,1)S(1)}, bf16[64,1024]{1,0:T(8,128)(2,1)S(1)}, u32[]{:S(2)}, u32[]{:S(2)}) collective-permute-start(bf16[64,1024]{1,0:T(8,128)(2,1)S(1)} %get-tuple-element.140), channel_id=1, source_target_pairs={{0,12},{4,8},{8,4},{12,0},{16,28},{20,24},{24,20},{28,16},{1,13},{... | collective-permute-start | bytes 393224 | tf_op jit(solution)/shard_map/ppermute | solution.py:125
  80.3 7.3 %copy-start.2 = (bf16[2,64,4096]{2,1,0:T(8,128)(2,1)S(1)}, bf16[2,64,4096]{2,1,0:T(8,128)(2,1)}, u32[]{:S(2)}) copy-start(bf16[2,64,4096]{2,1,0:T(8,128)(2,1)} %rest_4_.3) | copy-start | bytes 3145732
  80.3 7.3 %copy-start.9 = (f32[4096]{0:T(1024)S(1)}, f32[4096]{0:T(1024)}, u32[]{:S(2)}) copy-start(f32[4096]{0:T(1024)} %param.23) | copy-start | bytes 49156
  81.7 7.1 %collective-permute-start.12 = (bf16[64,1024]{1,0:T(8,128)(2,1)S(1)}, bf16[64,1024]{1,0:T(8,128)(2,1)S(1)}, u32[]{:S(2)}, u32[]{:S(2)}) collective-permute-start(bf16[64,1024]{1,0:T(8,128)(2,1)S(1)} %get-tuple-element.107), channel_id=1, source_target_pairs={{0,4},{4,0},{8,12},{12,8},{16,20},{20,16},{24,28},{28,24},{1,5},{5... | collective-permute-start | bytes 393224 | tf_op jit(solution)/shard_map/ppermute | solution.py:125
  83.2 5.6 %collective-permute-start.13 = (bf16[64,1024]{1,0:T(8,128)(2,1)S(1)}, bf16[64,1024]{1,0:T(8,128)(2,1)S(1)}, u32[]{:S(2)}, u32[]{:S(2)}) collective-permute-start(bf16[64,1024]{1,0:T(8,128)(2,1)S(1)} %get-tuple-element.108), channel_id=1, source_target_pairs={{0,8},{4,12},{8,0},{12,4},{16,24},{20,28},{24,16},{28,20},{1,9},{5... | collective-permute-start | bytes 393224 | tf_op jit(solution)/shard_map/ppermute | solution.py:125
  85.3 5.9 %collective-permute-start.14 = (bf16[64,1024]{1,0:T(8,128)(2,1)S(1)}, bf16[64,1024]{1,0:T(8,128)(2,1)S(1)}, u32[]{:S(2)}, u32[]{:S(2)}) collective-permute-start(bf16[64,1024]{1,0:T(8,128)(2,1)S(1)} %get-tuple-element.109), channel_id=1, source_target_pairs={{0,12},{4,8},{8,4},{12,0},{16,28},{20,24},{24,20},{28,16},{1,13},{... | collective-permute-start | bytes 393224 | tf_op jit(solution)/shard_map/ppermute | solution.py:125

commit v4 on v3

--- a/solution.py
+++ b/solution.py
@@ -51,14 +51,14 @@
 NT = ((1,), (1,))
 
 
-def pack_kv_kernel(sub, outer, batches, heads, first, extras, key_ref, value_ref, latent_ref, beta_ref, mark_ref, kind_ref, *rest):
-    outs, (latent, beta, mark, kind, wide, sem, small_sem) = rest[-sub - 7 : -7], rest[-7:]
+def pack_kv_kernel(sub, ways, outer, batches, heads, first, extras, key_ref, value_ref, latent_ref, beta_ref, mark_ref, kind_ref, *rest):
+    outs, (latent, beta, mark, kind, wide, sem, small_sem) = rest[-len(ways) - 7 : -7], rest[-7:]
     lo = lax.rem(lax.axis_index("head"), sub)
     hi = lax.div(lax.axis_index("head"), sub)
     rows, width = key_ref.shape[1], outs[0].shape[1]
     part = heads // outer * DK
     copies = []
-    for k in range(sub):
+    for place_out, k in enumerate(ways):
         for j in range(width // part):
             col = pl.multiple_of(((lo ^ k) * outer + (hi ^ ((first + j) % outer))) * part, part)
             for n, batch in enumerate(batches):
@@ -66,8 +66,8 @@
                     copies.append(
                         pltpu.make_async_copy(
                             ref.at[batch, :, pl.ds(col, part)],
-                            outs[k].at[pl.ds((2 * n + i) * rows, rows), pl.ds(j * part, part)],
-                            sem.at[k, j, 2 * n + i],
+                            outs[place_out].at[pl.ds((2 * n + i) * rows, rows), pl.ds(j * part, part)],
+                            sem.at[place_out, j, 2 * n + i],
                         )
                     )
                     copies[-1].start()
@@ -87,7 +87,7 @@
         misc = misc_rows(heads)
         wide[...] = beta[...].astype(f32)
         tokens = jnp.concatenate([mark[batch : batch + 1].astype(f32), kind[batch : batch + 1].astype(f32)], axis=0)
-        for k in range(sub):
+        for place_out, k in enumerate(ways):
             own = wide[pl.ds(pl.multiple_of((lo ^ k) * heads, heads), heads), :]
             values = jnp.concatenate([own, tokens, jnp.zeros((misc - heads - 2, rows), f32)], axis=0)
             values = jnp.concatenate([values, jnp.zeros((misc, 128 - rows), f32)], axis=1).astype(bf16)
@@ -96,7 +96,7 @@
             chunks += [jnp.zeros((16, 128), bf16)] * (-len(chunks) % lanes)
             for c, chunk in enumerate(chunks):
                 at = 2 * rows + 16 * (c // lanes)
-                outs[k][at : at + 16, (c % lanes) * 128 : (c % lanes + 1) * 128] = chunk
+                outs[place_out][at : at + 16, (c % lanes) * 128 : (c % lanes + 1) * 128] = chunk
     for c in copies:
         c.wait()
 
@@ -371,13 +371,13 @@
         rows_ref[i, n] = (grown[i, n] * alive_ref[n] - both[:, DK:]).astype(bf16)
 
 
-def output_kernel(sub, outer, sets, blocks, heads, tok, *rest):
+def output_kernel(sub, outer, sets, blocks, heads, tok, slots, *rest):
     seeds, rest = rest[:outer], rest[outer:]
-    outs = rest[-sub:]
+    per = BLOCK // tok
+    outs = rest[-len(slots) * per :]
     lo = lax.rem(lax.axis_index("head"), sub)
     hi = lax.div(lax.axis_index("head"), sub)
     share = heads // outer
-    per = BLOCK // tok
     for part, (first, shares) in enumerate(sets):
         base_ref, rows_ref, opre_ref, mpre_ref = rest[4 * part : 4 * part + 4]
         for r in range(shares * share):
@@ -388,11 +388,11 @@
                 (opre_ref[r, n] + dot(mpre_ref[r, n], seed)).astype(bf16) for n in range(blocks - 1)
             ]
             states = reorder(states, lax.div(lo, per), blocks.bit_length() - 1)
-            for n in range(blocks):
+            for m, n in enumerate(slots):
                 core = (base_ref[r, n] + dot(rows_ref[r, n], states[n])).astype(bf16)
                 rows = reorder([core[t * tok : (t + 1) * tok] for t in range(per)], lax.rem(lo, per), per.bit_length() - 1)
                 for t in range(per):
-                    outs[n * per + t][:, at] = rows[t]
+                    outs[m * per + t][:, at] = rows[t]
 
 
 def finish_kernel(sub, heads, *rest):
@@ -494,26 +494,26 @@
     sets = ([(1, outer - 1)] if outer > 1 else []) + [(0, 1)]
     misc = tok // 16 + misc_rows(heads) // 16
 
-    def pack_kv(of, first, shares, extras, *after):
+    def pack_kv(of, first, shares, extras, ways, direct, *after):
         lanes = shares * share
         rows = 2 * tok * len(of) + (16 * -(-misc // lanes) if extras else 0)
         return pl.pallas_call(
-            functools.partial(pack_kv_kernel, sub, outer, of, heads, first, extras),
-            out_shape=[sds((rows, lanes * DK), bf16)] * sub,
+            functools.partial(pack_kv_kernel, sub, ways, outer, of, heads, first, extras),
+            out_shape=[sds((rows, lanes * DK), bf16)] * len(ways),
             in_specs=[ANY] * (6 + len(after)),
-            out_specs=[VMEM] * sub,
+            out_specs=[VMEM] * len(ways),
             scratch_shapes=[
                 pltpu.VMEM(gate_latent.shape[1:], bf16),
                 pltpu.VMEM(by_head_t.shape[1:], bf16),
                 pltpu.VMEM(boundary.shape, jnp.int32),
                 pltpu.VMEM(modality.shape, jnp.int32),
                 pltpu.VMEM(by_head_t.shape[1:], f32),
-                pltpu.SemaphoreType.DMA((sub, shares, 2 * len(of))),
+                pltpu.SemaphoreType.DMA((len(ways), shares, 2 * len(of))),
                 pltpu.SemaphoreType.DMA((4,)),
             ],
-            compiler_params=params(16 if after else 60),
+            compiler_params=params(60 if direct else 16),
             cost_estimate=cost(0, 0),
-            name=f"pack_kv_{of[0]}_{first}",
+            name=f"pack_kv_{of[0]}_{ways[0]}",
         )(key_rows, value_rows, gate_latent, by_head_t, boundary, modality, *after)
 
     hp = min(share, max(1, 8 // blocks))
@@ -628,15 +628,27 @@
         operands = []
         for made, here in zip(queries, local[b]):
             operands += [*made, *here[4:6]]
-        return pl.pallas_call(
-            functools.partial(output_kernel, sub, outer, sets, blocks, heads, tok),
-            out_shape=[sds((tok, width), bf16)] * sub,
-            in_specs=[VMEM] * (len(operands) + outer),
-            out_specs=[VMEM] * sub,
-            compiler_params=params(),
-            cost_estimate=cost(SCALE * heads * blocks * 2e7, 0),
-            name=f"span_outputs_{b}",
-        )(*given, *operands)
+        pieces = {}
+        per = sub // blocks
+        near = (blocks + 1) // 2
+        after = []
+        for slots in (list(range(near, blocks)), list(range(near))):
+            if not slots:
+                continue
+            made = pl.pallas_call(
+                functools.partial(output_kernel, sub, outer, sets, blocks, heads, tok, slots),
+                out_shape=[sds((tok, width), bf16)] * (len(slots) * per),
+                in_specs=[VMEM] * (len(operands) + outer) + [ANY] * len(after),
+                out_specs=[VMEM] * (len(slots) * per),
+                compiler_params=params(),
+                cost_estimate=cost(SCALE * heads * len(slots) * 2e7, 0),
+                name=f"span_outputs_{b}_{slots[0]}",
+            )(*given, *operands, *after)
+            after = [made[0]]
+            for m, n in enumerate(slots):
+                for t in range(per):
+                    pieces[n * per + t] = made[m * per + t]
+        return [pieces[k] for k in range(sub)]
 
     def swapped(made):
         sent = []
@@ -653,7 +665,11 @@
     token = None
     kv = []
     for b in range(batches):
-        packed = pack_kv([b], sets[0][0], outer, True, *([] if token is None else [token]))
+        if b == 0:
+            far = pack_kv([b], sets[0][0], outer, True, [sub - 1], True)
+            packed = pack_kv([b], sets[0][0], outer, True, list(range(sub - 1)), True, far[0]) + far if sub > 1 else far
+        else:
+            packed = pack_kv([b], sets[0][0], outer, True, list(range(sub)), False, token)
         kv.append(exchange(packed))
         token = kv[b][-1]
     packed_q = pack_q(token)

time: 93.4 us -> 90.9 us (0.973)
  waiting for transfers between devices: 21.8 us -> 20.5 us
    pallas_call x2 -> x3, Pallas kernels: 3.08 us -> 4.5 us  [pack_kv(): pl.pallas_call(functools.partial(pack_kv_kernel, sub, ways, outer, of, he...]
    ppermute x15, waiting for transfers between devices: 15.3 us -> 14 us  [exchange(): lax.ppermute(pieces[k], 'head', [(i, i ^ k) for i in range(count)])]
    pallas_call x2 -> x4, Pallas kernels: 2.8 us -> 1.64 us  [outputs(): pl.pallas_call(functools.partial(output_kernel, sub, outer, sets, blocks,...]
  transfers between devices with their start and end apart: 25 -> 25, of which waited for: 8 -> 8; matrix products, arithmetic and copies ran while one was open for 0% -> 0% of each run, Pallas kernels for 33% -> 35%
where the time goes in v4:
time: 90.9 us; the launch traced here: 89.7 us
  Pallas kernels  34.2 us (38%)
  starting transfers between devices  33.8 us (37%)
  waiting for transfers between devices  20.5 us (23%)
    ppermute x15, starting transfers between devices, exchange(): lax.ppermute(pieces[k], 'head', [(i, i ^ k) for i in range(count)])  20.6 us
    pallas_call x4, Pallas kernels, state_maps(): pl.pallas_call(functools.partial(state_kernel, sub, outer, first, lane, b...  20.3 us
    ppermute x15, waiting for transfers between devices, exchange(): lax.ppermute(pieces[k], 'head', [(i, i ^ k) for i in range(count)])  14 us
    ppermute x6, starting transfers between devices, before(): part = lax.ppermute(payload, 'seq', pairs)  6.71 us
    ppermute x4, starting transfers between devices, swap(): lax.ppermute(parts[j], 'head', [(i, i ^ j * sub) for i in range(count)])  6.5 us
    pallas_call x3, Pallas kernels, pack_kv(): pl.pallas_call(functools.partial(pack_kv_kernel, sub, ways, outer, of, he...  4.5 us
    ppermute x4, waiting for transfers between devices, swap(): lax.ppermute(parts[j], 'head', [(i, i ^ j * sub) for i in range(count)])  3.7 us
    pallas_call x4, Pallas kernels, query_parts(): pl.pallas_call(functools.partial(query_kernel, sub, outer, first, blocks,...  3.29 us
  transfers between devices with their start and end apart: 25, of which 8 were waited for; matrix products, arithmetic and copies ran while one was open for 0% of the time, Pallas kernels for 35%

profile of v4, /device:TPU:2, one launch (start us, length us, event | category | flops | bytes accessed | tf_op | source)
XLA Modules:
  0.0 89.7 jit_solution(15756917364069587749)
XLA Ops:
  0.0 1.8 %pack_kv_0_3.1.rest_0_ = bf16[144,1024]{1,0:T(8,128)(2,1)} custom-call(bf16[2,64,4096]{2,1,0:T(8,128)(2,1)} %key_ref.5, bf16[2,64,4096]{2,1,0:T(8,128)(2,1)} %value_ref.5, bf16[2,64,128]{2,1,0:T(8,128)(2,1)} %latent_ref.5, bf16[2,32,64]{2,1,0:T(8,128)(2,1)} %bitcast.2, s32[2,64]{1,0:T(2,128)} %mark_ref.5, s32[2,64]{1,0:T(2,128)} %kind_ref.5), custom_call_target="tpu_custom_call" | custom-call | tf_op jit(solution)/shard_map/pack_kv_0_3/pallas_call | solution.py:500
  1.8 2.6 %collective-permute-start = (bf16[144,1024]{1,0:T(8,128)(2,1)}, bf16[144,1024]{1,0:T(8,128)(2,1)S(1)}, u32[]{:S(2)}, u32[]{:S(2)}) collective-permute-start(bf16[144,1024]{1,0:T(8,128)(2,1)} %pack_kv_0_3.1.rest_0_), channel_id=1, source_target_pairs={{0,12},{4,8},{8,4},{12,0},{16,28},{20,24},{24,20},{28,16},{1,13},{... | collective-permute-start | bytes 884744 | tf_op jit(solution)/shard_map/ppermute | solution.py:125
  4.4 2.2 %pack_kv_0_0.1 = (bf16[144,1024]{1,0:T(8,128)(2,1)}, bf16[144,1024]{1,0:T(8,128)(2,1)}, bf16[144,1024]{1,0:T(8,128)(2,1)}) custom-call(bf16[2,64,4096]{2,1,0:T(8,128)(2,1)} %key_ref.5, bf16[2,64,4096]{2,1,0:T(8,128)(2,1)} %value_ref.5, bf16[2,64,128]{2,1,0:T(8,128)(2,1)} %latent_ref.5, bf16[2,32,64]{2,1,0:T(8,128)(2,1)} %bitcast.3, s32[2,64]{1,0:T(2,128)} %mark_ref.5, ...), custom_call_target="tpu_custom_call" | custom-call | tf_op jit(solution)/shard_map/pack_kv_0_0/pallas_call | solution.py:500
  6.7 0.6 collective-permute-start.15
  7.3 0.6 collective-permute-start.16
  7.9 5.0 %collective-permute-done.rest_0_.rest_3_.rest_7_ = bf16[144,1024]{1,0:T(8,128)(2,1)S(1)} collective-permute-done((bf16[144,1024]{1,0:T(8,128)(2,1)}, bf16[144,1024]{1,0:T(8,128)(2,1)S(1)}, u32[]{:S(2)}, u32[]{:S(2)}) %collective-permute-start) | collective-permute-done | bytes 294944 | tf_op jit(solution)/shard_map/ppermute | solution.py:125
  12.9 0.5 pack_kv_1_0.1
  13.4 2.6 %collective-permute-start.3 = (bf16[144,1024]{1,0:T(8,128)(2,1)S(1)}, bf16[144,1024]{1,0:T(8,128)(2,1)S(1)}, u32[]{:S(2)}, u32[]{:S(2)}) collective-permute-start(bf16[144,1024]{1,0:T(8,128)(2,1)S(1)} %get-tuple-element.75), channel_id=1, source_target_pairs={{0,12},{4,8},{8,4},{12,0},{16,28},{20,24},{24,20},{28,16},{1,13},{... | collective-permute-start | bytes 884744 | tf_op jit(solution)/shard_map/ppermute | solution.py:125
  16.1 0.5 collective-permute-start.1
  17.0 2.3 %collective-permute-done.15.rest_1_.rest_5_ = bf16[144,1024]{1,0:T(8,128)(2,1)S(1)} collective-permute-done((bf16[144,1024]{1,0:T(8,128)(2,1)}, bf16[144,1024]{1,0:T(8,128)(2,1)S(1)}, u32[]{:S(2)}, u32[]{:S(2)}) %collective-permute-start.15) | collective-permute-done | bytes 294944 | tf_op jit(solution)/shard_map/ppermute | solution.py:125
  19.3 0.6 copy-done.12
  20.0 4.9 %state_maps_0_1.1 = (bf16[4,2,128,128]{3,2,1,0:T(8,128)(2,1)S(1)}, f32[4,2,128,128]{3,2,1,0:T(8,128)S(1)}, bf16[4,2,128,256]{3,2,1,0:T(8,128)(2,1)S(1)}, f32[4,2...) custom-call(f32[32]{0:T(128)S(1)} %copy-done.12, ...), custom_call_target="tpu_custom_call" | custom-call | flops 160000000 | tf_op jit(solution)/shard_map/state_maps_0_1/pallas_call | solution.py:548
  24.9 2.7 %collective-permute-start.17 = (bf16[4,128,256]{2,1,0:T(8,128)(2,1)S(1)}, bf16[4,128,256]{2,1,0:T(8,128)(2,1)S(1)}, u32[]{:S(2)}, u32[]{:S(2)}) collective-permute-start(bf16[4,128,256]{2,1,0:T(8,128)(2,1)S(1)} %get-tuple-element.112), channel_id=1, source_target_pairs={{0,16},{4,20},{8,24},{12,28},{16,0},{20,4},{24,8},{28,12},{1,17},{... | collective-permute-start | bytes 786440 | tf_op jit(solution)/shard_map/ppermute | solution.py:568
  27.8 1.6 %collective-permute-start.5 = (bf16[128,1024]{1,0:T(8,128)(2,1)S(1)}, bf16[128,1024]{1,0:T(8,128)(2,1)S(1)}, u32[]{:S(2)}, u32[]{:S(2)}) collective-permute-start(bf16[128,1024]{1,0:T(8,128)(2,1)S(1)} %get-tuple-element.79), channel_id=1, source_target_pairs={{0,4},{4,0},{8,12},{12,8},{16,20},{20,16},{24,28},{28,24},{1,5},{5... | collective-permute-start | bytes 786440 | tf_op jit(solution)/shard_map/ppermute | solution.py:125
  29.4 1.6 %collective-permute-start.6 = (bf16[128,1024]{1,0:T(8,128)(2,1)S(1)}, bf16[128,1024]{1,0:T(8,128)(2,1)S(1)}, u32[]{:S(2)}, u32[]{:S(2)}) collective-permute-start(bf16[128,1024]{1,0:T(8,128)(2,1)S(1)} %get-tuple-element.80), channel_id=1, source_target_pairs={{0,8},{4,12},{8,0},{12,4},{16,24},{20,28},{24,16},{28,20},{1,9},{5... | collective-permute-start | bytes 786440 | tf_op jit(solution)/shard_map/ppermute | solution.py:125
  31.0 2.3 %collective-permute-start.7 = (bf16[128,1024]{1,0:T(8,128)(2,1)S(1)}, bf16[128,1024]{1,0:T(8,128)(2,1)S(1)}, u32[]{:S(2)}, u32[]{:S(2)}) collective-permute-start(bf16[128,1024]{1,0:T(8,128)(2,1)S(1)} %get-tuple-element.81), channel_id=1, source_target_pairs={{0,12},{4,8},{8,4},{12,0},{16,28},{20,24},{24,20},{28,16},{1,13},{... | collective-permute-start | bytes 786440 | tf_op jit(solution)/shard_map/ppermute | solution.py:125
  33.3 3.3 %collective-permute-done.2.rest_2_.rest_6_ = bf16[144,1024]{1,0:T(8,128)(2,1)S(1)} collective-permute-done((bf16[144,1024]{1,0:T(8,128)(2,1)S(1)}, bf16[144,1024]{1,0:T(8,128)(2,1)S(1)}, u32[]{:S(2)}, u32[]{:S(2)}) %collective-permute-start.2) | collective-permute-done | bytes 294944 | tf_op jit(solution)/shard_map/ppermute | solution.py:125
  36.7 5.6 %state_maps_1_1.1 = (bf16[4,2,128,128]{3,2,1,0:T(8,128)(2,1)S(1)}, f32[4,2,128,128]{3,2,1,0:T(8,128)S(1)}, bf16[4,2,128,256]{3,2,1,0:T(8,128)(2,1)S(1)}, f32[4,2...) custom-call(f32[32]{0:T(128)S(1)} %copy-done.12, ...), custom_call_target="tpu_custom_call" | custom-call | flops 160000000 | tf_op jit(solution)/shard_map/state_maps_1_1/pallas_call | solution.py:548
  42.3 4.9 %state_maps_0_0.1 = (bf16[4,2,128,128]{3,2,1,0:T(8,128)(2,1)S(1)}, f32[4,2,128,128]{3,2,1,0:T(8,128)S(1)}, bf16[4,2,128,256]{3,2,1,0:T(8,128)(2,1)S(1)}, f32[4,2...) custom-call(f32[32]{0:T(128)S(1)} %copy-done.12, ...), custom_call_target="tpu_custom_call" | custom-call | flops 160000000 | tf_op jit(solution)/shard_map/state_maps_0_0/pallas_call | solution.py:548
  47.5 1.5 %collective-permute-start.18 = (bf16[4,128,256]{2,1,0:T(8,128)(2,1)S(1)}, bf16[4,128,256]{2,1,0:T(8,128)(2,1)S(1)}, u32[]{:S(2)}, u32[]{:S(2)}) collective-permute-start(bf16[4,128,256]{2,1,0:T(8,128)(2,1)S(1)} %compose_0.1.whole_ref), channel_id=1, source_target_pairs={{0,1},{2,3},{4,5},{6,7},{8,9},{10,11},{12,13},{14,15},{16,17},{18,... | collective-permute-start | bytes 786440 | tf_op jit(solution)/shard_map/ppermute | solution.py:432
  49.0 4.9 %state_maps_1_0.1 = (bf16[4,2,128,128]{3,2,1,0:T(8,128)(2,1)S(1)}, f32[4,2,128,128]{3,2,1,0:T(8,128)S(1)}, bf16[4,2,128,256]{3,2,1,0:T(8,128)(2,1)S(1)}, f32[4,2...) custom-call(f32[32]{0:T(128)S(1)} %copy-done.12, ...), custom_call_target="tpu_custom_call" | custom-call | flops 160000000 | tf_op jit(solution)/shard_map/state_maps_1_0/pallas_call | solution.py:548
  53.9 0.8 query_parts_1_1.1
  54.8 0.8 query_parts_1_0.1
  55.9 1.3 %collective-permute-start.8 = (bf16[4,128,256]{2,1,0:T(8,128)(2,1)S(1)}, bf16[4,128,256]{2,1,0:T(8,128)(2,1)S(1)}, u32[]{:S(2)}, u32[]{:S(2)}) collective-permute-start(bf16[4,128,256]{2,1,0:T(8,128)(2,1)S(1)} %compose_1.1.whole_ref), channel_id=1, source_target_pairs={{0,1},{2,3},{4,5},{6,7},{8,9},{10,11},{12,13},{14,15},{16,17},{18,... | collective-permute-start | bytes 786440 | tf_op jit(solution)/shard_map/ppermute | solution.py:432
  57.4 0.7 collective-permute-start.20
  58.1 1.3 %collective-permute-start.19 = (bf16[4,128,128]{2,1,0:T(8,128)(2,1)S(1)}, bf16[4,128,128]{2,1,0:T(8,128)(2,1)S(1)}, u32[]{:S(2)}, u32[]{:S(2)}) collective-permute-start(bf16[4,128,128]{2,1,0:T(8,128)(2,1)S(1)} %relay_1.3), channel_id=1, source_target_pairs={{1,2},{5,6},{9,10},{13,14},{17,18},{21,22},{25,26},{29,30}} | collective-permute-start | bytes 393224 | tf_op jit(solution)/shard_map/ppermute | solution.py:432
  59.6 0.7 collective-permute-start.10
  60.3 1.3 %collective-permute-start.9 = (bf16[4,128,128]{2,1,0:T(8,128)(2,1)S(1)}, bf16[4,128,128]{2,1,0:T(8,128)(2,1)S(1)}, u32[]{:S(2)}, u32[]{:S(2)}) collective-permute-start(bf16[4,128,128]{2,1,0:T(8,128)(2,1)S(1)} %relay_1.2), channel_id=1, source_target_pairs={{1,2},{5,6},{9,10},{13,14},{17,18},{21,22},{25,26},{29,30}} | collective-permute-start | bytes 393224 | tf_op jit(solution)/shard_map/ppermute | solution.py:432
  61.6 2.8 %collective-permute-done.19 = bf16[4,128,128]{2,1,0:T(8,128)(2,1)S(1)} collective-permute-done((bf16[4,128,128]{2,1,0:T(8,128)(2,1)S(1)}, bf16[4,128,128]{2,1,0:T(8,128)(2,1)S(1)}, u32[]{:S(2)}, u32[]{:S(2)}) %collective-permute-start.19) | collective-permute-done | bytes 131104 | tf_op jit(solution)/shard_map/ppermute | solution.py:432
  64.8 3.0 %collective-permute-start.21 = (bf16[4,128,128]{2,1,0:T(8,128)(2,1)S(1)}, bf16[4,128,128]{2,1,0:T(8,128)(2,1)S(1)}, u32[]{:S(2)}, u32[]{:S(2)}) collective-permute-start(bf16[4,128,128]{2,1,0:T(8,128)(2,1)S(1)} %get-tuple-element.114), channel_id=1, source_target_pairs={{0,16},{4,20},{8,24},{12,28},{16,0},{20,4},{24,8},{28,12},{1,17},{... | collective-permute-start | bytes 393224 | tf_op jit(solution)/shard_map/ppermute | solution.py:568
  67.8 0.8 query_parts_0_1.1
  68.6 0.8 query_parts_0_0.1
  69.9 0.9 collective-permute-start.11
  70.7 3.7 %collective-permute-done.21.rest_1_ = bf16[4,128,128]{2,1,0:T(8,128)(2,1)S(1)} collective-permute-done((bf16[4,128,128]{2,1,0:T(8,128)(2,1)S(1)}, bf16[4,128,128]{2,1,0:T(8,128)(2,1)S(1)}, u32[]{:S(2)}, u32[]{:S(2)}) %collective-permute-start.21) | collective-permute-done | bytes 131104 | tf_op jit(solution)/shard_map/ppermute | solution.py:568
  74.4 0.4 span_outputs_0_1.1
  74.8 0.4 span_outputs_0_0.1
  75.2 1.2 %collective-permute-start.22 = (bf16[64,1024]{1,0:T(8,128)(2,1)S(1)}, bf16[64,1024]{1,0:T(8,128)(2,1)S(1)}, u32[]{:S(2)}, u32[]{:S(2)}) collective-permute-start(bf16[64,1024]{1,0:T(8,128)(2,1)S(1)} %get-tuple-element.137), channel_id=1, source_target_pairs={{0,4},{4,0},{8,12},{12,8},{16,20},{20,16},{24,28},{28,24},{1,5},{5... | collective-permute-start | bytes 393224 | tf_op jit(solution)/shard_map/ppermute | solution.py:125
  76.5 1.2 %collective-permute-start.23 = (bf16[64,1024]{1,0:T(8,128)(2,1)S(1)}, bf16[64,1024]{1,0:T(8,128)(2,1)S(1)}, u32[]{:S(2)}, u32[]{:S(2)}) collective-permute-start(bf16[64,1024]{1,0:T(8,128)(2,1)S(1)} %get-tuple-element.135.rest_10_), channel_id=1, source_target_pairs={{0,8},{4,12},{8,0},{12,4},{16,24},{20,28},{24,16},{28,20},{1,9},{5... | collective-permute-start | bytes 393224 | tf_op jit(solution)/shard_map/ppermute | solution.py:125
  77.6 1.1 %collective-permute-start.24 = (bf16[64,1024]{1,0:T(8,128)(2,1)S(1)}, bf16[64,1024]{1,0:T(8,128)(2,1)S(1)}, u32[]{:S(2)}, u32[]{:S(2)}) collective-permute-start(bf16[64,1024]{1,0:T(8,128)(2,1)S(1)} %get-tuple-element.138), channel_id=1, source_target_pairs={{0,12},{4,8},{8,4},{12,0},{16,28},{20,24},{24,20},{28,16},{1,13},{... | collective-permute-start | bytes 393224 | tf_op jit(solution)/shard_map/ppermute | solution.py:125
  79.2 0.4 span_outputs_1_0.1
  79.7 1.2 %collective-permute-start.12 = (bf16[64,1024]{1,0:T(8,128)(2,1)S(1)}, bf16[64,1024]{1,0:T(8,128)(2,1)S(1)}, u32[]{:S(2)}, u32[]{:S(2)}) collective-permute-start(bf16[64,1024]{1,0:T(8,128)(2,1)S(1)} %get-tuple-element.106), channel_id=1, source_target_pairs={{0,4},{4,0},{8,12},{12,8},{16,20},{20,16},{24,28},{28,24},{1,5},{5... | collective-permute-start | bytes 393224 | tf_op jit(solution)/shard_map/ppermute | solution.py:125
  80.9 1.6 %collective-permute-start.14 = (bf16[64,1024]{1,0:T(8,128)(2,1)S(1)}, bf16[64,1024]{1,0:T(8,128)(2,1)S(1)}, u32[]{:S(2)}, u32[]{:S(2)}) collective-permute-start(bf16[64,1024]{1,0:T(8,128)(2,1)S(1)} %get-tuple-element.107), channel_id=1, source_target_pairs={{0,12},{4,8},{8,4},{12,0},{16,28},{20,24},{24,20},{28,16},{1,13},{... | collective-permute-start | bytes 393224 | tf_op jit(solution)/shard_map/ppermute | solution.py:125
  82.5 1.4 %collective-permute-start.13 = (bf16[64,1024]{1,0:T(8,128)(2,1)S(1)}, bf16[64,1024]{1,0:T(8,128)(2,1)S(1)}, u32[]{:S(2)}, u32[]{:S(2)}) collective-permute-start(bf16[64,1024]{1,0:T(8,128)(2,1)S(1)} %get-tuple-element.104.rest_10_), channel_id=1, source_target_pairs={{0,8},{4,12},{8,0},{12,4},{16,24},{20,28},{24,16},{28,20},{1,9},{5... | collective-permute-start | bytes 393224 | tf_op jit(solution)/shard_map/ppermute | solution.py:125
  83.9 1.1 %collective-permute-done.24.rest_3_ = bf16[64,1024]{1,0:T(8,128)(2,1)S(1)} collective-permute-done((bf16[64,1024]{1,0:T(8,128)(2,1)S(1)}, bf16[64,1024]{1,0:T(8,128)(2,1)S(1)}, u32[]{:S(2)}, u32[]{:S(2)}) %collective-permute-start.24) | collective-permute-done | bytes 131104 | tf_op jit(solution)/shard_map/ppermute | solution.py:125
  85.0 1.2 %finish_0.1.rest_6_ = bf16[2,64,4096]{2,1,0:T(8,128)(2,1)} custom-call(bf16[64,1024]{1,0:T(8,128)(2,1)S(1)} %get-tuple-element.136.rest_0_, bf16[64,1024]{1,0:T(8,128)(2,1)S(1)} %collective-permute-done.22.rest_1_, bf16[64,1024]{1,0:T(8,128)(2,1)S(1)} %collective-permute-done.23.rest_2_, bf16[64,1024]{1,0:T(8,128)(2,1)S(1)} %collective-permute-done.24.rest_3_, ...), custom_call_target="tpu_custom_call" | custom-call | tf_op jit(solution)/shard_map/finish_0/pallas_call | solution.py:702
  86.3 1.6 %collective-permute-done.12.rest_1_ = bf16[64,1024]{1,0:T(8,128)(2,1)S(1)} collective-permute-done((bf16[64,1024]{1,0:T(8,128)(2,1)S(1)}, bf16[64,1024]{1,0:T(8,128)(2,1)S(1)}, u32[]{:S(2)}, u32[]{:S(2)}) %collective-permute-start.12) | collective-permute-done | bytes 131104 | tf_op jit(solution)/shard_map/ppermute | solution.py:125
  87.9 0.6 collective-permute-done.13.rest_2_
  88.5 1.2 %finish_1.1 = bf16[2,64,4096]{2,1,0:T(8,128)(2,1)} custom-call(bf16[64,1024]{1,0:T(8,128)(2,1)S(1)} %get-tuple-element.105.rest_0_, bf16[64,1024]{1,0:T(8,128)(2,1)S(1)} %collective-permute-done.12.rest_1_, bf16[64,1024]{1,0:T(8,128)(2,1)S(1)} %collective-permute-done.13.rest_2_, ...), custom_call_target="tpu_custom_call", output_to_operand_aliasing={{}: (6, {})} | custom-call | tf_op jit(solution)/shard_map/finish_1/pallas_call | solution.py:702
  (54 shorter events, 2.9 us)
Async XLA Ops:
  1.8 11.1 %copy-start.1 = (bf16[2,64,4096]{2,1,0:T(8,128)(2,1)S(1)}, bf16[2,64,4096]{2,1,0:T(8,128)(2,1)}, u32[]{:S(2)}) copy-start(bf16[2,64,4096]{2,1,0:T(8,128)(2,1)} %key_ref.5) | copy-start | bytes 3145732
  1.8 11.1 %copy-start.2 = (bf16[2,64,4096]{2,1,0:T(8,128)(2,1)S(1)}, bf16[2,64,4096]{2,1,0:T(8,128)(2,1)}, u32[]{:S(2)}) copy-start(bf16[2,64,4096]{2,1,0:T(8,128)(2,1)} %value_ref.5) | copy-start | bytes 3145732
  1.8 11.1 %copy-start.7 = (bf16[2,64,128]{2,1,0:T(8,128)(2,1)S(1)}, bf16[2,64,128]{2,1,0:T(8,128)(2,1)}, u32[]{:S(2)}) copy-start(bf16[2,64,128]{2,1,0:T(8,128)(2,1)} %latent_ref.5) | copy-start | bytes 98308
  1.8 11.1 %copy-start.8 = (bf16[2,64,32]{1,2,0:T(8,128)(2,1)S(1)}, bf16[2,64,32]{1,2,0:T(8,128)(2,1)}, u32[]{:S(2)}) copy-start(bf16[2,64,32]{1,2,0:T(8,128)(2,1)} %param.15) | copy-start | bytes 24580
  1.8 11.1 %collective-permute-start = (bf16[144,1024]{1,0:T(8,128)(2,1)}, bf16[144,1024]{1,0:T(8,128)(2,1)S(1)}, u32[]{:S(2)}, u32[]{:S(2)}) collective-permute-start(bf16[144,1024]{1,0:T(8,128)(2,1)} %pack_kv_0_3.1.rest_0_), channel_id=1, source_target_pairs={{0,12},{4,8},{8,4},{12,0},{16,28},{20,24},{24,20},{28,16},{1,13},{... | collective-permute-start | bytes 884744 | tf_op jit(solution)/shard_map/ppermute | solution.py:125
  6.7 6.2 %copy-start.11 = (s32[2,64]{1,0:T(2,128)S(1)}, s32[2,64]{1,0:T(2,128)}, u32[]{:S(2)}) copy-start(s32[2,64]{1,0:T(2,128)} %kind_ref.5) | copy-start | bytes 1540
  6.7 6.2 %copy-start.10 = (s32[2,64]{1,0:T(2,128)S(1)}, s32[2,64]{1,0:T(2,128)}, u32[]{:S(2)}) copy-start(s32[2,64]{1,0:T(2,128)} %mark_ref.5) | copy-start | bytes 1540
  6.7 12.6 %collective-permute-start.15 = (bf16[144,1024]{1,0:T(8,128)(2,1)}, bf16[144,1024]{1,0:T(8,128)(2,1)S(1)}, u32[]{:S(2)}, u32[]{:S(2)}) collective-permute-start(bf16[144,1024]{1,0:T(8,128)(2,1)} %get-tuple-element.109), channel_id=1, source_target_pairs={{0,4},{4,0},{8,12},{12,8},{16,20},{20,16},{24,28},{28,24},{1,5},{5... | collective-permute-start | bytes 884744 | tf_op jit(solution)/shard_map/ppermute | solution.py:125
  7.3 12.1 %copy-start = (bf16[128,4096]{1,0:T(8,128)(2,1)S(1)}, bf16[128,4096]{1,0:T(8,128)(2,1)}, u32[]{:S(2)}) copy-start(bf16[128,4096]{1,0:T(8,128)(2,1)} %rest_8_.7) | copy-start | bytes 3145732
  7.3 12.1 %copy-start.3 = (bf16[144,1024]{1,0:T(8,128)(2,1)S(1)}, bf16[144,1024]{1,0:T(8,128)(2,1)}, u32[]{:S(2)}) copy-start(bf16[144,1024]{1,0:T(8,128)(2,1)} %get-tuple-element.108.rest_0_.rest_4_) | copy-start | bytes 884740
  7.3 12.1 %copy-start.6 = (f32[2,4096]{1,0:T(2,128)S(1)}, f32[2,4096]{1,0:T(2,128)}, u32[]{:S(2)}) copy-start(f32[2,4096]{1,0:T(2,128)} %rest_9_.7) | copy-start | bytes 98308
  7.3 12.0 %collective-permute-start.16 = (bf16[144,1024]{1,0:T(8,128)(2,1)}, bf16[144,1024]{1,0:T(8,128)(2,1)S(1)}, u32[]{:S(2)}, u32[]{:S(2)}) collective-permute-start(bf16[144,1024]{1,0:T(8,128)(2,1)} %get-tuple-element.110), channel_id=1, source_target_pairs={{0,8},{4,12},{8,0},{12,4},{16,24},{20,28},{24,16},{28,20},{1,9},{5... | collective-permute-start | bytes 884744 | tf_op jit(solution)/shard_map/ppermute | solution.py:125
  13.4 14.1 %collective-permute-start.3 = (bf16[144,1024]{1,0:T(8,128)(2,1)S(1)}, bf16[144,1024]{1,0:T(8,128)(2,1)S(1)}, u32[]{:S(2)}, u32[]{:S(2)}) collective-permute-start(bf16[144,1024]{1,0:T(8,128)(2,1)S(1)} %get-tuple-element.75), channel_id=1, source_target_pairs={{0,12},{4,8},{8,4},{12,0},{16,28},{20,24},{24,20},{28,16},{1,13},{... | collective-permute-start | bytes 884744 | tf_op jit(solution)/shard_map/ppermute | solution.py:125
  16.1 14.9 %collective-permute-start.1 = (bf16[144,1024]{1,0:T(8,128)(2,1)S(1)}, bf16[144,1024]{1,0:T(8,128)(2,1)S(1)}, u32[]{:S(2)}, u32[]{:S(2)}) collective-permute-start(bf16[144,1024]{1,0:T(8,128)(2,1)S(1)} %get-tuple-element.73), channel_id=1, source_target_pairs={{0,4},{4,0},{8,12},{12,8},{16,20},{20,16},{24,28},{28,24},{1,5},{5... | collective-permute-start | bytes 884744 | tf_op jit(solution)/shard_map/ppermute | solution.py:125
  16.6 20.1 %collective-permute-start.2 = (bf16[144,1024]{1,0:T(8,128)(2,1)S(1)}, bf16[144,1024]{1,0:T(8,128)(2,1)S(1)}, u32[]{:S(2)}, u32[]{:S(2)}) collective-permute-start(bf16[144,1024]{1,0:T(8,128)(2,1)S(1)} %get-tuple-element.74), channel_id=1, source_target_pairs={{0,8},{4,12},{8,0},{12,4},{16,24},{20,28},{24,16},{28,20},{1,9},{5... | collective-permute-start | bytes 884744 | tf_op jit(solution)/shard_map/ppermute | solution.py:125
  19.3 0.7 copy-start.12
  20.0 7.6 %copy-start.5 = (bf16[2,64,4096]{2,1,0:T(8,128)(2,1)S(1)}, bf16[2,64,4096]{2,1,0:T(8,128)(2,1)}, u32[]{:S(2)}) copy-start(bf16[2,64,4096]{2,1,0:T(8,128)(2,1)} %query_ref.1) | copy-start | bytes 3145732
  24.9 22.3 %collective-permute-start.17 = (bf16[4,128,256]{2,1,0:T(8,128)(2,1)S(1)}, bf16[4,128,256]{2,1,0:T(8,128)(2,1)S(1)}, u32[]{:S(2)}, u32[]{:S(2)}) collective-permute-start(bf16[4,128,256]{2,1,0:T(8,128)(2,1)S(1)} %get-tuple-element.112), channel_id=1, source_target_pairs={{0,16},{4,20},{8,24},{12,28},{16,0},{20,4},{24,8},{28,12},{1,17},{... | collective-permute-start | bytes 786440 | tf_op jit(solution)/shard_map/ppermute | solution.py:568
  27.8 26.1 %collective-permute-start.5 = (bf16[128,1024]{1,0:T(8,128)(2,1)S(1)}, bf16[128,1024]{1,0:T(8,128)(2,1)S(1)}, u32[]{:S(2)}, u32[]{:S(2)}) collective-permute-start(bf16[128,1024]{1,0:T(8,128)(2,1)S(1)} %get-tuple-element.79), channel_id=1, source_target_pairs={{0,4},{4,0},{8,12},{12,8},{16,20},{20,16},{24,28},{28,24},{1,5},{5... | collective-permute-start | bytes 786440 | tf_op jit(solution)/shard_map/ppermute | solution.py:125
  29.4 24.5 %collective-permute-start.6 = (bf16[128,1024]{1,0:T(8,128)(2,1)S(1)}, bf16[128,1024]{1,0:T(8,128)(2,1)S(1)}, u32[]{:S(2)}, u32[]{:S(2)}) collective-permute-start(bf16[128,1024]{1,0:T(8,128)(2,1)S(1)} %get-tuple-element.80), channel_id=1, source_target_pairs={{0,8},{4,12},{8,0},{12,4},{16,24},{20,28},{24,16},{28,20},{1,9},{5... | collective-permute-start | bytes 786440 | tf_op jit(solution)/shard_map/ppermute | solution.py:125
  31.0 22.9 %collective-permute-start.7 = (bf16[128,1024]{1,0:T(8,128)(2,1)S(1)}, bf16[128,1024]{1,0:T(8,128)(2,1)S(1)}, u32[]{:S(2)}, u32[]{:S(2)}) collective-permute-start(bf16[128,1024]{1,0:T(8,128)(2,1)S(1)} %get-tuple-element.81), channel_id=1, source_target_pairs={{0,12},{4,8},{8,4},{12,0},{16,28},{20,24},{24,20},{28,16},{1,13},{... | collective-permute-start | bytes 786440 | tf_op jit(solution)/shard_map/ppermute | solution.py:125
  42.3 13.3 %collective-permute-start.4 = (bf16[4,128,256]{2,1,0:T(8,128)(2,1)}, bf16[4,128,256]{2,1,0:T(8,128)(2,1)S(1)}, u32[]{:S(2)}, u32[]{:S(2)}) collective-permute-start(bf16[4,128,256]{2,1,0:T(8,128)(2,1)} %get-tuple-element.77), channel_id=1, source_target_pairs={{0,16},{4,20},{8,24},{12,28},{16,0},{20,4},{24,8},{28,12},{1,17},{... | collective-permute-start | bytes 786440 | tf_op jit(solution)/shard_map/ppermute | solution.py:568
  47.5 9.7 %collective-permute-start.18 = (bf16[4,128,256]{2,1,0:T(8,128)(2,1)S(1)}, bf16[4,128,256]{2,1,0:T(8,128)(2,1)S(1)}, u32[]{:S(2)}, u32[]{:S(2)}) collective-permute-start(bf16[4,128,256]{2,1,0:T(8,128)(2,1)S(1)} %compose_0.1.whole_ref), channel_id=1, source_target_pairs={{0,1},{2,3},{4,5},{6,7},{8,9},{10,11},{12,13},{14,15},{16,17},{18,... | collective-permute-start | bytes 786440 | tf_op jit(solution)/shard_map/ppermute | solution.py:432
  55.9 3.5 %collective-permute-start.8 = (bf16[4,128,256]{2,1,0:T(8,128)(2,1)S(1)}, bf16[4,128,256]{2,1,0:T(8,128)(2,1)S(1)}, u32[]{:S(2)}, u32[]{:S(2)}) collective-permute-start(bf16[4,128,256]{2,1,0:T(8,128)(2,1)S(1)} %compose_1.1.whole_ref), channel_id=1, source_target_pairs={{0,1},{2,3},{4,5},{6,7},{8,9},{10,11},{12,13},{14,15},{16,17},{18,... | collective-permute-start | bytes 786440 | tf_op jit(solution)/shard_map/ppermute | solution.py:432
  57.4 4.2 %collective-permute-start.20 = (bf16[4,128,128]{2,1,0:T(8,128)(2,1)S(1)}, bf16[4,128,128]{2,1,0:T(8,128)(2,1)S(1)}, u32[]{:S(2)}, u32[]{:S(2)}) collective-permute-start(bf16[4,128,128]{2,1,0:T(8,128)(2,1)S(1)} %relay_1.3), channel_id=1, source_target_pairs={{1,3},{5,7},{9,11},{13,15},{17,19},{21,23},{25,27},{29,31}} | collective-permute-start | bytes 393224 | tf_op jit(solution)/shard_map/ppermute | solution.py:432
  58.1 6.3 %collective-permute-start.19 = (bf16[4,128,128]{2,1,0:T(8,128)(2,1)S(1)}, bf16[4,128,128]{2,1,0:T(8,128)(2,1)S(1)}, u32[]{:S(2)}, u32[]{:S(2)}) collective-permute-start(bf16[4,128,128]{2,1,0:T(8,128)(2,1)S(1)} %relay_1.3), channel_id=1, source_target_pairs={{1,2},{5,6},{9,10},{13,14},{17,18},{21,22},{25,26},{29,30}} | collective-permute-start | bytes 393224 | tf_op jit(solution)/shard_map/ppermute | solution.py:432
  59.6 9.8 %collective-permute-start.10 = (bf16[4,128,128]{2,1,0:T(8,128)(2,1)S(1)}, bf16[4,128,128]{2,1,0:T(8,128)(2,1)S(1)}, u32[]{:S(2)}, u32[]{:S(2)}) collective-permute-start(bf16[4,128,128]{2,1,0:T(8,128)(2,1)S(1)} %relay_1.2), channel_id=1, source_target_pairs={{1,3},{5,7},{9,11},{13,15},{17,19},{21,23},{25,27},{29,31}} | collective-permute-start | bytes 393224 | tf_op jit(solution)/shard_map/ppermute | solution.py:432
  60.3 9.1 %collective-permute-start.9 = (bf16[4,128,128]{2,1,0:T(8,128)(2,1)S(1)}, bf16[4,128,128]{2,1,0:T(8,128)(2,1)S(1)}, u32[]{:S(2)}, u32[]{:S(2)}) collective-permute-start(bf16[4,128,128]{2,1,0:T(8,128)(2,1)S(1)} %relay_1.2), channel_id=1, source_target_pairs={{1,2},{5,6},{9,10},{13,14},{17,18},{21,22},{25,26},{29,30}} | collective-permute-start | bytes 393224 | tf_op jit(solution)/shard_map/ppermute | solution.py:432
  64.8 9.6 %collective-permute-start.21 = (bf16[4,128,128]{2,1,0:T(8,128)(2,1)S(1)}, bf16[4,128,128]{2,1,0:T(8,128)(2,1)S(1)}, u32[]{:S(2)}, u32[]{:S(2)}) collective-permute-start(bf16[4,128,128]{2,1,0:T(8,128)(2,1)S(1)} %get-tuple-element.114), channel_id=1, source_target_pairs={{0,16},{4,20},{8,24},{12,28},{16,0},{20,4},{24,8},{28,12},{1,17},{... | collective-permute-start | bytes 393224 | tf_op jit(solution)/shard_map/ppermute | solution.py:568
  69.9 8.9 %collective-permute-start.11 = (bf16[4,128,128]{2,1,0:T(8,128)(2,1)S(1)}, bf16[4,128,128]{2,1,0:T(8,128)(2,1)S(1)}, u32[]{:S(2)}, u32[]{:S(2)}) collective-permute-start(bf16[4,128,128]{2,1,0:T(8,128)(2,1)S(1)} %get-tuple-element.97), channel_id=1, source_target_pairs={{0,16},{4,20},{8,24},{12,28},{16,0},{20,4},{24,8},{28,12},{1,17},{... | collective-permute-start | bytes 393224 | tf_op jit(solution)/shard_map/ppermute | solution.py:568
  75.2 7.2 %collective-permute-start.22 = (bf16[64,1024]{1,0:T(8,128)(2,1)S(1)}, bf16[64,1024]{1,0:T(8,128)(2,1)S(1)}, u32[]{:S(2)}, u32[]{:S(2)}) collective-permute-start(bf16[64,1024]{1,0:T(8,128)(2,1)S(1)} %get-tuple-element.137), channel_id=1, source_target_pairs={{0,4},{4,0},{8,12},{12,8},{16,20},{20,16},{24,28},{28,24},{1,5},{5... | collective-permute-start | bytes 393224 | tf_op jit(solution)/shard_map/ppermute | solution.py:125
  76.5 8.6 %collective-permute-start.23 = (bf16[64,1024]{1,0:T(8,128)(2,1)S(1)}, bf16[64,1024]{1,0:T(8,128)(2,1)S(1)}, u32[]{:S(2)}, u32[]{:S(2)}) collective-permute-start(bf16[64,1024]{1,0:T(8,128)(2,1)S(1)} %get-tuple-element.135.rest_10_), channel_id=1, source_target_pairs={{0,8},{4,12},{8,0},{12,4},{16,24},{20,28},{24,16},{28,20},{1,9},{5... | collective-permute-start | bytes 393224 | tf_op jit(solution)/shard_map/ppermute | solution.py:125
  77.6 7.4 %collective-permute-start.24 = (bf16[64,1024]{1,0:T(8,128)(2,1)S(1)}, bf16[64,1024]{1,0:T(8,128)(2,1)S(1)}, u32[]{:S(2)}, u32[]{:S(2)}) collective-permute-start(bf16[64,1024]{1,0:T(8,128)(2,1)S(1)} %get-tuple-element.138), channel_id=1, source_target_pairs={{0,12},{4,8},{8,4},{12,0},{16,28},{20,24},{24,20},{28,16},{1,13},{... | collective-permute-start | bytes 393224 | tf_op jit(solution)/shard_map/ppermute | solution.py:125
  79.2 5.8 %copy-start.4 = (bf16[2,64,4096]{2,1,0:T(8,128)(2,1)S(1)}, bf16[2,64,4096]{2,1,0:T(8,128)(2,1)}, u32[]{:S(2)}) copy-start(bf16[2,64,4096]{2,1,0:T(8,128)(2,1)} %rest_4_.3) | copy-start | bytes 3145732
  79.2 5.8 %copy-start.9 = (f32[4096]{0:T(1024)S(1)}, f32[4096]{0:T(1024)}, u32[]{:S(2)}) copy-start(f32[4096]{0:T(1024)} %param.23) | copy-start | bytes 49156
  79.7 8.2 %collective-permute-start.12 = (bf16[64,1024]{1,0:T(8,128)(2,1)S(1)}, bf16[64,1024]{1,0:T(8,128)(2,1)S(1)}, u32[]{:S(2)}, u32[]{:S(2)}) collective-permute-start(bf16[64,1024]{1,0:T(8,128)(2,1)S(1)} %get-tuple-element.106), channel_id=1, source_target_pairs={{0,4},{4,0},{8,12},{12,8},{16,20},{20,16},{24,28},{28,24},{1,5},{5... | collective-permute-start | bytes 393224 | tf_op jit(solution)/shard_map/ppermute | solution.py:125
  80.9 7.0 %collective-permute-start.14 = (bf16[64,1024]{1,0:T(8,128)(2,1)S(1)}, bf16[64,1024]{1,0:T(8,128)(2,1)S(1)}, u32[]{:S(2)}, u32[]{:S(2)}) collective-permute-start(bf16[64,1024]{1,0:T(8,128)(2,1)S(1)} %get-tuple-element.107), channel_id=1, source_target_pairs={{0,12},{4,8},{8,4},{12,0},{16,28},{20,24},{24,20},{28,16},{1,13},{... | collective-permute-start | bytes 393224 | tf_op jit(solution)/shard_map/ppermute | solution.py:125
  82.5 6.0 %collective-permute-start.13 = (bf16[64,1024]{1,0:T(8,128)(2,1)S(1)}, bf16[64,1024]{1,0:T(8,128)(2,1)S(1)}, u32[]{:S(2)}, u32[]{:S(2)}) collective-permute-start(bf16[64,1024]{1,0:T(8,128)(2,1)S(1)} %get-tuple-element.104.rest_10_), channel_id=1, source_target_pairs={{0,8},{4,12},{8,0},{12,4},{16,24},{20,28},{24,16},{28,20},{1,9},{5... | collective-permute-start | bytes 393224 | tf_op jit(solution)/shard_map/ppermute | solution.py:125

commit v5 on v4

--- a/solution.py
+++ b/solution.py
@@ -58,19 +58,24 @@
     rows, width = key_ref.shape[1], outs[0].shape[1]
     part = heads // outer * DK
     copies = []
+    cuts = sem.shape[3]
     for place_out, k in enumerate(ways):
         for j in range(width // part):
             col = pl.multiple_of(((lo ^ k) * outer + (hi ^ ((first + j) % outer))) * part, part)
             for n, batch in enumerate(batches):
                 for i, ref in enumerate((key_ref, value_ref)):
-                    copies.append(
-                        pltpu.make_async_copy(
-                            ref.at[batch, :, pl.ds(col, part)],
-                            outs[place_out].at[pl.ds((2 * n + i) * rows, rows), pl.ds(j * part, part)],
-                            sem.at[place_out, j, 2 * n + i],
+                    for t in range(cuts):
+                        piece = rows // cuts
+                        copies.append(
+                            pltpu.make_async_copy(
+                                ref.at[batch, pl.ds(t * piece, piece), pl.ds(col, part)],
+                                outs[place_out].at[
+                                    pl.ds((2 * n + i) * rows + t * piece, piece), pl.ds(j * part, part)
+                                ],
+                                sem.at[place_out, j, 2 * n + i, t],
+                            )
                         )
-                    )
-                    copies[-1].start()
+                        copies[-1].start()
     if extras:
         (batch,) = batches
         small = [
@@ -508,7 +513,7 @@
                 pltpu.VMEM(boundary.shape, jnp.int32),
                 pltpu.VMEM(modality.shape, jnp.int32),
                 pltpu.VMEM(by_head_t.shape[1:], f32),
-                pltpu.SemaphoreType.DMA((len(ways), shares, 2 * len(of))),
+                pltpu.SemaphoreType.DMA((len(ways), shares, 2 * len(of), max(1, tok // 16) if direct else 1)),
                 pltpu.SemaphoreType.DMA((4,)),
             ],
             compiler_params=params(60 if direct else 16),

time: 90.9 us -> 90.9 us (level)
  transfers between devices with their start and end apart: 25 -> 25, of which waited for: 8 -> 9; matrix products, arithmetic and copies ran while one was open for 0% -> 0% of each run, Pallas kernels for 35% -> 35%
where the time goes in v5:
time: 90.9 us; the launch traced here: 89.8 us
  Pallas kernels  34.6 us (38%)
  starting transfers between devices  33.1 us (36%)
  waiting for transfers between devices  20.9 us (23%)
    pallas_call x4, Pallas kernels, state_maps(): pl.pallas_call(functools.partial(state_kernel, sub, outer, first, lane, b...  20.3 us
    ppermute x15, starting transfers between devices, exchange(): lax.ppermute(pieces[k], 'head', [(i, i ^ k) for i in range(count)])  19.9 us
    ppermute x15, waiting for transfers between devices, exchange(): lax.ppermute(pieces[k], 'head', [(i, i ^ k) for i in range(count)])  14.4 us
    ppermute x6, starting transfers between devices, before(): part = lax.ppermute(payload, 'seq', pairs)  6.71 us
    ppermute x4, starting transfers between devices, swap(): lax.ppermute(parts[j], 'head', [(i, i ^ j * sub) for i in range(count)])  6.5 us
    pallas_call x3, Pallas kernels, pack_kv(): pl.pallas_call(functools.partial(pack_kv_kernel, sub, ways, outer, of, he...  4.89 us
    ppermute x4, waiting for transfers between devices, swap(): lax.ppermute(parts[j], 'head', [(i, i ^ j * sub) for i in range(count)])  3.7 us
    pallas_call x4, Pallas kernels, query_parts(): pl.pallas_call(functools.partial(query_kernel, sub, outer, first, blocks,...  3.29 us
  transfers between devices with their start and end apart: 25, of which 9 were waited for; matrix products, arithmetic and copies ran while one was open for 0% of the time, Pallas kernels for 35%

profile of v5, /device:TPU:2, one launch (start us, length us, event | category | flops | bytes accessed | tf_op | source)
XLA Modules:
  0.0 89.8 jit_solution(6159789159063978295)
XLA Ops:
  0.0 1.8 %pack_kv_0_3.1.rest_0_ = bf16[144,1024]{1,0:T(8,128)(2,1)} custom-call(bf16[2,64,4096]{2,1,0:T(8,128)(2,1)} %key_ref.5, bf16[2,64,4096]{2,1,0:T(8,128)(2,1)} %value_ref.5, bf16[2,64,128]{2,1,0:T(8,128)(2,1)} %latent_ref.5, bf16[2,32,64]{2,1,0:T(8,128)(2,1)} %bitcast.2, s32[2,64]{1,0:T(2,128)} %mark_ref.5, s32[2,64]{1,0:T(2,128)} %kind_ref.5), custom_call_target="tpu_custom_call" | custom-call | tf_op jit(solution)/shard_map/pack_kv_0_3/pallas_call | solution.py:505
  1.9 2.6 %collective-permute-start = (bf16[144,1024]{1,0:T(8,128)(2,1)}, bf16[144,1024]{1,0:T(8,128)(2,1)S(1)}, u32[]{:S(2)}, u32[]{:S(2)}) collective-permute-start(bf16[144,1024]{1,0:T(8,128)(2,1)} %pack_kv_0_3.1.rest_0_), channel_id=1, source_target_pairs={{0,12},{4,8},{8,4},{12,0},{16,28},{20,24},{24,20},{28,16},{1,13},{... | collective-permute-start | bytes 884744 | tf_op jit(solution)/shard_map/ppermute | solution.py:130
  4.5 2.6 %pack_kv_0_0.1 = (bf16[144,1024]{1,0:T(8,128)(2,1)}, bf16[144,1024]{1,0:T(8,128)(2,1)}, bf16[144,1024]{1,0:T(8,128)(2,1)}) custom-call(bf16[2,64,4096]{2,1,0:T(8,128)(2,1)} %key_ref.5, bf16[2,64,4096]{2,1,0:T(8,128)(2,1)} %value_ref.5, bf16[2,64,128]{2,1,0:T(8,128)(2,1)} %latent_ref.5, bf16[2,32,64]{2,1,0:T(8,128)(2,1)} %bitcast.3, s32[2,64]{1,0:T(2,128)} %mark_ref.5, ...), custom_call_target="tpu_custom_call" | custom-call | tf_op jit(solution)/shard_map/pack_kv_0_0/pallas_call | solution.py:505
  7.1 0.6 collective-permute-start.15
  7.7 0.6 collective-permute-start.16
  8.2 4.6 %collective-permute-done.rest_0_.rest_3_.rest_7_ = bf16[144,1024]{1,0:T(8,128)(2,1)S(1)} collective-permute-done((bf16[144,1024]{1,0:T(8,128)(2,1)}, bf16[144,1024]{1,0:T(8,128)(2,1)S(1)}, u32[]{:S(2)}, u32[]{:S(2)}) %collective-permute-start) | collective-permute-done | bytes 294944 | tf_op jit(solution)/shard_map/ppermute | solution.py:130
  12.9 0.5 pack_kv_1_0.1
  13.4 2.8 %collective-permute-start.3 = (bf16[144,1024]{1,0:T(8,128)(2,1)S(1)}, bf16[144,1024]{1,0:T(8,128)(2,1)S(1)}, u32[]{:S(2)}, u32[]{:S(2)}) collective-permute-start(bf16[144,1024]{1,0:T(8,128)(2,1)S(1)} %get-tuple-element.75), channel_id=1, source_target_pairs={{0,12},{4,8},{8,4},{12,0},{16,28},{20,24},{24,20},{28,16},{1,13},{... | collective-permute-start | bytes 884744 | tf_op jit(solution)/shard_map/ppermute | solution.py:130
  16.1 0.5 collective-permute-start.1
  16.9 2.3 %collective-permute-done.15.rest_1_.rest_5_ = bf16[144,1024]{1,0:T(8,128)(2,1)S(1)} collective-permute-done((bf16[144,1024]{1,0:T(8,128)(2,1)}, bf16[144,1024]{1,0:T(8,128)(2,1)S(1)}, u32[]{:S(2)}, u32[]{:S(2)}) %collective-permute-start.15) | collective-permute-done | bytes 294944 | tf_op jit(solution)/shard_map/ppermute | solution.py:130
  19.4 0.6 copy-done.12
  20.0 4.9 %state_maps_0_1.1 = (bf16[4,2,128,128]{3,2,1,0:T(8,128)(2,1)S(1)}, f32[4,2,128,128]{3,2,1,0:T(8,128)S(1)}, bf16[4,2,128,256]{3,2,1,0:T(8,128)(2,1)S(1)}, f32[4,2...) custom-call(f32[32]{0:T(128)S(1)} %copy-done.12, ...), custom_call_target="tpu_custom_call" | custom-call | flops 160000000 | tf_op jit(solution)/shard_map/state_maps_0_1/pallas_call | solution.py:553
  24.9 2.7 %collective-permute-start.17 = (bf16[4,128,256]{2,1,0:T(8,128)(2,1)S(1)}, bf16[4,128,256]{2,1,0:T(8,128)(2,1)S(1)}, u32[]{:S(2)}, u32[]{:S(2)}) collective-permute-start(bf16[4,128,256]{2,1,0:T(8,128)(2,1)S(1)} %get-tuple-element.112), channel_id=1, source_target_pairs={{0,16},{4,20},{8,24},{12,28},{16,0},{20,4},{24,8},{28,12},{1,17},{... | collective-permute-start | bytes 786440 | tf_op jit(solution)/shard_map/ppermute | solution.py:573
  27.9 1.6 %collective-permute-start.5 = (bf16[128,1024]{1,0:T(8,128)(2,1)S(1)}, bf16[128,1024]{1,0:T(8,128)(2,1)S(1)}, u32[]{:S(2)}, u32[]{:S(2)}) collective-permute-start(bf16[128,1024]{1,0:T(8,128)(2,1)S(1)} %get-tuple-element.79), channel_id=1, source_target_pairs={{0,4},{4,0},{8,12},{12,8},{16,20},{20,16},{24,28},{28,24},{1,5},{5... | collective-permute-start | bytes 786440 | tf_op jit(solution)/shard_map/ppermute | solution.py:130
  29.5 1.6 %collective-permute-start.6 = (bf16[128,1024]{1,0:T(8,128)(2,1)S(1)}, bf16[128,1024]{1,0:T(8,128)(2,1)S(1)}, u32[]{:S(2)}, u32[]{:S(2)}) collective-permute-start(bf16[128,1024]{1,0:T(8,128)(2,1)S(1)} %get-tuple-element.80), channel_id=1, source_target_pairs={{0,8},{4,12},{8,0},{12,4},{16,24},{20,28},{24,16},{28,20},{1,9},{5... | collective-permute-start | bytes 786440 | tf_op jit(solution)/shard_map/ppermute | solution.py:130
  31.0 2.3 %collective-permute-start.7 = (bf16[128,1024]{1,0:T(8,128)(2,1)S(1)}, bf16[128,1024]{1,0:T(8,128)(2,1)S(1)}, u32[]{:S(2)}, u32[]{:S(2)}) collective-permute-start(bf16[128,1024]{1,0:T(8,128)(2,1)S(1)} %get-tuple-element.81), channel_id=1, source_target_pairs={{0,12},{4,8},{8,4},{12,0},{16,28},{20,24},{24,20},{28,16},{1,13},{... | collective-permute-start | bytes 786440 | tf_op jit(solution)/shard_map/ppermute | solution.py:130
  33.4 3.5 %collective-permute-done.2.rest_2_.rest_6_ = bf16[144,1024]{1,0:T(8,128)(2,1)S(1)} collective-permute-done((bf16[144,1024]{1,0:T(8,128)(2,1)S(1)}, bf16[144,1024]{1,0:T(8,128)(2,1)S(1)}, u32[]{:S(2)}, u32[]{:S(2)}) %collective-permute-start.2) | collective-permute-done | bytes 294944 | tf_op jit(solution)/shard_map/ppermute | solution.py:130
  36.8 5.6 %state_maps_1_1.1 = (bf16[4,2,128,128]{3,2,1,0:T(8,128)(2,1)S(1)}, f32[4,2,128,128]{3,2,1,0:T(8,128)S(1)}, bf16[4,2,128,256]{3,2,1,0:T(8,128)(2,1)S(1)}, f32[4,2...) custom-call(f32[32]{0:T(128)S(1)} %copy-done.12, ...), custom_call_target="tpu_custom_call" | custom-call | flops 160000000 | tf_op jit(solution)/shard_map/state_maps_1_1/pallas_call | solution.py:553
  42.5 4.9 %state_maps_0_0.1 = (bf16[4,2,128,128]{3,2,1,0:T(8,128)(2,1)S(1)}, f32[4,2,128,128]{3,2,1,0:T(8,128)S(1)}, bf16[4,2,128,256]{3,2,1,0:T(8,128)(2,1)S(1)}, f32[4,2...) custom-call(f32[32]{0:T(128)S(1)} %copy-done.12, ...), custom_call_target="tpu_custom_call" | custom-call | flops 160000000 | tf_op jit(solution)/shard_map/state_maps_0_0/pallas_call | solution.py:553
  47.6 1.5 %collective-permute-start.18 = (bf16[4,128,256]{2,1,0:T(8,128)(2,1)S(1)}, bf16[4,128,256]{2,1,0:T(8,128)(2,1)S(1)}, u32[]{:S(2)}, u32[]{:S(2)}) collective-permute-start(bf16[4,128,256]{2,1,0:T(8,128)(2,1)S(1)} %compose_0.1.whole_ref), channel_id=1, source_target_pairs={{0,1},{2,3},{4,5},{6,7},{8,9},{10,11},{12,13},{14,15},{16,17},{18,... | collective-permute-start | bytes 786440 | tf_op jit(solution)/shard_map/ppermute | solution.py:437
  49.1 4.9 %state_maps_1_0.1 = (bf16[4,2,128,128]{3,2,1,0:T(8,128)(2,1)S(1)}, f32[4,2,128,128]{3,2,1,0:T(8,128)S(1)}, bf16[4,2,128,256]{3,2,1,0:T(8,128)(2,1)S(1)}, f32[4,2...) custom-call(f32[32]{0:T(128)S(1)} %copy-done.12, ...), custom_call_target="tpu_custom_call" | custom-call | flops 160000000 | tf_op jit(solution)/shard_map/state_maps_1_0/pallas_call | solution.py:553
  54.1 0.8 query_parts_1_1.1
  54.9 0.8 query_parts_1_0.1
  56.0 1.3 %collective-permute-start.8 = (bf16[4,128,256]{2,1,0:T(8,128)(2,1)S(1)}, bf16[4,128,256]{2,1,0:T(8,128)(2,1)S(1)}, u32[]{:S(2)}, u32[]{:S(2)}) collective-permute-start(bf16[4,128,256]{2,1,0:T(8,128)(2,1)S(1)} %compose_1.1.whole_ref), channel_id=1, source_target_pairs={{0,1},{2,3},{4,5},{6,7},{8,9},{10,11},{12,13},{14,15},{16,17},{18,... | collective-permute-start | bytes 786440 | tf_op jit(solution)/shard_map/ppermute | solution.py:437
  57.6 0.7 collective-permute-start.20
  58.3 1.3 %collective-permute-start.19 = (bf16[4,128,128]{2,1,0:T(8,128)(2,1)S(1)}, bf16[4,128,128]{2,1,0:T(8,128)(2,1)S(1)}, u32[]{:S(2)}, u32[]{:S(2)}) collective-permute-start(bf16[4,128,128]{2,1,0:T(8,128)(2,1)S(1)} %relay_1.3), channel_id=1, source_target_pairs={{1,2},{5,6},{9,10},{13,14},{17,18},{21,22},{25,26},{29,30}} | collective-permute-start | bytes 393224 | tf_op jit(solution)/shard_map/ppermute | solution.py:437
  59.8 0.7 collective-permute-start.10
  60.5 1.3 %collective-permute-start.9 = (bf16[4,128,128]{2,1,0:T(8,128)(2,1)S(1)}, bf16[4,128,128]{2,1,0:T(8,128)(2,1)S(1)}, u32[]{:S(2)}, u32[]{:S(2)}) collective-permute-start(bf16[4,128,128]{2,1,0:T(8,128)(2,1)S(1)} %relay_1.2), channel_id=1, source_target_pairs={{1,2},{5,6},{9,10},{13,14},{17,18},{21,22},{25,26},{29,30}} | collective-permute-start | bytes 393224 | tf_op jit(solution)/shard_map/ppermute | solution.py:437
  61.8 2.8 %collective-permute-done.19 = bf16[4,128,128]{2,1,0:T(8,128)(2,1)S(1)} collective-permute-done((bf16[4,128,128]{2,1,0:T(8,128)(2,1)S(1)}, bf16[4,128,128]{2,1,0:T(8,128)(2,1)S(1)}, u32[]{:S(2)}, u32[]{:S(2)}) %collective-permute-start.19) | collective-permute-done | bytes 131104 | tf_op jit(solution)/shard_map/ppermute | solution.py:437
  65.0 3.0 %collective-permute-start.21 = (bf16[4,128,128]{2,1,0:T(8,128)(2,1)S(1)}, bf16[4,128,128]{2,1,0:T(8,128)(2,1)S(1)}, u32[]{:S(2)}, u32[]{:S(2)}) collective-permute-start(bf16[4,128,128]{2,1,0:T(8,128)(2,1)S(1)} %get-tuple-element.114), channel_id=1, source_target_pairs={{0,16},{4,20},{8,24},{12,28},{16,0},{20,4},{24,8},{28,12},{1,17},{... | collective-permute-start | bytes 393224 | tf_op jit(solution)/shard_map/ppermute | solution.py:573
  67.9 0.8 query_parts_0_1.1
  68.8 0.8 query_parts_0_0.1
  70.0 0.9 collective-permute-start.11
  70.9 3.7 %collective-permute-done.21.rest_1_ = bf16[4,128,128]{2,1,0:T(8,128)(2,1)S(1)} collective-permute-done((bf16[4,128,128]{2,1,0:T(8,128)(2,1)S(1)}, bf16[4,128,128]{2,1,0:T(8,128)(2,1)S(1)}, u32[]{:S(2)}, u32[]{:S(2)}) %collective-permute-start.21) | collective-permute-done | bytes 131104 | tf_op jit(solution)/shard_map/ppermute | solution.py:573
  75.0 0.4 span_outputs_0_0.1
  75.4 1.1 %collective-permute-start.22 = (bf16[64,1024]{1,0:T(8,128)(2,1)S(1)}, bf16[64,1024]{1,0:T(8,128)(2,1)S(1)}, u32[]{:S(2)}, u32[]{:S(2)}) collective-permute-start(bf16[64,1024]{1,0:T(8,128)(2,1)S(1)} %get-tuple-element.137), channel_id=1, source_target_pairs={{0,4},{4,0},{8,12},{12,8},{16,20},{20,16},{24,28},{28,24},{1,5},{5... | collective-permute-start | bytes 393224 | tf_op jit(solution)/shard_map/ppermute | solution.py:130
  76.5 1.1 %collective-permute-start.23 = (bf16[64,1024]{1,0:T(8,128)(2,1)S(1)}, bf16[64,1024]{1,0:T(8,128)(2,1)S(1)}, u32[]{:S(2)}, u32[]{:S(2)}) collective-permute-start(bf16[64,1024]{1,0:T(8,128)(2,1)S(1)} %get-tuple-element.135.rest_10_), channel_id=1, source_target_pairs={{0,8},{4,12},{8,0},{12,4},{16,24},{20,28},{24,16},{28,20},{1,9},{5... | collective-permute-start | bytes 393224 | tf_op jit(solution)/shard_map/ppermute | solution.py:130
  77.6 1.4 %collective-permute-start.24 = (bf16[64,1024]{1,0:T(8,128)(2,1)S(1)}, bf16[64,1024]{1,0:T(8,128)(2,1)S(1)}, u32[]{:S(2)}, u32[]{:S(2)}) collective-permute-start(bf16[64,1024]{1,0:T(8,128)(2,1)S(1)} %get-tuple-element.138), channel_id=1, source_target_pairs={{0,12},{4,8},{8,4},{12,0},{16,28},{20,24},{24,20},{28,16},{1,13},{... | collective-permute-start | bytes 393224 | tf_op jit(solution)/shard_map/ppermute | solution.py:130
  79.0 0.4 span_outputs_1_1.1
  79.4 0.4 span_outputs_1_0.1
  79.8 1.1 %collective-permute-start.12 = (bf16[64,1024]{1,0:T(8,128)(2,1)S(1)}, bf16[64,1024]{1,0:T(8,128)(2,1)S(1)}, u32[]{:S(2)}, u32[]{:S(2)}) collective-permute-start(bf16[64,1024]{1,0:T(8,128)(2,1)S(1)} %get-tuple-element.106), channel_id=1, source_target_pairs={{0,4},{4,0},{8,12},{12,8},{16,20},{20,16},{24,28},{28,24},{1,5},{5... | collective-permute-start | bytes 393224 | tf_op jit(solution)/shard_map/ppermute | solution.py:130
  80.9 1.4 %collective-permute-start.14 = (bf16[64,1024]{1,0:T(8,128)(2,1)S(1)}, bf16[64,1024]{1,0:T(8,128)(2,1)S(1)}, u32[]{:S(2)}, u32[]{:S(2)}) collective-permute-start(bf16[64,1024]{1,0:T(8,128)(2,1)S(1)} %get-tuple-element.107), channel_id=1, source_target_pairs={{0,12},{4,8},{8,4},{12,0},{16,28},{20,24},{24,20},{28,16},{1,13},{... | collective-permute-start | bytes 393224 | tf_op jit(solution)/shard_map/ppermute | solution.py:130
  82.4 1.0 %collective-permute-start.13 = (bf16[64,1024]{1,0:T(8,128)(2,1)S(1)}, bf16[64,1024]{1,0:T(8,128)(2,1)S(1)}, u32[]{:S(2)}, u32[]{:S(2)}) collective-permute-start(bf16[64,1024]{1,0:T(8,128)(2,1)S(1)} %get-tuple-element.104.rest_10_), channel_id=1, source_target_pairs={{0,8},{4,12},{8,0},{12,4},{16,24},{20,28},{24,16},{28,20},{1,9},{5... | collective-permute-start | bytes 393224 | tf_op jit(solution)/shard_map/ppermute | solution.py:130
  83.4 1.6 %collective-permute-done.24.rest_3_ = bf16[64,1024]{1,0:T(8,128)(2,1)S(1)} collective-permute-done((bf16[64,1024]{1,0:T(8,128)(2,1)S(1)}, bf16[64,1024]{1,0:T(8,128)(2,1)S(1)}, u32[]{:S(2)}, u32[]{:S(2)}) %collective-permute-start.24) | collective-permute-done | bytes 131104 | tf_op jit(solution)/shard_map/ppermute | solution.py:130
  85.0 1.2 %finish_0.1.rest_6_ = bf16[2,64,4096]{2,1,0:T(8,128)(2,1)} custom-call(bf16[64,1024]{1,0:T(8,128)(2,1)S(1)} %get-tuple-element.136.rest_0_, bf16[64,1024]{1,0:T(8,128)(2,1)S(1)} %collective-permute-done.22.rest_1_, bf16[64,1024]{1,0:T(8,128)(2,1)S(1)} %collective-permute-done.23.rest_2_, bf16[64,1024]{1,0:T(8,128)(2,1)S(1)} %collective-permute-done.24.rest_3_, ...), custom_call_target="tpu_custom_call" | custom-call | tf_op jit(solution)/shard_map/finish_0/pallas_call | solution.py:707
  86.3 1.6 %collective-permute-done.12.rest_1_ = bf16[64,1024]{1,0:T(8,128)(2,1)S(1)} collective-permute-done((bf16[64,1024]{1,0:T(8,128)(2,1)S(1)}, bf16[64,1024]{1,0:T(8,128)(2,1)S(1)}, u32[]{:S(2)}, u32[]{:S(2)}) %collective-permute-start.12) | collective-permute-done | bytes 131104 | tf_op jit(solution)/shard_map/ppermute | solution.py:130
  87.9 0.6 collective-permute-done.13.rest_2_
  88.5 1.2 %finish_1.1 = bf16[2,64,4096]{2,1,0:T(8,128)(2,1)} custom-call(bf16[64,1024]{1,0:T(8,128)(2,1)S(1)} %get-tuple-element.105.rest_0_, bf16[64,1024]{1,0:T(8,128)(2,1)S(1)} %collective-permute-done.12.rest_1_, bf16[64,1024]{1,0:T(8,128)(2,1)S(1)} %collective-permute-done.13.rest_2_, ...), custom_call_target="tpu_custom_call", output_to_operand_aliasing={{}: (6, {})} | custom-call | tf_op jit(solution)/shard_map/finish_1/pallas_call | solution.py:707
  (54 shorter events, 2.9 us)
Async XLA Ops:
  1.8 11.0 %copy-start.1 = (bf16[2,64,4096]{2,1,0:T(8,128)(2,1)S(1)}, bf16[2,64,4096]{2,1,0:T(8,128)(2,1)}, u32[]{:S(2)}) copy-start(bf16[2,64,4096]{2,1,0:T(8,128)(2,1)} %key_ref.5) | copy-start | bytes 3145732
  1.8 11.0 %copy-start.2 = (bf16[2,64,4096]{2,1,0:T(8,128)(2,1)S(1)}, bf16[2,64,4096]{2,1,0:T(8,128)(2,1)}, u32[]{:S(2)}) copy-start(bf16[2,64,4096]{2,1,0:T(8,128)(2,1)} %value_ref.5) | copy-start | bytes 3145732
  1.8 11.0 %copy-start.7 = (bf16[2,64,128]{2,1,0:T(8,128)(2,1)S(1)}, bf16[2,64,128]{2,1,0:T(8,128)(2,1)}, u32[]{:S(2)}) copy-start(bf16[2,64,128]{2,1,0:T(8,128)(2,1)} %latent_ref.5) | copy-start | bytes 98308
  1.9 11.0 %copy-start.8 = (bf16[2,64,32]{1,2,0:T(8,128)(2,1)S(1)}, bf16[2,64,32]{1,2,0:T(8,128)(2,1)}, u32[]{:S(2)}) copy-start(bf16[2,64,32]{1,2,0:T(8,128)(2,1)} %param.15) | copy-start | bytes 24580
  1.9 11.0 %collective-permute-start = (bf16[144,1024]{1,0:T(8,128)(2,1)}, bf16[144,1024]{1,0:T(8,128)(2,1)S(1)}, u32[]{:S(2)}, u32[]{:S(2)}) collective-permute-start(bf16[144,1024]{1,0:T(8,128)(2,1)} %pack_kv_0_3.1.rest_0_), channel_id=1, source_target_pairs={{0,12},{4,8},{8,4},{12,0},{16,28},{20,24},{24,20},{28,16},{1,13},{... | collective-permute-start | bytes 884744 | tf_op jit(solution)/shard_map/ppermute | solution.py:130
  7.1 5.8 %copy-start.11 = (s32[2,64]{1,0:T(2,128)S(1)}, s32[2,64]{1,0:T(2,128)}, u32[]{:S(2)}) copy-start(s32[2,64]{1,0:T(2,128)} %kind_ref.5) | copy-start | bytes 1540
  7.1 5.8 %copy-start.10 = (s32[2,64]{1,0:T(2,128)S(1)}, s32[2,64]{1,0:T(2,128)}, u32[]{:S(2)}) copy-start(s32[2,64]{1,0:T(2,128)} %mark_ref.5) | copy-start | bytes 1540
  7.1 12.2 %collective-permute-start.15 = (bf16[144,1024]{1,0:T(8,128)(2,1)}, bf16[144,1024]{1,0:T(8,128)(2,1)S(1)}, u32[]{:S(2)}, u32[]{:S(2)}) collective-permute-start(bf16[144,1024]{1,0:T(8,128)(2,1)} %get-tuple-element.109), channel_id=1, source_target_pairs={{0,4},{4,0},{8,12},{12,8},{16,20},{20,16},{24,28},{28,24},{1,5},{5... | collective-permute-start | bytes 884744 | tf_op jit(solution)/shard_map/ppermute | solution.py:130
  7.7 11.7 %copy-start = (bf16[128,4096]{1,0:T(8,128)(2,1)S(1)}, bf16[128,4096]{1,0:T(8,128)(2,1)}, u32[]{:S(2)}) copy-start(bf16[128,4096]{1,0:T(8,128)(2,1)} %rest_8_.7) | copy-start | bytes 3145732
  7.7 11.7 %copy-start.3 = (bf16[144,1024]{1,0:T(8,128)(2,1)S(1)}, bf16[144,1024]{1,0:T(8,128)(2,1)}, u32[]{:S(2)}) copy-start(bf16[144,1024]{1,0:T(8,128)(2,1)} %get-tuple-element.108.rest_0_.rest_4_) | copy-start | bytes 884740
  7.7 11.7 %copy-start.6 = (f32[2,4096]{1,0:T(2,128)S(1)}, f32[2,4096]{1,0:T(2,128)}, u32[]{:S(2)}) copy-start(f32[2,4096]{1,0:T(2,128)} %rest_9_.7) | copy-start | bytes 98308
  7.7 11.7 %collective-permute-start.16 = (bf16[144,1024]{1,0:T(8,128)(2,1)}, bf16[144,1024]{1,0:T(8,128)(2,1)S(1)}, u32[]{:S(2)}, u32[]{:S(2)}) collective-permute-start(bf16[144,1024]{1,0:T(8,128)(2,1)} %get-tuple-element.110), channel_id=1, source_target_pairs={{0,8},{4,12},{8,0},{12,4},{16,24},{20,28},{24,16},{28,20},{1,9},{5... | collective-permute-start | bytes 884744 | tf_op jit(solution)/shard_map/ppermute | solution.py:130
  13.4 14.2 %collective-permute-start.3 = (bf16[144,1024]{1,0:T(8,128)(2,1)S(1)}, bf16[144,1024]{1,0:T(8,128)(2,1)S(1)}, u32[]{:S(2)}, u32[]{:S(2)}) collective-permute-start(bf16[144,1024]{1,0:T(8,128)(2,1)S(1)} %get-tuple-element.75), channel_id=1, source_target_pairs={{0,12},{4,8},{8,4},{12,0},{16,28},{20,24},{24,20},{28,16},{1,13},{... | collective-permute-start | bytes 884744 | tf_op jit(solution)/shard_map/ppermute | solution.py:130
  16.1 14.9 %collective-permute-start.1 = (bf16[144,1024]{1,0:T(8,128)(2,1)S(1)}, bf16[144,1024]{1,0:T(8,128)(2,1)S(1)}, u32[]{:S(2)}, u32[]{:S(2)}) collective-permute-start(bf16[144,1024]{1,0:T(8,128)(2,1)S(1)} %get-tuple-element.73), channel_id=1, source_target_pairs={{0,4},{4,0},{8,12},{12,8},{16,20},{20,16},{24,28},{28,24},{1,5},{5... | collective-permute-start | bytes 884744 | tf_op jit(solution)/shard_map/ppermute | solution.py:130
  16.6 20.2 %collective-permute-start.2 = (bf16[144,1024]{1,0:T(8,128)(2,1)S(1)}, bf16[144,1024]{1,0:T(8,128)(2,1)S(1)}, u32[]{:S(2)}, u32[]{:S(2)}) collective-permute-start(bf16[144,1024]{1,0:T(8,128)(2,1)S(1)} %get-tuple-element.74), channel_id=1, source_target_pairs={{0,8},{4,12},{8,0},{12,4},{16,24},{20,28},{24,16},{28,20},{1,9},{5... | collective-permute-start | bytes 884744 | tf_op jit(solution)/shard_map/ppermute | solution.py:130
  19.4 0.7 copy-start.12
  20.0 7.6 %copy-start.5 = (bf16[2,64,4096]{2,1,0:T(8,128)(2,1)S(1)}, bf16[2,64,4096]{2,1,0:T(8,128)(2,1)}, u32[]{:S(2)}) copy-start(bf16[2,64,4096]{2,1,0:T(8,128)(2,1)} %query_ref.1) | copy-start | bytes 3145732
  24.9 22.4 %collective-permute-start.17 = (bf16[4,128,256]{2,1,0:T(8,128)(2,1)S(1)}, bf16[4,128,256]{2,1,0:T(8,128)(2,1)S(1)}, u32[]{:S(2)}, u32[]{:S(2)}) collective-permute-start(bf16[4,128,256]{2,1,0:T(8,128)(2,1)S(1)} %get-tuple-element.112), channel_id=1, source_target_pairs={{0,16},{4,20},{8,24},{12,28},{16,0},{20,4},{24,8},{28,12},{1,17},{... | collective-permute-start | bytes 786440 | tf_op jit(solution)/shard_map/ppermute | solution.py:573
  27.9 26.2 %collective-permute-start.5 = (bf16[128,1024]{1,0:T(8,128)(2,1)S(1)}, bf16[128,1024]{1,0:T(8,128)(2,1)S(1)}, u32[]{:S(2)}, u32[]{:S(2)}) collective-permute-start(bf16[128,1024]{1,0:T(8,128)(2,1)S(1)} %get-tuple-element.79), channel_id=1, source_target_pairs={{0,4},{4,0},{8,12},{12,8},{16,20},{20,16},{24,28},{28,24},{1,5},{5... | collective-permute-start | bytes 786440 | tf_op jit(solution)/shard_map/ppermute | solution.py:130
  29.5 24.6 %collective-permute-start.6 = (bf16[128,1024]{1,0:T(8,128)(2,1)S(1)}, bf16[128,1024]{1,0:T(8,128)(2,1)S(1)}, u32[]{:S(2)}, u32[]{:S(2)}) collective-permute-start(bf16[128,1024]{1,0:T(8,128)(2,1)S(1)} %get-tuple-element.80), channel_id=1, source_target_pairs={{0,8},{4,12},{8,0},{12,4},{16,24},{20,28},{24,16},{28,20},{1,9},{5... | collective-permute-start | bytes 786440 | tf_op jit(solution)/shard_map/ppermute | solution.py:130
  31.0 23.1 %collective-permute-start.7 = (bf16[128,1024]{1,0:T(8,128)(2,1)S(1)}, bf16[128,1024]{1,0:T(8,128)(2,1)S(1)}, u32[]{:S(2)}, u32[]{:S(2)}) collective-permute-start(bf16[128,1024]{1,0:T(8,128)(2,1)S(1)} %get-tuple-element.81), channel_id=1, source_target_pairs={{0,12},{4,8},{8,4},{12,0},{16,28},{20,24},{24,20},{28,16},{1,13},{... | collective-permute-start | bytes 786440 | tf_op jit(solution)/shard_map/ppermute | solution.py:130
  42.5 13.3 %collective-permute-start.4 = (bf16[4,128,256]{2,1,0:T(8,128)(2,1)}, bf16[4,128,256]{2,1,0:T(8,128)(2,1)S(1)}, u32[]{:S(2)}, u32[]{:S(2)}) collective-permute-start(bf16[4,128,256]{2,1,0:T(8,128)(2,1)} %get-tuple-element.77), channel_id=1, source_target_pairs={{0,16},{4,20},{8,24},{12,28},{16,0},{20,4},{24,8},{28,12},{1,17},{... | collective-permute-start | bytes 786440 | tf_op jit(solution)/shard_map/ppermute | solution.py:573
  47.6 9.7 %collective-permute-start.18 = (bf16[4,128,256]{2,1,0:T(8,128)(2,1)S(1)}, bf16[4,128,256]{2,1,0:T(8,128)(2,1)S(1)}, u32[]{:S(2)}, u32[]{:S(2)}) collective-permute-start(bf16[4,128,256]{2,1,0:T(8,128)(2,1)S(1)} %compose_0.1.whole_ref), channel_id=1, source_target_pairs={{0,1},{2,3},{4,5},{6,7},{8,9},{10,11},{12,13},{14,15},{16,17},{18,... | collective-permute-start | bytes 786440 | tf_op jit(solution)/shard_map/ppermute | solution.py:437
  56.0 3.5 %collective-permute-start.8 = (bf16[4,128,256]{2,1,0:T(8,128)(2,1)S(1)}, bf16[4,128,256]{2,1,0:T(8,128)(2,1)S(1)}, u32[]{:S(2)}, u32[]{:S(2)}) collective-permute-start(bf16[4,128,256]{2,1,0:T(8,128)(2,1)S(1)} %compose_1.1.whole_ref), channel_id=1, source_target_pairs={{0,1},{2,3},{4,5},{6,7},{8,9},{10,11},{12,13},{14,15},{16,17},{18,... | collective-permute-start | bytes 786440 | tf_op jit(solution)/shard_map/ppermute | solution.py:437
  57.6 4.2 %collective-permute-start.20 = (bf16[4,128,128]{2,1,0:T(8,128)(2,1)S(1)}, bf16[4,128,128]{2,1,0:T(8,128)(2,1)S(1)}, u32[]{:S(2)}, u32[]{:S(2)}) collective-permute-start(bf16[4,128,128]{2,1,0:T(8,128)(2,1)S(1)} %relay_1.3), channel_id=1, source_target_pairs={{1,3},{5,7},{9,11},{13,15},{17,19},{21,23},{25,27},{29,31}} | collective-permute-start | bytes 393224 | tf_op jit(solution)/shard_map/ppermute | solution.py:437
  58.3 6.3 %collective-permute-start.19 = (bf16[4,128,128]{2,1,0:T(8,128)(2,1)S(1)}, bf16[4,128,128]{2,1,0:T(8,128)(2,1)S(1)}, u32[]{:S(2)}, u32[]{:S(2)}) collective-permute-start(bf16[4,128,128]{2,1,0:T(8,128)(2,1)S(1)} %relay_1.3), channel_id=1, source_target_pairs={{1,2},{5,6},{9,10},{13,14},{17,18},{21,22},{25,26},{29,30}} | collective-permute-start | bytes 393224 | tf_op jit(solution)/shard_map/ppermute | solution.py:437
  59.8 9.8 %collective-permute-start.10 = (bf16[4,128,128]{2,1,0:T(8,128)(2,1)S(1)}, bf16[4,128,128]{2,1,0:T(8,128)(2,1)S(1)}, u32[]{:S(2)}, u32[]{:S(2)}) collective-permute-start(bf16[4,128,128]{2,1,0:T(8,128)(2,1)S(1)} %relay_1.2), channel_id=1, source_target_pairs={{1,3},{5,7},{9,11},{13,15},{17,19},{21,23},{25,27},{29,31}} | collective-permute-start | bytes 393224 | tf_op jit(solution)/shard_map/ppermute | solution.py:437
  60.5 9.1 %collective-permute-start.9 = (bf16[4,128,128]{2,1,0:T(8,128)(2,1)S(1)}, bf16[4,128,128]{2,1,0:T(8,128)(2,1)S(1)}, u32[]{:S(2)}, u32[]{:S(2)}) collective-permute-start(bf16[4,128,128]{2,1,0:T(8,128)(2,1)S(1)} %relay_1.2), channel_id=1, source_target_pairs={{1,2},{5,6},{9,10},{13,14},{17,18},{21,22},{25,26},{29,30}} | collective-permute-start | bytes 393224 | tf_op jit(solution)/shard_map/ppermute | solution.py:437
  65.0 9.6 %collective-permute-start.21 = (bf16[4,128,128]{2,1,0:T(8,128)(2,1)S(1)}, bf16[4,128,128]{2,1,0:T(8,128)(2,1)S(1)}, u32[]{:S(2)}, u32[]{:S(2)}) collective-permute-start(bf16[4,128,128]{2,1,0:T(8,128)(2,1)S(1)} %get-tuple-element.114), channel_id=1, source_target_pairs={{0,16},{4,20},{8,24},{12,28},{16,0},{20,4},{24,8},{28,12},{1,17},{... | collective-permute-start | bytes 393224 | tf_op jit(solution)/shard_map/ppermute | solution.py:573
  70.0 8.9 %collective-permute-start.11 = (bf16[4,128,128]{2,1,0:T(8,128)(2,1)S(1)}, bf16[4,128,128]{2,1,0:T(8,128)(2,1)S(1)}, u32[]{:S(2)}, u32[]{:S(2)}) collective-permute-start(bf16[4,128,128]{2,1,0:T(8,128)(2,1)S(1)} %get-tuple-element.97), channel_id=1, source_target_pairs={{0,16},{4,20},{8,24},{12,28},{16,0},{20,4},{24,8},{28,12},{1,17},{... | collective-permute-start | bytes 393224 | tf_op jit(solution)/shard_map/ppermute | solution.py:573
  75.4 6.9 %collective-permute-start.22 = (bf16[64,1024]{1,0:T(8,128)(2,1)S(1)}, bf16[64,1024]{1,0:T(8,128)(2,1)S(1)}, u32[]{:S(2)}, u32[]{:S(2)}) collective-permute-start(bf16[64,1024]{1,0:T(8,128)(2,1)S(1)} %get-tuple-element.137), channel_id=1, source_target_pairs={{0,4},{4,0},{8,12},{12,8},{16,20},{20,16},{24,28},{28,24},{1,5},{5... | collective-permute-start | bytes 393224 | tf_op jit(solution)/shard_map/ppermute | solution.py:130
  76.5 8.5 %collective-permute-start.23 = (bf16[64,1024]{1,0:T(8,128)(2,1)S(1)}, bf16[64,1024]{1,0:T(8,128)(2,1)S(1)}, u32[]{:S(2)}, u32[]{:S(2)}) collective-permute-start(bf16[64,1024]{1,0:T(8,128)(2,1)S(1)} %get-tuple-element.135.rest_10_), channel_id=1, source_target_pairs={{0,8},{4,12},{8,0},{12,4},{16,24},{20,28},{24,16},{28,20},{1,9},{5... | collective-permute-start | bytes 393224 | tf_op jit(solution)/shard_map/ppermute | solution.py:130
  77.6 7.4 %collective-permute-start.24 = (bf16[64,1024]{1,0:T(8,128)(2,1)S(1)}, bf16[64,1024]{1,0:T(8,128)(2,1)S(1)}, u32[]{:S(2)}, u32[]{:S(2)}) collective-permute-start(bf16[64,1024]{1,0:T(8,128)(2,1)S(1)} %get-tuple-element.138), channel_id=1, source_target_pairs={{0,12},{4,8},{8,4},{12,0},{16,28},{20,24},{24,20},{28,16},{1,13},{... | collective-permute-start | bytes 393224 | tf_op jit(solution)/shard_map/ppermute | solution.py:130
  79.4 5.6 %copy-start.4 = (bf16[2,64,4096]{2,1,0:T(8,128)(2,1)S(1)}, bf16[2,64,4096]{2,1,0:T(8,128)(2,1)}, u32[]{:S(2)}) copy-start(bf16[2,64,4096]{2,1,0:T(8,128)(2,1)} %rest_4_.3) | copy-start | bytes 3145732
  79.4 5.6 %copy-start.9 = (f32[4096]{0:T(1024)S(1)}, f32[4096]{0:T(1024)}, u32[]{:S(2)}) copy-start(f32[4096]{0:T(1024)} %param.23) | copy-start | bytes 49156
  79.8 8.1 %collective-permute-start.12 = (bf16[64,1024]{1,0:T(8,128)(2,1)S(1)}, bf16[64,1024]{1,0:T(8,128)(2,1)S(1)}, u32[]{:S(2)}, u32[]{:S(2)}) collective-permute-start(bf16[64,1024]{1,0:T(8,128)(2,1)S(1)} %get-tuple-element.106), channel_id=1, source_target_pairs={{0,4},{4,0},{8,12},{12,8},{16,20},{20,16},{24,28},{28,24},{1,5},{5... | collective-permute-start | bytes 393224 | tf_op jit(solution)/shard_map/ppermute | solution.py:130
  80.9 7.0 %collective-permute-start.14 = (bf16[64,1024]{1,0:T(8,128)(2,1)S(1)}, bf16[64,1024]{1,0:T(8,128)(2,1)S(1)}, u32[]{:S(2)}, u32[]{:S(2)}) collective-permute-start(bf16[64,1024]{1,0:T(8,128)(2,1)S(1)} %get-tuple-element.107), channel_id=1, source_target_pairs={{0,12},{4,8},{8,4},{12,0},{16,28},{20,24},{24,20},{28,16},{1,13},{... | collective-permute-start | bytes 393224 | tf_op jit(solution)/shard_map/ppermute | solution.py:130
  82.4 6.2 %collective-permute-start.13 = (bf16[64,1024]{1,0:T(8,128)(2,1)S(1)}, bf16[64,1024]{1,0:T(8,128)(2,1)S(1)}, u32[]{:S(2)}, u32[]{:S(2)}) collective-permute-start(bf16[64,1024]{1,0:T(8,128)(2,1)S(1)} %get-tuple-element.104.rest_10_), channel_id=1, source_target_pairs={{0,8},{4,12},{8,0},{12,4},{16,24},{20,28},{24,16},{28,20},{1,9},{5... | collective-permute-start | bytes 393224 | tf_op jit(solution)/shard_map/ppermute | solution.py:130
